TPU v7x, 32 devices: a whole 2x2x4 slice. The times are simulated.
32 devices in a mesh: dp: 4 (over y, x), fsdp: 8 (over z, core).
Axes of the slice: x: 2, y: 2, z: 4, core: 2. Of those that a mesh axis runs over, the one named last changes fastest.
Arguments:
- tokens: bfloat16 [32, 128, 2048], P(('dp', 'fsdp')), may hold values from -6 to 6
- cotangent: bfloat16 [32, 128, 2048], P(('dp', 'fsdp')), may hold values from -6 to 6
- lengths: int32 [32, 4], P(('dp', 'fsdp')), may hold values from 0 to 128, as said below
- prefix: int32 [32, 4], P(('dp', 'fsdp')), may hold values from 0 to 128, as said below
- qkv_weight: bfloat16 [2048, 6144], P(('dp', 'fsdp')), may hold values from -0.125 to 0.125
- dense_weight: bfloat16 [2048, 2048], P(('dp', 'fsdp')), may hold values from -2 to 2
- ffin_weight: bfloat16 [2048, 10922], P(('dp', 'fsdp')), may hold values from -0.125 to 0.125
- ffout_weight: bfloat16 [2048, 5461], P(('dp', 'fsdp')), may hold values from -0.4375 to 0.4375
- biases: bfloat16 [2048, 7], P(('dp', 'fsdp')), may hold values from -3 to 3
- norm_gains: bfloat16 [2048, 2], P(('dp', 'fsdp')), may hold values from 0.099609375 to 1.8984375
Outputs:
- output: bfloat16 [32, 128, 2048], P(('dp', 'fsdp'))
- grad_tokens: float32 [32, 128, 2048], P(('dp', 'fsdp'))
- grad_qkv: float32 [2048, 6144], P(('dp', 'fsdp'))
- grad_dense: float32 [2048, 2048], P(('dp', 'fsdp'))
- grad_ffin: float32 [2048, 10922], P(('dp', 'fsdp'))
- grad_ffout: float32 [2048, 5461], P(('dp', 'fsdp'))
- grad_biases: float32 [2048, 7], P(('dp', 'fsdp'))
- grad_gains: float32 [2048, 2], P(('dp', 'fsdp'))
Inputs may be any that keep to these rules, and one draw needn't show every extreme that they name: Row s holds up to 4 proteins packed from position 0: each length is 0 or from 50 to 128, zeros come last, a row's lengths sum to at most 128, and some row holds one protein of length 128. prefix[s,k] is at most lengths[s,k]; it is 0 for an empty slot and equals lengths[s,k] for a protein of 128 residues.
All inputs are finite; a program needn't handle non-finite values.
Results may differ from a plain program's by a relative error of at most 0.014.
Values may be sent and summed in bfloat16 or wider, within the bound.
A program may use at most 384 MiB of HBM per device.

v0:
```python
import jax
import jax.numpy as jnp
from jax import lax
from jax.sharding import PartitionSpec as P

HEADS = 16
LAYERS = 24


MASKED_SCORE = -1e30
EPSILON = 1e-05
ROPE_BASE = 10000.0


def token_layout(lengths, prefix, seq_len):
    doc_count = lengths.shape[1]
    doc_ends = jnp.cumsum(lengths, axis=1)
    doc_starts = doc_ends - lengths
    positions = jnp.arange(seq_len, dtype=jnp.int32)
    doc_index = jnp.sum(
        (positions[None, :, None] >= doc_ends[:, None, :]).astype(jnp.int32), axis=2
    )
    member = doc_index[:, :, None] == jnp.arange(doc_count, dtype=jnp.int32)[None, None, :]
    start_at = jnp.sum(jnp.where(member, doc_starts[:, None, :], 0), axis=2)
    prefix_at = jnp.sum(jnp.where(member, prefix[:, None, :], 0), axis=2)
    valid_pos = positions[None, :] < doc_ends[:, -1:]
    local_pos = jnp.where(valid_pos, positions[None, :] - start_at, 0)
    same_doc = doc_index[:, :, None] == doc_index[:, None, :]
    earlier = (positions[:, None] >= positions[None, :])[None]
    in_prefix = local_pos[:, None, :] < prefix_at[:, :, None]
    inside = valid_pos[:, :, None] & valid_pos[:, None, :] & same_doc & (in_prefix | earlier)
    itself = (
        jnp.logical_not(valid_pos)[:, :, None] & (positions[:, None] == positions[None, :])[None]
    )
    return (inside | itself, local_pos, valid_pos)


def rotary_tables(local_pos, head_dim):
    half_dim = head_dim // 2
    inverse = ROPE_BASE ** (-jnp.arange(half_dim, dtype=jnp.float32) * 2.0 / head_dim)
    angles = local_pos.astype(jnp.float32)[..., None] * inverse
    return (jnp.cos(angles)[:, :, None, :], jnp.sin(angles)[:, :, None, :])


def rotate(values, cosine_table, sine_table):
    half_dim = values.shape[-1] // 2
    first_half = values[..., :half_dim]
    second_half = values[..., half_dim:]
    return jnp.concatenate(
        [
            first_half * cosine_table - second_half * sine_table,
            second_half * cosine_table + first_half * sine_table,
        ],
        axis=-1,
    )


def layer_norm(token_matrix, scale_vec, shift_vec):
    centered = token_matrix - jnp.mean(token_matrix, axis=-1, keepdims=True)
    variance = jnp.mean(centered * centered, axis=-1, keepdims=True)
    return centered * lax.rsqrt(variance + EPSILON) * scale_vec + shift_vec


def contract_rows(left_rows, right_rows):
    return lax.dot_general(
        left_rows, right_rows, (((0,), (0,)), ((), ())), preferred_element_type=jnp.float32
    )


def times_transposed(left_rows, weight_rows):
    return lax.dot_general(
        left_rows, weight_rows, (((1,), (1,)), ((), ())), preferred_element_type=jnp.float32
    )


def owner_rows(term):
    return lax.psum_scatter(term, ("dp", "fsdp"), scatter_dimension=0, tiled=True)


def on_device(
    tokens,
    cotangent,
    lengths,
    prefix,
    qkv_weight,
    dense_weight,
    ffin_weight,
    ffout_weight,
    biases,
    norm_gains,
):
    sequences, seq_len, model_width = tokens.shape
    head_count = HEADS
    head_dim = model_width // head_count
    hidden_units = ffout_weight.shape[1]
    score_scale = head_dim ** (-0.5)
    residual_scale = (2.0 * LAYERS) ** 0.5
    total_rows = sequences * seq_len
    gathered = (
        lax.all_gather(qkv_weight, ("dp", "fsdp"), axis=0, tiled=True),
        lax.all_gather(dense_weight, ("dp", "fsdp"), axis=0, tiled=True),
        lax.all_gather(ffin_weight, ("dp", "fsdp"), axis=0, tiled=True),
        lax.all_gather(ffout_weight, ("dp", "fsdp"), axis=0, tiled=True),
        lax.all_gather(biases, ("dp", "fsdp"), axis=0, tiled=True),
        lax.all_gather(norm_gains, ("dp", "fsdp"), axis=0, tiled=True),
    )
    (
        query_key_value_weight,
        dense_matrix,
        input_weight,
        output_weight,
        bias_stacked_layers,
        gain_all,
    ) = gathered
    bias_vals = bias_stacked_layers.astype(jnp.float32)
    gain_vals = gain_all.astype(jnp.float32)
    attention, local_pos, valid_pos = token_layout(lengths, prefix, seq_len)
    cosine_table, sine_table = rotary_tables(local_pos, head_dim)
    token_matrix = tokens.reshape(total_rows, model_width)
    query_key_value_rows = jnp.dot(
        token_matrix, query_key_value_weight, preferred_element_type=jnp.float32
    ) + bias_vals[:, 0:3].T.reshape(-1)
    head_shape = (sequences, seq_len, head_count, head_dim)
    query_part = query_key_value_rows[:, :model_width].reshape(head_shape)
    key_part = query_key_value_rows[:, model_width : 2 * model_width].reshape(head_shape)
    q_low = rotate(query_part, cosine_table, sine_table).astype(jnp.bfloat16)
    k_low = rotate(key_part, cosine_table, sine_table).astype(jnp.bfloat16)
    v_low = query_key_value_rows[:, 2 * model_width :].reshape(head_shape).astype(jnp.bfloat16)
    scores = score_scale * jnp.einsum(
        "sqhe,skhe->shqk", q_low, k_low, preferred_element_type=jnp.float32
    )
    masked = jnp.where(attention[:, None], scores, MASKED_SCORE)
    row_max = jnp.max(masked, axis=-1, keepdims=True)
    exponent = jnp.exp(masked - row_max)
    row_total = jnp.sum(exponent, axis=-1, keepdims=True)
    log_total = row_max + jnp.log(row_total)
    probs_low = (exponent / row_total).astype(jnp.bfloat16)
    context_vectors = jnp.einsum(
        "shqk,skhe->sqhe", probs_low, v_low, preferred_element_type=jnp.float32
    )
    ctx_low = context_vectors.reshape(total_rows, model_width).astype(jnp.bfloat16)
    attention_output = (
        jnp.dot(ctx_low, dense_matrix, preferred_element_type=jnp.float32) + bias_vals[:, 3]
    )
    resid_one = residual_scale * token_matrix.astype(jnp.float32) + attention_output
    first_normalized, norm_one_back = jax.vjp(
        layer_norm, resid_one, gain_vals[:, 0], bias_vals[:, 4]
    )
    normed_low = first_normalized.astype(jnp.bfloat16)
    inner_projection = jnp.dot(normed_low, input_weight, preferred_element_type=jnp.float32)

    def gated_units(both_parts):
        return (
            jax.nn.gelu(both_parts[:, :hidden_units], approximate=False)
            * both_parts[:, hidden_units:]
        )

    activation_result, gated_back = jax.vjp(gated_units, inner_projection)
    act_low = activation_result.astype(jnp.bfloat16)
    residual_branch = times_transposed(act_low, output_weight) + bias_vals[:, 5]
    resid_two = residual_scale * first_normalized + residual_branch
    result, norm_two_back = jax.vjp(layer_norm, resid_two, gain_vals[:, 1], bias_vals[:, 6])
    regathered = (
        lax.all_gather(qkv_weight, ("dp", "fsdp"), axis=0, tiled=True),
        lax.all_gather(dense_weight, ("dp", "fsdp"), axis=0, tiled=True),
        lax.all_gather(ffin_weight, ("dp", "fsdp"), axis=0, tiled=True),
        lax.all_gather(ffout_weight, ("dp", "fsdp"), axis=0, tiled=True),
        lax.all_gather(biases, ("dp", "fsdp"), axis=0, tiled=True),
        lax.all_gather(norm_gains, ("dp", "fsdp"), axis=0, tiled=True),
    )
    query_key_value_weight, dense_matrix, input_weight, output_weight = (
        regathered[0],
        regathered[1],
        regathered[2],
        regathered[3],
    )
    grad_out = cotangent.reshape(total_rows, model_width).astype(jnp.float32)
    grad_out = grad_out * valid_pos.reshape(total_rows, 1).astype(jnp.float32)
    d_resid_two, d_gain_two, d_bias_two = norm_two_back(grad_out)
    d_branch = d_resid_two.astype(jnp.bfloat16)
    d_act = jnp.dot(d_branch, output_weight, preferred_element_type=jnp.float32)
    (d_inner,) = gated_back(d_act)
    d_inner_low = d_inner.astype(jnp.bfloat16)
    d_normed = residual_scale * d_resid_two + times_transposed(d_inner_low, input_weight)
    d_resid_one, d_gain_one, d_bias_one = norm_one_back(d_normed)
    d_attn = d_resid_one.astype(jnp.bfloat16)
    d_ctx_low = times_transposed(d_attn, dense_matrix).reshape(head_shape).astype(jnp.bfloat16)
    scores_again = score_scale * jnp.einsum(
        "sqhe,skhe->shqk", q_low, k_low, preferred_element_type=jnp.float32
    )
    attn_probs = jnp.where(attention[:, None], jnp.exp(scores_again - log_total), 0.0)
    probs_again = attn_probs.astype(jnp.bfloat16)
    d_probs = jnp.einsum("sqhe,skhe->shqk", d_ctx_low, v_low, preferred_element_type=jnp.float32)
    d_value = jnp.einsum(
        "shqk,sqhe->skhe", probs_again, d_ctx_low, preferred_element_type=jnp.float32
    )
    d_scores = attn_probs * (d_probs - jnp.sum(attn_probs * d_probs, axis=-1, keepdims=True))
    d_scores_low = jnp.where(attention[:, None], d_scores, 0.0).astype(jnp.bfloat16)
    d_query = score_scale * jnp.einsum(
        "shqk,skhe->sqhe", d_scores_low, k_low, preferred_element_type=jnp.float32
    )
    d_key = score_scale * jnp.einsum(
        "shqk,sqhe->skhe", d_scores_low, q_low, preferred_element_type=jnp.float32
    )
    d_query = rotate(d_query, cosine_table, -sine_table).reshape(total_rows, model_width)
    d_key = rotate(d_key, cosine_table, -sine_table).reshape(total_rows, model_width)
    d_qkv_low = jnp.concatenate(
        [d_query, d_key, d_value.reshape(total_rows, model_width)], axis=1
    ).astype(jnp.bfloat16)
    d_tokens = residual_scale * d_resid_one + times_transposed(d_qkv_low, query_key_value_weight)
    qkv_sums = jnp.sum(d_qkv_low.astype(jnp.float32), axis=0).reshape(3, model_width).T
    bias_grads = jnp.concatenate(
        [
            qkv_sums,
            jnp.stack(
                [
                    jnp.sum(d_attn.astype(jnp.float32), axis=0),
                    d_bias_one,
                    jnp.sum(d_branch.astype(jnp.float32), axis=0),
                    d_bias_two,
                ],
                axis=1,
            ),
        ],
        axis=1,
    )
    gain_grads = jnp.stack([d_gain_one, d_gain_two], axis=1)
    grad_ffout_rows = owner_rows(contract_rows(d_branch, act_low))
    grad_ffin_rows = owner_rows(contract_rows(normed_low, d_inner_low))
    dense_and_small = owner_rows(
        jnp.concatenate([contract_rows(ctx_low, d_attn), bias_grads, gain_grads], axis=1)
    )
    grad_qkv_rows = owner_rows(contract_rows(token_matrix, d_qkv_low))
    return (
        result.astype(jnp.bfloat16).reshape(sequences, seq_len, model_width),
        d_tokens.reshape(sequences, seq_len, model_width),
        grad_qkv_rows,
        dense_and_small[:, :model_width],
        grad_ffin_rows,
        grad_ffout_rows,
        dense_and_small[:, model_width : model_width + 7],
        dense_and_small[:, model_width + 7 :],
    )


def solution(mesh):
    in_specs = (
        P(("dp", "fsdp"), None, None),
        P(("dp", "fsdp"), None, None),
        P(("dp", "fsdp"), None),
        P(("dp", "fsdp"), None),
        P(("dp", "fsdp"), None),
        P(("dp", "fsdp"), None),
        P(("dp", "fsdp"), None),
        P(("dp", "fsdp"), None),
        P(("dp", "fsdp"), None),
        P(("dp", "fsdp"), None),
    )
    out_specs = (
        P(("dp", "fsdp"), None, None),
        P(("dp", "fsdp"), None, None),
        P(("dp", "fsdp"), None),
        P(("dp", "fsdp"), None),
        P(("dp", "fsdp"), None),
        P(("dp", "fsdp"), None),
        P(("dp", "fsdp"), None),
        P(("dp", "fsdp"), None),
    )
    return jax.shard_map(
        on_device, mesh=mesh, in_specs=in_specs, out_specs=out_specs, check_vma=False
    )
```

profile of v0, /device:TPU:0, one launch (start us, length us, event | category | flops | bytes accessed | tf_op | source)
XLA Modules:
  0.0 2871.3 jit_solution(2436182001089027719)
XLA Ops:
  7.3 0.7 all-gather.7.cloned.1.call-update
  8.0 0.7 all-gather.9.cloned.1.call-update
  8.7 0.7 all-gather.11.cloned.1.call-update
  10.8 43.2 %all-gather.1 = bf16[32,64,2]{1,2,0:T(2,128)(2,1)S(1)} all-gather(bf16[1,64,2]{1,2,0:T(2,128)(2,1)S(1)} %bitcast.149), channel_id=1, replica_groups=mesh['dp'=4,'fsdp'=8] {'dp','fsdp'}, dimensions={0}, use_global_device_ids=true | all-gather | bytes 8448 | tf_op jit(solution)/shard_map/all_gather | solution.py:105
  54.2 37.6 %all-gather = bf16[32,64,7]{1,2,0:T(8,128)(2,1)S(1)} all-gather(bf16[1,64,7]{1,2,0:T(8,128)(2,1)S(1)} %bitcast.148), channel_id=1, replica_groups=mesh['dp'=4,'fsdp'=8] {'dp','fsdp'}, dimensions={0}, use_global_device_ids=true | all-gather | bytes 29568 | tf_op jit(solution)/shard_map/all_gather | solution.py:104
  92.0 0.7 fusion.74
  92.6 0.7 iota_compare_fusion.4
  93.5 0.7 fusion.81
  94.3 0.9 fusion.59
  95.3 0.6 fusion.84
  95.9 73.1 %all-gather.7.cloned.1.call-done = bf16[2048,6144]{1,0:T(8,128)(2,1)} async-done(((bf16[64,6144]{1,0:T(8,128)(2,1)}), bf16[2048,6144]{1,0:T(8,128)(2,1)}) %all-gather.7.cloned.1.call-update) | async-done | bytes 25165840 | tf_op jit(solution)/shard_map/all_gather | solution.py:100
  168.9 10.0 convolution_add_fusion
  179.5 0.7 fusion.82
  180.2 1.4 fusion.32
  181.6 0.8 select_reduce_fusion
  183.8 63.7 %all-gather.9.cloned.1.call-done = bf16[2048,2048]{1,0:T(8,128)(2,1)} async-done(((bf16[64,2048]{1,0:T(8,128)(2,1)}), bf16[2048,2048]{1,0:T(8,128)(2,1)}) %all-gather.9.cloned.1.call-update) | async-done | bytes 8388624 | tf_op jit(solution)/shard_map/all_gather | solution.py:101
  247.5 4.7 fusion.86
  252.6 246.8 %all-gather.11.cloned.1.call-done = bf16[2048,10922]{1,0:T(8,128)(2,1)} async-done(((bf16[64,10922]{1,0:T(8,128)(2,1)}), bf16[2048,10922]{1,0:T(8,128)(2,1)}) %all-gather.11.cloned.1.call-update) | async-done | bytes 44736528 | tf_op jit(solution)/shard_map/all_gather | solution.py:102
  499.4 25.2 fusion.76
  524.6 8.5 multiply_convert_fusion
  533.1 109.3 %all-gather.13.cloned.1.call-done = bf16[2048,5461]{1,0:T(8,128)(2,1)} async-done(((bf16[64,5461]{1,0:T(8,128)(2,1)}), bf16[2048,5461]{1,0:T(8,128)(2,1)}) %all-gather.13.cloned.1.call-update) | async-done | bytes 22368272 | tf_op jit(solution)/shard_map/all_gather | solution.py:103
  642.4 12.1 fusion.87
  654.7 1.1 fusion.23
  655.9 2.0 fusion.79
  657.8 1.5 convert_reduce_fusion.1
  659.4 17.3 fusion.29
  676.6 23.2 multiply_reduce_fusion
  699.8 1.6 fusion.78
  701.5 0.9 copy-done.12
  702.4 0.8 convert_reduce_fusion.2
  703.2 0.8 copy-done.8
  704.0 7.1 convolution_convert_fusion
  711.1 2.1 copy.143
  713.2 2.7 fusion.39
  715.9 1.3 convolution_convert_fusion.1
  717.2 3.8 fusion.15
  721.0 3.7 fusion.14
  724.7 9.5 fusion.88
  734.1 1.5 subtract_convert_fusion.1
  735.6 1.1 pad_maximum_fusion.3
  736.7 1.3 copy.115
  738.1 2.1 pad_maximum_fusion.4
  740.2 1.3 copy.119
  741.5 2.3 convert_reduce_fusion
  743.9 0.8 reshape.728
  744.6 39.3 %concatenate.48 = f32[2048,2057]{0,1:T(8,128)} concatenate(f32[2048,2048]{0,1:T(8,128)} %fusion.88, f32[2048,3]{0,1:T(4,128)S(1)} %bitcast.136, f32[2048,1]{0,1:T(1,128)} %bitcast.146, f32[2048,1]{0,1:T(1,128)} %bitcast.145, f32[2048,1]{0,1:T(1,128)} %bitcast.143, f32[2048,1]{0,1:T(1,128)} %bitcast.142, f32[2048,1]{0,1:T(1,128)} %bitcast.144, f32[2048,1]{0,1:T(1,128)S(1)} %bitcast.141), dimensions={1} | concatenate | bytes 33701888 | tf_op jit(solution)/shard_map/concatenate | solution.py:231
  783.9 16.9 copy.134
  800.9 1.0 copy-done.4
  801.9 21.1 convolution_bitcast_fusion
  823.0 49.1 %copy.132 = f32[2048,6144]{1,0:T(8,128)} copy(f32[2048,6144]{0,1:T(8,128)} %convolution_bitcast_fusion) | data formatting | bytes 100663296
  872.2 1.0 copy-done.15
  873.2 17.9 fusion.89
  891.8 35.1 %fusion.54 = f32[2048,10922]{1,0:T(8,128)} fusion(f32[128,5461]{0,1:T(8,128)} %get-tuple-element.69, f32[128,5461]{0,1:T(8,128)} %get-tuple-element.68, f32[128,2048]{1,0:T(8,128)S(1)} %get-tuple-element.101, f32[2048]{0:T(1024)S(1)} %bitcast.135, f32[2048]{0:T(1024)S(1)} %bitcast.132, f32[128]{0:T(128)S(1)} %fusion.67, f32[128]{0:T(128)S(1)} %broadcast_multiply_fusion.1), kind=kOutput, calls=%fused_computation.110 | convolution fusion | flops 5730380288 | bytes 96131072 | tf_op jit(solution)/shard_map/dot_general | solution.py:65
  926.9 1.0 copy-done.6
  928.4 20.4 fusion.8
  948.8 48.0 %reduce-scatter.15.cloned.1.call-done = f32[64,2057]{1,0:T(8,128)} async-done(((f32[2048,2057]{1,0:T(8,128)}), f32[64,2057]{1,0:T(8,128)}) %reduce-scatter.15.cloned.1.call-update) | async-done | bytes 526608
  996.8 0.8 slice.118
  997.5 0.7 copy.141
  998.2 0.8 slice.119
  999.0 0.6 copy.142
  999.7 1.9 slice.117
  1001.5 431.1 %reduce-scatter.13.cloned.1.call-done = f32[64,6144]{1,0:T(8,128)} async-done(((f32[2048,6144]{1,0:T(8,128)}), f32[64,6144]{1,0:T(8,128)}) %reduce-scatter.13.cloned.1.call-update) | async-done | bytes 1572880
  1432.6 482.9 %reduce-scatter.11.cloned.1.call-done = f32[64,5461]{1,0:T(8,128)} async-done(((f32[2048,5461]{1,0:T(8,128)}), f32[64,5461]{1,0:T(8,128)}) %reduce-scatter.11.cloned.1.call-update) | async-done | bytes 1398032 | tf_op jit(solution)/shard_map/reduce_scatter | solution.py:77
  1915.6 948.5 %reduce-scatter.9.cloned.1.call-done = f32[64,10922]{1,0:T(8,128)} async-done(((f32[2048,10922]{1,0:T(8,128)}), f32[64,10922]{1,0:T(8,128)}) %reduce-scatter.9.cloned.1.call-update) | async-done | bytes 2796048 | tf_op jit(solution)/shard_map/reduce_scatter | solution.py:77
  (112 shorter events, 5.9 us)
Async XLA Ops:
  7.2 2.9 copy-start.36
  7.2 3.7 copy-start.34
  7.2 47.0 %copy-start.29 = (bf16[64,7]{0,1:T(8,128)(2,1)S(1)}, bf16[64,7]{0,1:T(8,128)(2,1)}, u32[]{:S(2)}) copy-start(bf16[64,7]{0,1:T(8,128)(2,1)} %param.18) | copy-start | bytes 2692
  7.2 86.2 %copy-start.35 = (s32[1,4]{1,0:T(1,128)S(1)}, s32[1,4]{1,0:T(1,128)}, u32[]{:S(2)}) copy-start(s32[1,4]{1,0:T(1,128)} %param.13) | copy-start | bytes 52
  7.2 161.7 %copy-start.3 = (bf16[1,128,2048]{2,1,0:T(8,128)(2,1)S(1)}, bf16[1,128,2048]{2,1,0:T(8,128)(2,1)}, u32[]{:S(2)}) copy-start(bf16[1,128,2048]{2,1,0:T(8,128)(2,1)} %param.10) | copy-start | bytes 1572868
  7.2 161.7 %all-gather.7.cloned.1.call-start = ((), (), s32[]{:S(2)}) async-start(), calls=%async_computation.4 | async-start | bytes 25952256 | tf_op jit(solution)/shard_map/all_gather | solution.py:100
  8.0 239.6 %all-gather.9.cloned.1.call-start = ((), (), s32[]{:S(2)}) async-start(), calls=%async_computation.5 | async-start | bytes 8650752 | tf_op jit(solution)/shard_map/all_gather | solution.py:101
  8.7 490.6 %all-gather.11.cloned.1.call-start = ((), (), s32[]{:S(2)}) async-start(), calls=%async_computation.6 | async-start | bytes 46497792 | tf_op jit(solution)/shard_map/all_gather | solution.py:102
  9.4 632.9 %all-gather.13.cloned.1.call-start = ((), (), s32[]{:S(2)}) async-start(), calls=%async_computation.7 | async-start | bytes 23248896 | tf_op jit(solution)/shard_map/all_gather | solution.py:103
  10.0 986.7 %reduce-scatter.15.cloned.1.call-start = ((), (), s32[]{:S(2)}) async-start(), calls=%async_computation.11 | async-start | bytes 18382848
  92.6 562.1 %copy-start.28 = (f32[128]{0:T(128)}, f32[128]{0:T(128)S(1)}, u32[]{:S(2)}) copy-start(f32[128]{0:T(128)S(1)} %fusion.74) | copy-start | bytes 1540
  95.2 85.0 %copy-start.23 = (f32[128,64]{1,0:T(8,128)}, f32[128,64]{1,0:T(8,128)S(1)}, u32[]{:S(2)}) copy-start(f32[128,64]{1,0:T(8,128)S(1)} %get-tuple-element.97) | copy-start | bytes 98308
  95.9 546.5 %copy-start.21 = (f32[2048,1]{0,1:T(1,128)}, f32[2048,1]{0,1:T(1,128)S(1)}, u32[]{:S(2)}) copy-start(f32[2048,1]{0,1:T(1,128)S(1)} %get-tuple-element.91) | copy-start | bytes 24580
  178.9 3.6 copy-start
  181.6 0.8 copy-start.16
  181.6 1.0 copy-start.17
  181.6 1.2 copy-start.18
  181.6 1.3 copy-start.19
  182.4 1.0 copy-start.1
  183.8 68.5 %copy-start.14 = (bf16[16,128,128]{2,1,0:T(8,128)(2,1)}, bf16[16,128,128]{2,1,0:T(8,128)(2,1)S(1)}, u32[]{:S(2)}) copy-start(bf16[16,128,128]{2,1,0:T(8,128)(2,1)S(1)} %convolution_convert_fusion.2) | copy-start | bytes 1572868
  252.6 246.8 %copy-start.30 = (f32[128]{0:T(128)}, f32[128]{0:T(128)S(1)}, u32[]{:S(2)}) copy-start(f32[128]{0:T(128)S(1)} %multiply_reduce_fusion.3) | copy-start | bytes 1540
  642.4 12.4 copy-start.20
  642.4 13.5 copy-start.26
  676.6 23.2 copy-start.31
  701.5 1.0 copy-start.12
  701.5 9.6 copy-start.32
  703.2 0.8 copy-start.8
  711.1 4.8 copy-start.2
  713.2 2.7 copy-start.9
  724.6 9.5 copy-start.10
  724.6 9.5 copy-start.11
  724.6 9.5 copy-start.24
  724.6 9.5 copy-start.25
  736.7 7.9 copy-start.27
  741.5 42.4 %copy-start.5 = (bf16[1,128,16,128]{1,3,2,0:T(8,128)(2,1)}, bf16[1,128,16,128]{1,3,2,0:T(8,128)(2,1)S(1)}, u32[]{:S(2)}) copy-start(bf16[1,128,16,128]{1,3,2,0:T(8,128)(2,1)S(1)} %copy.119) | copy-start | bytes 1572868
  800.9 1.0 copy-start.4
  800.9 631.7 %reduce-scatter.13.cloned.1.call-start = ((), (), s32[]{:S(2)}) async-start(), calls=%async_computation.10 | async-start | bytes 51904512
  872.1 1.1 copy-start.15
  872.1 1043.4 %reduce-scatter.11.cloned.1.call-start = ((), (), s32[]{:S(2)}) async-start(), calls=%async_computation.9 | async-start | bytes 46497792 | tf_op jit(solution)/shard_map/reduce_scatter | solution.py:77
  891.1 0.7 copy-start.22
  891.1 1972.9 %reduce-scatter.9.cloned.1.call-start = ((), (), s32[]{:S(2)}) async-start(), calls=%async_computation.8 | async-start | bytes 92995584 | tf_op jit(solution)/shard_map/reduce_scatter | solution.py:77
  926.8 1.0 copy-start.6
  926.8 1.2 copy-start.7
  926.8 1.6 copy-start.13
  926.8 1.6 copy-start.33
Sparse Core Ops, SparseCore 0:
  11.1 157.8 all-gather.6
  171.9 75.5 all-gather.8
  250.4 248.8 all-gather.10
  502.1 140.2 all-gather.12
  801.0 195.7 reduce-scatter.14
  1003.6 428.9 reduce-scatter.12
  1435.5 480.0 reduce-scatter.10
  1918.5 945.4 reduce-scatter.8
where the time goes:
time: 2880 us; the launch traced here: 2870 us
  waiting for transfers between devices  2410 us (84%)
  matrix products  216 us (8%)
  local copies, waits for them, and re-layouts  125 us (4%)
  blocking collectives  80.9 us (3%)
    reduce_scatter x2, waiting for transfers between devices, owner_rows(): lax.psum_scatter(term, ('dp', 'fsdp'), scatter_dimension=0, tiled=True)  1430 us
    unnamed x10, waiting for transfers between devices  482 us
    all_gather x1, waiting for transfers between devices, on_device(): lax.all_gather(ffin_weight, ('dp', 'fsdp'), axis=0, tiled=True)  247 us
    all_gather x1, waiting for transfers between devices, on_device(): lax.all_gather(ffout_weight, ('dp', 'fsdp'), axis=0, tiled=True)  109 us
    dot_general x4, matrix products, contract_rows(): lax.dot_general(left_rows, right_rows, (((0,), (0,)), ((), ())), preferre...  83.5 us
    unnamed x81, local copies, waits for them, and re-layouts  74.6 us
    all_gather x1, waiting for transfers between devices, on_device(): lax.all_gather(qkv_weight, ('dp', 'fsdp'), axis=0, tiled=True)  73.1 us
    all_gather x1, waiting for transfers between devices, on_device(): lax.all_gather(dense_weight, ('dp', 'fsdp'), axis=0, tiled=True)  63.7 us
  transfers between devices with their start and end apart: 8, of which 8 were waited for; matrix products, arithmetic and copies ran while one was open for 7% of the time, Pallas kernels for 0%

commit v1 on v0

v1 whole, which is shorter than its diff:
```python
import functools

import jax
import jax.numpy as jnp
from jax import lax
from jax.experimental import pallas as pl
from jax.experimental.pallas import tpu as pltpu
from jax.sharding import Mesh
from jax.sharding import PartitionSpec as P

HEADS = 16
LAYERS = 24
MASKED_SCORE = -1e30
EPSILON = 1e-05
ROPE_BASE = 10000.0

AXES = ("a", "b", "e", "f", "c")
TENSOR = ("b", "f", "c")
GROUP = 8
DEVICE_MESH = pl.DeviceIdType.MESH
BF16 = jnp.bfloat16
F32 = jnp.float32


def token_layout(lengths, prefix, seq_len):
    doc_count = lengths.shape[1]
    doc_ends = jnp.cumsum(lengths, axis=1)
    doc_starts = doc_ends - lengths
    positions = jnp.arange(seq_len, dtype=jnp.int32)
    doc_index = jnp.sum(
        (positions[None, :, None] >= doc_ends[:, None, :]).astype(jnp.int32), axis=2
    )
    member = doc_index[:, :, None] == jnp.arange(doc_count, dtype=jnp.int32)[None, None, :]
    start_at = jnp.sum(jnp.where(member, doc_starts[:, None, :], 0), axis=2)
    prefix_at = jnp.sum(jnp.where(member, prefix[:, None, :], 0), axis=2)
    valid_pos = positions[None, :] < doc_ends[:, -1:]
    local_pos = jnp.where(valid_pos, positions[None, :] - start_at, 0)
    same_doc = doc_index[:, :, None] == doc_index[:, None, :]
    earlier = (positions[:, None] >= positions[None, :])[None]
    in_prefix = local_pos[:, None, :] < prefix_at[:, :, None]
    inside = valid_pos[:, :, None] & valid_pos[:, None, :] & same_doc & (in_prefix | earlier)
    itself = (
        jnp.logical_not(valid_pos)[:, :, None] & (positions[:, None] == positions[None, :])[None]
    )
    return (inside | itself, local_pos, valid_pos)


def rotary_tables(local_pos, head_dim):
    half_dim = head_dim // 2
    inverse = ROPE_BASE ** (-jnp.arange(half_dim, dtype=jnp.float32) * 2.0 / head_dim)
    angles = local_pos.astype(jnp.float32)[..., None] * inverse
    return (jnp.cos(angles)[:, :, None, :], jnp.sin(angles)[:, :, None, :])


def rotate(values, cosine_table, sine_table):
    half_dim = values.shape[-1] // 2
    first_half = values[..., :half_dim]
    second_half = values[..., half_dim:]
    return jnp.concatenate(
        [
            first_half * cosine_table - second_half * sine_table,
            second_half * cosine_table + first_half * sine_table,
        ],
        axis=-1,
    )


def layer_norm(token_matrix, scale_vec, shift_vec):
    centered = token_matrix - jnp.mean(token_matrix, axis=-1, keepdims=True)
    variance = jnp.mean(centered * centered, axis=-1, keepdims=True)
    return centered * lax.rsqrt(variance + EPSILON) * scale_vec + shift_vec


def contract_rows(left_rows, right_rows):
    return lax.dot_general(
        left_rows, right_rows, (((0,), (0,)), ((), ())), preferred_element_type=F32
    )


def times_transposed(left_rows, weight_rows):
    return lax.dot_general(
        left_rows, weight_rows, (((1,), (1,)), ((), ())), preferred_element_type=F32
    )


def neighbours():
    b, f, c = (lax.axis_index(axis) for axis in TENSOR)
    slot = lambda bb, ff, cc: (bb * 2 + ff) * 2 + cc
    return b, f, c, slot


def greet(b, f, c):
    barrier = pltpu.get_barrier_semaphore()
    for target in ({"b": 1 - b}, {"f": 1 - f}, {"c": 1 - c}):
        pl.semaphore_signal(barrier, inc=1, device_id=target, device_id_type=DEVICE_MESH)
    pl.semaphore_wait(barrier, 3)


def gather_kernel(x_ref, o_ref, local_sem, send_sem, recv_sem):
    b, f, c, slot = neighbours()
    half = x_ref.shape[0] // 2
    low, high = pl.ds(0, half), pl.ds(half, half)
    me, nb, nf, dg = slot(b, f, c), slot(1 - b, f, c), slot(b, 1 - f, c), slot(1 - b, 1 - f, c)
    to_b, to_f, to_c = {"b": 1 - b}, {"f": 1 - f}, {"c": 1 - c}

    def copy(number, source, target, device):
        return pltpu.make_async_remote_copy(
            src_ref=source,
            dst_ref=target,
            send_sem=send_sem.at[number],
            recv_sem=recv_sem.at[number],
            device_id=device,
            device_id_type=DEVICE_MESH,
        )

    mine = pltpu.make_async_copy(x_ref, o_ref.at[me], local_sem)
    mine.start()
    greet(b, f, c)
    own = [
        copy(0, x_ref.at[low], o_ref.at[me, low], to_b),
        copy(1, x_ref.at[high], o_ref.at[me, high], to_f),
        copy(2, x_ref.at[high], o_ref.at[me, high], to_b),
        copy(3, x_ref.at[low], o_ref.at[me, low], to_f),
        copy(4, x_ref, o_ref.at[me], to_c),
    ]
    for one in own:
        one.start()
    own[0].wait_recv()
    relay_f = copy(5, o_ref.at[nb, low], o_ref.at[nb, low], to_f)
    relay_f.start()
    own[1].wait_recv()
    relay_b = copy(6, o_ref.at[nf, high], o_ref.at[nf, high], to_b)
    relay_b.start()
    own[2].wait_recv()
    over_b = copy(7, o_ref.at[nb], o_ref.at[nb], to_c)
    over_b.start()
    own[3].wait_recv()
    over_f = copy(8, o_ref.at[nf], o_ref.at[nf], to_c)
    over_f.start()
    relay_f.wait_recv()
    relay_b.wait_recv()
    over_d = copy(9, o_ref.at[dg], o_ref.at[dg], to_c)
    over_d.start()
    own[4].wait_recv()
    for one in (over_b, over_f, over_d):
        one.wait_recv()
    for one in own + [relay_f, relay_b, over_b, over_f, over_d]:
        one.wait_send()
    mine.wait()


def group_gather(x, collective_id):
    rows, width = x.shape
    out = pl.pallas_call(
        gather_kernel,
        out_shape=jax.ShapeDtypeStruct((GROUP, rows, width), x.dtype),
        in_specs=[pl.BlockSpec(memory_space=pl.ANY)],
        out_specs=pl.BlockSpec(memory_space=pl.ANY),
        scratch_shapes=[
            pltpu.SemaphoreType.DMA(()),
            pltpu.SemaphoreType.DMA((10,)),
            pltpu.SemaphoreType.DMA((10,)),
        ],
        compiler_params=pltpu.CompilerParams(collective_id=collective_id, has_side_effects=True),
        cost_estimate=pl.CostEstimate(
            flops=0, bytes_accessed=20 * GROUP * rows * width, transcendentals=0
        ),
    )(x)
    return out.reshape(GROUP * rows, width)


def scatter_kernel(
    p_ref, o_ref, own_ref, core_ref, out_ref, relay_ref, land_ref, local_sem, send_sem, recv_sem
):
    b, f, c, slot = neighbours()
    rows = own_ref.shape[1]
    half = rows // 2
    low, high = pl.ds(0, half), pl.ds(half, half)
    to_b, to_f, to_c = {"b": 1 - b}, {"f": 1 - f}, {"c": 1 - c}
    places = [(1 - b, 1 - f), (1 - b, f), (b, 1 - f), (b, f)]

    def copy(number, source, target, device):
        return pltpu.make_async_remote_copy(
            src_ref=source,
            dst_ref=target,
            send_sem=send_sem.at[number],
            recv_sem=recv_sem.at[number],
            device_id=device,
            device_id_type=DEVICE_MESH,
        )

    local = [
        pltpu.make_async_copy(p_ref.at[slot(*place, c)], own_ref.at[k], local_sem.at[k])
        for k, place in enumerate(places)
    ]
    for one in local:
        one.start()
    greet(b, f, c)
    core = [
        copy(k, p_ref.at[slot(*place, 1 - c)], core_ref.at[k], to_c)
        for k, place in enumerate(places)
    ]
    for one in core:
        one.start()
    step = 16

    def add(target, at, count, terms):
        @pl.loop(0, count // step)
        def _(i):
            window = pl.ds(pl.multiple_of(at + i * step, step), step)
            total = terms[0][window, :].astype(F32)
            for term in terms[1:]:
                total = total + term[window, :].astype(F32)
            target[window, :] = total.astype(target.dtype)

    local[0].wait()
    core[0].wait_recv()
    add(out_ref.at[0], 0, rows, [own_ref.at[0], core_ref.at[0]])
    diag_b = copy(4, out_ref.at[0, low], relay_ref.at[low], to_b)
    diag_b.start()
    diag_f = copy(5, out_ref.at[0, high], relay_ref.at[high], to_f)
    diag_f.start()
    local[1].wait()
    core[1].wait_recv()
    add(out_ref.at[1], 0, half, [own_ref.at[1], core_ref.at[1]])
    b_low = copy(6, out_ref.at[1, low], land_ref.at[0, low], to_b)
    b_low.start()
    local[2].wait()
    core[2].wait_recv()
    add(out_ref.at[2], half, half, [own_ref.at[2], core_ref.at[2]])
    f_high = copy(7, out_ref.at[2, high], land_ref.at[1, high], to_f)
    f_high.start()
    diag_f.wait_recv()
    add(out_ref.at[1], half, half, [own_ref.at[1], core_ref.at[1], relay_ref])
    b_high = copy(8, out_ref.at[1, high], land_ref.at[0, high], to_b)
    b_high.start()
    diag_b.wait_recv()
    add(out_ref.at[2], 0, half, [own_ref.at[2], core_ref.at[2], relay_ref])
    f_low = copy(9, out_ref.at[2, low], land_ref.at[1, low], to_f)
    f_low.start()
    local[3].wait()
    core[3].wait_recv()
    for one in (b_low, f_high, b_high, f_low):
        one.wait_recv()
    add(o_ref, 0, rows, [own_ref.at[3], core_ref.at[3], land_ref.at[0], land_ref.at[1]])
    for one in core + [diag_b, diag_f, b_low, f_high, b_high, f_low]:
        one.wait_send()


def group_scatter(partial, collective_id):
    rows, width = partial.shape[0] // GROUP, partial.shape[1]
    block = (rows, width)
    return pl.pallas_call(
        scatter_kernel,
        out_shape=jax.ShapeDtypeStruct(block, F32),
        in_specs=[pl.BlockSpec(memory_space=pl.ANY)],
        out_specs=pl.BlockSpec(memory_space=pltpu.VMEM),
        scratch_shapes=[
            pltpu.VMEM((4,) + block, BF16),
            pltpu.VMEM((4,) + block, BF16),
            pltpu.VMEM((3,) + block, BF16),
            pltpu.VMEM(block, BF16),
            pltpu.VMEM((2,) + block, BF16),
            pltpu.SemaphoreType.DMA((4,)),
            pltpu.SemaphoreType.DMA((10,)),
            pltpu.SemaphoreType.DMA((10,)),
        ],
        compiler_params=pltpu.CompilerParams(
            collective_id=collective_id, has_side_effects=True, vmem_limit_bytes=24 << 20
        ),
        cost_estimate=pl.CostEstimate(
            flops=0, bytes_accessed=20 * partial.size, transcendentals=0
        ),
    )(partial.astype(BF16).reshape((GROUP,) + block))


def exchange(x, axis):
    count = lax.axis_size(axis)
    me = lax.axis_index(axis)
    got = {0: x}
    for shift in range(1, count):
        got[shift] = lax.ppermute(x, axis, [(i, (i + shift) % count) for i in range(count)])
    if count == 2:
        first = me == 0
        return [jnp.where(first, x, got[1]), jnp.where(first, got[1], x)]
    whole = jnp.stack([got[s] for s in range(count)])
    order = (me - jnp.arange(count)) % count
    return [whole[order[k]] for k in range(count)]


def gather_weight(pieces):
    mine = lax.all_to_all(pieces, TENSOR, split_axis=0, concat_axis=0, tiled=True)
    rows, cols = mine.shape[1:]
    mine = mine.reshape(2, 4 * rows, cols)
    along_e = jnp.stack(exchange(mine, "e"), axis=1)
    along_a = jnp.stack(exchange(along_e, "a"), axis=0)
    return along_a.reshape(-1, cols)


def scatter_axis(x, axis):
    count = lax.axis_size(axis)
    me = lax.axis_index(axis)
    total = lax.dynamic_index_in_dim(x, me, 0, keepdims=False)
    for shift in range(1, count):
        out = lax.dynamic_index_in_dim(x, (me + shift) % count, 0, keepdims=False).astype(BF16)
        total = total + lax.ppermute(
            out, axis, [(i, (i + shift) % count) for i in range(count)]
        ).astype(F32)
    return total


def scatter_weight(grad):
    a, e = lax.axis_size("a"), lax.axis_size("e")
    cols = grad.shape[1]
    rows = grad.shape[0] // (a * e * GROUP)
    grad = scatter_axis(grad.reshape(a, 2, e, 4 * rows, cols), "a")
    grad = scatter_axis(jnp.swapaxes(grad, 0, 1), "e")
    grad = grad.reshape(GROUP, rows, cols).astype(BF16)
    return lax.all_to_all(grad, TENSOR, split_axis=0, concat_axis=0, tiled=True)


def on_device(
    tokens,
    cotangent,
    lengths,
    prefix,
    qkv_weight,
    dense_weight,
    ffin_weight,
    ffout_weight,
    biases,
    norm_gains,
):
    sequences, seq_len, model_width = tokens.shape
    head_count = HEADS
    head_dim = model_width // head_count
    my_heads = head_count // GROUP
    hidden_units = ffout_weight.shape[1]
    unit_cols = -(-hidden_units // (GROUP * 128)) * 128
    padded = unit_cols * GROUP
    slice_width = my_heads * head_dim
    score_scale = head_dim ** (-0.5)
    residual_scale = (2.0 * LAYERS) ** 0.5
    total_rows = sequences * seq_len
    group_rows = GROUP * total_rows
    own_rows = qkv_weight.shape[0]

    token_matrix = tokens.reshape(total_rows, model_width)
    tokens_all = group_gather(token_matrix, 0)

    qkv_pieces = (
        qkv_weight.reshape(own_rows, 3, GROUP, slice_width)
        .transpose(2, 0, 1, 3)
        .reshape(GROUP, own_rows, 3 * slice_width)
    )
    dense_pieces = dense_weight.reshape(own_rows, GROUP, slice_width).transpose(1, 0, 2)

    def unit_pieces(weight):
        wide = jnp.pad(weight, ((0, 0), (0, padded - hidden_units)))
        return wide.reshape(own_rows, GROUP, unit_cols).transpose(1, 0, 2)

    ffin_pieces = jnp.concatenate(
        [unit_pieces(ffin_weight[:, :hidden_units]), unit_pieces(ffin_weight[:, hidden_units:])],
        axis=2,
    )
    ffout_pieces = unit_pieces(ffout_weight)

    qkv_cols = gather_weight(qkv_pieces)
    dense_cols = gather_weight(dense_pieces)
    dense_rows = (
        lax.all_to_all(
            dense_cols.reshape(GROUP, slice_width, slice_width),
            TENSOR,
            split_axis=0,
            concat_axis=0,
            tiled=True,
        )
        .transpose(1, 0, 2)
        .reshape(slice_width, model_width)
    )
    ffin_cols = gather_weight(ffin_pieces)
    ffout_cols = gather_weight(ffout_pieces)

    small = lax.all_gather(
        jnp.concatenate([biases, norm_gains], axis=1), AXES, axis=0, tiled=True
    ).astype(F32)
    bias_vals, gain_vals = small[:, :7], small[:, 7:]
    layout = lax.all_gather(
        jnp.concatenate([lengths, prefix], axis=1), TENSOR, axis=0, tiled=True
    )
    docs = lengths.shape[1]
    attention, local_pos, _ = token_layout(layout[:, :docs], layout[:, docs:], seq_len)
    valid_pos = jnp.arange(seq_len, dtype=jnp.int32)[None, :] < jnp.sum(
        lengths, axis=1, keepdims=True
    )
    cosine_table, sine_table = rotary_tables(local_pos, head_dim)

    me = (lax.axis_index("b") * 2 + lax.axis_index("f")) * 2 + lax.axis_index("c")
    my_bias = lax.dynamic_index_in_dim(
        bias_vals[:, 0:3].T.reshape(3, GROUP, slice_width), me, 1, keepdims=False
    ).reshape(-1)

    query_key_value_rows = jnp.dot(tokens_all, qkv_cols, preferred_element_type=F32) + my_bias
    head_shape = (GROUP * sequences, seq_len, my_heads, head_dim)
    query_part = query_key_value_rows[:, :slice_width].reshape(head_shape)
    key_part = query_key_value_rows[:, slice_width : 2 * slice_width].reshape(head_shape)
    q_low = rotate(query_part, cosine_table, sine_table).astype(BF16)
    k_low = rotate(key_part, cosine_table, sine_table).astype(BF16)
    v_low = query_key_value_rows[:, 2 * slice_width :].reshape(head_shape).astype(BF16)
    scores = score_scale * jnp.einsum(
        "sqhe,skhe->shqk", q_low, k_low, preferred_element_type=F32
    )
    masked = jnp.where(attention[:, None], scores, MASKED_SCORE)
    row_max = jnp.max(masked, axis=-1, keepdims=True)
    exponent = jnp.exp(masked - row_max)
    row_total = jnp.sum(exponent, axis=-1, keepdims=True)
    attn_probs = exponent / row_total
    probs_low = attn_probs.astype(BF16)
    context_vectors = jnp.einsum("shqk,skhe->sqhe", probs_low, v_low, preferred_element_type=F32)
    ctx_low = context_vectors.reshape(group_rows, slice_width).astype(BF16)
    attention_output = (
        group_scatter(jnp.dot(ctx_low, dense_rows, preferred_element_type=F32), 1)
        + bias_vals[:, 3]
    )
    resid_one = residual_scale * token_matrix.astype(F32) + attention_output
    first_normalized, norm_one_back = jax.vjp(
        layer_norm, resid_one, gain_vals[:, 0], bias_vals[:, 4]
    )
    normed_all = group_gather(first_normalized.astype(BF16), 2)
    inner_projection = jnp.dot(normed_all, ffin_cols, preferred_element_type=F32)

    def gated_units(both_parts):
        return (
            jax.nn.gelu(both_parts[:, :unit_cols], approximate=False) * both_parts[:, unit_cols:]
        )

    activation_result, gated_back = jax.vjp(gated_units, inner_projection)
    act_low = activation_result.astype(BF16)
    residual_branch = group_scatter(times_transposed(act_low, ffout_cols), 3) + bias_vals[:, 5]
    resid_two = residual_scale * first_normalized + residual_branch
    result, norm_two_back = jax.vjp(layer_norm, resid_two, gain_vals[:, 1], bias_vals[:, 6])

    grad_out = cotangent.reshape(total_rows, model_width).astype(F32)
    grad_out = grad_out * valid_pos.reshape(total_rows, 1).astype(F32)
    d_resid_two, d_gain_two, d_bias_two = norm_two_back(grad_out)
    d_branch = d_resid_two.astype(BF16)
    d_branch_all = group_gather(d_branch, 4)
    d_act = jnp.dot(d_branch_all, ffout_cols, preferred_element_type=F32)
    (d_inner,) = gated_back(d_act)
    d_inner_low = d_inner.astype(BF16)
    ffout_grad = scatter_weight(contract_rows(d_branch_all, act_low))
    d_normed = residual_scale * d_resid_two + group_scatter(
        times_transposed(d_inner_low, ffin_cols), 5
    )
    ffin_grad = scatter_weight(contract_rows(normed_all, d_inner_low))
    d_resid_one, d_gain_one, d_bias_one = norm_one_back(d_normed)
    d_attn = d_resid_one.astype(BF16)
    d_attn_all = group_gather(d_attn, 6)
    d_ctx_low = times_transposed(d_attn_all, dense_rows).reshape(head_shape).astype(BF16)
    dense_grad_rows = contract_rows(ctx_low, d_attn_all).astype(BF16)
    dense_grad = scatter_weight(
        lax.all_to_all(
            dense_grad_rows.reshape(slice_width, GROUP, slice_width).transpose(1, 0, 2),
            TENSOR,
            split_axis=0,
            concat_axis=0,
            tiled=True,
        )
        .reshape(model_width, slice_width)
        .astype(F32)
    )
    d_probs = jnp.einsum("sqhe,skhe->shqk", d_ctx_low, v_low, preferred_element_type=F32)
    d_value = jnp.einsum("shqk,sqhe->skhe", probs_low, d_ctx_low, preferred_element_type=F32)
    d_scores = attn_probs * (d_probs - jnp.sum(attn_probs * d_probs, axis=-1, keepdims=True))
    d_scores_low = jnp.where(attention[:, None], d_scores, 0.0).astype(BF16)
    d_query = score_scale * jnp.einsum(
        "shqk,skhe->sqhe", d_scores_low, k_low, preferred_element_type=F32
    )
    d_key = score_scale * jnp.einsum(
        "shqk,sqhe->skhe", d_scores_low, q_low, preferred_element_type=F32
    )
    d_query = rotate(d_query, cosine_table, -sine_table).reshape(group_rows, slice_width)
    d_key = rotate(d_key, cosine_table, -sine_table).reshape(group_rows, slice_width)
    d_qkv_low = jnp.concatenate(
        [d_query, d_key, d_value.reshape(group_rows, slice_width)], axis=1
    ).astype(BF16)
    qkv_grad = scatter_weight(contract_rows(tokens_all, d_qkv_low))
    d_tokens = residual_scale * d_resid_one + group_scatter(
        times_transposed(d_qkv_low, qkv_cols), 7
    )

    qkv_sums = jnp.sum(d_qkv_low.astype(F32), axis=0).reshape(3, 1, slice_width)
    qkv_sums = jnp.where(
        (jnp.arange(GROUP) == me)[None, :, None], qkv_sums, jnp.zeros_like(qkv_sums)
    ).reshape(3, model_width)
    small_grads = jnp.concatenate(
        [
            qkv_sums,
            jnp.stack(
                [
                    jnp.sum(d_attn.astype(F32), axis=0),
                    d_bias_one,
                    jnp.sum(d_branch.astype(F32), axis=0),
                    d_bias_two,
                    d_gain_one,
                    d_gain_two,
                ]
            ),
        ]
    ).T
    small_grads = lax.psum_scatter(small_grads, AXES, scatter_dimension=0, tiled=True)

    def unit_columns(pieces):
        return (
            pieces.transpose(1, 0, 2).reshape(own_rows, padded)[:, :hidden_units].astype(F32)
        )

    grad_qkv = (
        qkv_grad.reshape(GROUP, own_rows, 3, slice_width)
        .transpose(1, 2, 0, 3)
        .reshape(own_rows, 3 * model_width)
        .astype(F32)
    )
    grad_dense = dense_grad.transpose(1, 0, 2).reshape(own_rows, model_width).astype(F32)
    grad_ffin = jnp.concatenate(
        [unit_columns(ffin_grad[:, :, :unit_cols]), unit_columns(ffin_grad[:, :, unit_cols:])],
        axis=1,
    )
    grad_ffout = unit_columns(ffout_grad)
    return (
        result.astype(BF16).reshape(sequences, seq_len, model_width),
        d_tokens.reshape(sequences, seq_len, model_width),
        grad_qkv,
        grad_dense,
        grad_ffin,
        grad_ffout,
        small_grads[:, :7],
        small_grads[:, 7:],
    )


def solution(mesh):
    dp, fsdp = mesh.shape["dp"], mesh.shape["fsdp"]
    fine = Mesh(mesh.devices.reshape(dp // 2, 2, fsdp // 4, 2, 2), AXES)
    cube, flat = P(AXES, None, None), P(AXES, None)
    return jax.shard_map(
        on_device,
        mesh=fine,
        in_specs=(cube, cube) + (flat,) * 8,
        out_specs=(cube, cube) + (flat,) * 6,
        check_vma=False,
    )
```

time: 2880 us -> 1040 us (0.36)
  waiting for transfers between devices: 2410 us -> 399 us
  Pallas kernels: 0 us -> 213 us
  matrix products: 216 us -> 90.4 us
  starting transfers between devices: 0.32 us -> 58 us
  other arithmetic: 28.1 us -> 71.8 us
    reduce_scatter x2 -> x0, waiting for transfers between devices: 1430 us -> none  [owner_rows(): lax.psum_scatter(term, ('dp', 'fsdp'), scatter_dimension=0, tiled=True)]
    all_gather x4 -> x0, waiting for transfers between devices: 493 us -> none  [the longest x1 247 us: on_device(): lax.all_gather(ffin_weight, ('dp', 'fsdp'), axis=0, tiled=True)]
    unnamed x10 -> x2, waiting for transfers between devices: 482 us -> 135 us
    ppermute x0 -> x16, waiting for transfers between devices: none -> 232 us  [the longest x8 121 us: scatter_axis(): lax.ppermute(out, axis, [(i, (i + shift) % count) for i in range(count)])]
    pallas_call x0 -> x8, Pallas kernels: none -> 213 us  [the longest x4 125 us: group_scatter(): pl.pallas_call(scatter_kernel, out_shape=jax.ShapeDtypeStruct(block, F32)...]
    dot_general x4, matrix products: 83.5 us -> 25 us  [contract_rows(): lax.dot_general(left_rows, right_rows, (((0,), (0,)), ((), ())), preferre...]
    all_to_all x0 -> x10, starting transfers between devices: none -> 39.6 us  [the longest x4 16.6 us: gather_weight(): lax.all_to_all(pieces, TENSOR, split_axis=0, concat_axis=0, tiled=True)]
    dot_general x4, matrix products: 62.8 us -> 24.2 us  [times_transposed(): lax.dot_general(left_rows, weight_rows, (((1,), (1,)), ((), ())), preferr...]
  transfers between devices with their start and end apart: 8 -> 27, of which waited for: 8 -> 14; matrix products, arithmetic and copies ran while one was open for 7% -> 17% of each run, Pallas kernels for 0% -> 12%
where the time goes in v1:
time: 1040 us; the launch traced here: 1030 us
  waiting for transfers between devices  399 us (38%)
  Pallas kernels  213 us (20%)
  local copies, waits for them, and re-layouts  119 us (11%)
  matrix products  90.4 us (9%)
  other arithmetic  71.8 us (7%)
  blocking collectives  65.2 us (6%)
  starting transfers between devices  58 us (6%)
  between operations  16 us (2%)
    unnamed x2, waiting for transfers between devices  135 us
    pallas_call x4, Pallas kernels, group_scatter(): pl.pallas_call(scatter_kernel, out_shape=jax.ShapeDtypeStruct(block, F32)...  125 us
    ppermute x8, waiting for transfers between devices, scatter_axis(): lax.ppermute(out, axis, [(i, (i + shift) % count) for i in range(count)])  121 us
    ppermute x8, waiting for transfers between devices, exchange(): lax.ppermute(x, axis, [(i, (i + shift) % count) for i in range(count)])  111 us
    pallas_call x4, Pallas kernels, group_gather(): pl.pallas_call(gather_kernel, out_shape=jax.ShapeDtypeStruct((GROUP, rows...  87.3 us
    unnamed x180, local copies, waits for them, and re-layouts  46.9 us
    all_gather x1, blocking collectives, on_device(): lax.all_gather(jnp.concatenate([biases, norm_gains], axis=1), AXES, axis=...  41.3 us
    dot_general x4, matrix products, contract_rows(): lax.dot_general(left_rows, right_rows, (((0,), (0,)), ((), ())), preferre...  25 us
  transfers between devices with their start and end apart: 27, of which 14 were waited for; matrix products, arithmetic and copies ran while one was open for 17% of the time, Pallas kernels for 12%

profile of v1, /device:TPU:0, one launch (start us, length us, event | category | flops | bytes accessed | tf_op | source)
XLA Modules:
  0.0 1032.0 jit_solution(14904363936455849677)
XLA Ops:
  8.9 5.2 all-to-all-start.1
  16.6 4.5 all-to-all-done.1
  21.1 3.5 all-to-all-start.4
  27.4 9.8 all-to-all-done.4
  37.2 3.5 all-to-all-start
  43.9 9.4 all-to-all-done
  53.3 4.3 all-to-all-start.3
  57.7 23.9 %all-gather.1 = s32[8,1,8]{2,1,0:T(1,128)S(1)} all-gather(s32[1,1,8]{2,1,0:T(1,128)S(1)} %add_bitcast_fusion.2), channel_id=1, replica_groups=mesh['a'=2,'b'=2,'e'=2,'f'=2,'c'=2] {'b','f','c'}, dimensions={0}, use_global_device_ids=true | all-gather | bytes 288 | tf_op jit(solution)/shard_map/all_gather | solution.py:388
  81.7 41.3 %all-gather = bf16[32,64,9]{1,2,0:T(8,128)(2,1)S(1)} all-gather(bf16[1,64,9]{1,2,0:T(8,128)(2,1)S(1)} %maximum_bitcast_fusion), channel_id=1, replica_groups=mesh['a'=2,'b'=2,'e'=2,'f'=2,'c'=2] {'a','b','e','f','c'}, dimensions={0}, use_global_device_ids=true | all-gather | bytes 38016 | tf_op jit(solution)/shard_map/all_gather | solution.py:384
  123.5 11.8 %collective-permute-done.2 = bf16[2,256,256]{2,1,0:T(8,128)(2,1)S(1)} collective-permute-done((bf16[2,256,256]{2,1,0:T(8,128)(2,1)S(1)}, bf16[2,256,256]{2,1,0:T(8,128)(2,1)S(1)}, u32[]{:S(2)}, u32[]{:S(2)}) %collective-permute-start.2) | collective-permute-done | bytes 262176 | tf_op jit(solution)/shard_map/ppermute | solution.py:282
  136.8 2.9 collective-permute-start
  141.4 8.0 collective-permute-done.3
  151.7 3.6 all-to-all-start.2
  155.3 32.9 %collective-permute-done.6 = bf16[2,256,768]{2,1,0:T(8,128)(2,1)S(1)} collective-permute-done((bf16[2,256,768]{2,1,0:T(8,128)(2,1)S(1)}, bf16[2,256,768]{2,1,0:T(8,128)(2,1)S(1)}, u32[]{:S(2)}, u32[]{:S(2)}) %collective-permute-start.6) | collective-permute-done | bytes 786464 | tf_op jit(solution)/shard_map/ppermute | solution.py:282
  188.2 16.9 %collective-permute-done = bf16[2,256,768]{2,1,0:T(8,128)(2,1)} collective-permute-done((bf16[2,256,768]{2,1,0:T(8,128)(2,1)S(1)}, bf16[2,256,768]{2,1,0:T(8,128)(2,1)}, u32[]{:S(2)}, u32[]{:S(2)}) %collective-permute-start) | collective-permute-done | bytes 786464 | tf_op jit(solution)/shard_map/ppermute | solution.py:282
  211.2 21.6 %shard_map.161 = bf16[8,128,2048]{2,1,0:T(8,128)(2,1)} custom-call(bf16[128,2048]{1,0:T(8,128)(2,1)} %bitcast.359), custom_call_target="tpu_custom_call" | custom-call | bytes 41943040 | tf_op jit(solution)/shard_map/pallas_call | solution.py:154
  234.8 3.1 fusion.65
  251.9 3.0 copy-done.20
  254.9 3.6 add_bitcast_fusion
  272.1 41.6 %collective-permute-done.4 = bf16[2,256,1536]{2,1,0:T(8,128)(2,1)} collective-permute-done((bf16[2,256,1536]{2,1,0:T(8,128)(2,1)}, bf16[2,256,1536]{2,1,0:T(8,128)(2,1)}, u32[]{:S(2)}, u32[]{:S(2)}) %collective-permute-start.4) | collective-permute-done | bytes 1572896 | tf_op jit(solution)/shard_map/ppermute | solution.py:282
  321.6 3.9 fusion.91
  325.6 3.6 fusion.33
  332.0 22.2 %shard_map.162 = f32[128,2048]{1,0:T(8,128)S(1)} custom-call(bf16[8,128,2048]{2,1,0:T(8,128)(2,1)S(1)} %bitcast.311), custom_call_target="tpu_custom_call" | custom-call | bytes 41943040 | tf_op jit(solution)/shard_map/pallas_call | solution.py:253
  356.9 22.3 %shard_map.163 = bf16[8,128,2048]{2,1,0:T(8,128)(2,1)} custom-call(bf16[128,2048]{1,0:T(8,128)(2,1)} %fusion.47.x_ref), custom_call_target="tpu_custom_call" | custom-call | bytes 41943040 | tf_op jit(solution)/shard_map/pallas_call | solution.py:154
  379.2 6.4 copy.286
  391.9 3.4 copy.265
  395.5 8.8 fusion.92
  404.3 7.8 multiply_convert_fusion
  412.0 3.7 convolution_convert_fusion.3
  415.8 22.9 %shard_map.164 = f32[128,2048]{1,0:T(8,128)S(1)} custom-call(bf16[8,128,2048]{2,1,0:T(8,128)(2,1)S(1)} %bitcast.314), custom_call_target="tpu_custom_call" | custom-call | bytes 41943040 | tf_op jit(solution)/shard_map/pallas_call | solution.py:253
  443.2 21.7 %shard_map.165 = bf16[8,128,2048]{2,1,0:T(8,128)(2,1)} custom-call(bf16[128,2048]{1,0:T(8,128)(2,1)} %get-tuple-element.17.x_ref), custom_call_target="tpu_custom_call" | custom-call | bytes 41943040 | tf_op jit(solution)/shard_map/pallas_call | solution.py:154
  464.9 10.2 fusion.42
  475.0 11.1 %convolution_convert_fusion = bf16[1024,2048]{1,0:T(8,128)(2,1)S(1)} fusion(bf16[2048,1536]{1,0:T(8,128)(2,1)} %bitcast.323, f32[1024,768]{1,0:T(8,128)S(1)} %get-tuple-element.34, f32[1024,768]{1,0:T(8,128)S(1)} %get-tuple-element.33), kind=kOutput, calls=%fused_computation.9 | convolution fusion | flops 6447693824 | bytes 16777216 | tf_op jit(solution)/shard_map/dot_general | solution.py:81
  486.2 22.7 %shard_map.166 = f32[128,2048]{1,0:T(8,128)S(1)} custom-call(bf16[8,128,2048]{2,1,0:T(8,128)(2,1)S(1)} %bitcast.312), custom_call_target="tpu_custom_call" | custom-call | bytes 41943040 | tf_op jit(solution)/shard_map/pallas_call | solution.py:253
  512.4 21.7 %shard_map.167 = bf16[8,128,2048]{2,1,0:T(8,128)(2,1)} custom-call(bf16[128,2048]{1,0:T(8,128)(2,1)} %get-tuple-element.19.x_ref), custom_call_target="tpu_custom_call" | custom-call | bytes 41943040 | tf_op jit(solution)/shard_map/pallas_call | solution.py:154
  534.1 3.6 fusion.30
  542.1 3.3 fusion.27
  545.4 3.5 fusion.34
  554.8 3.4 convolution_convert_fusion.4
  559.2 3.8 all-to-all-start.6
  564.2 8.0 convolution_bitcast_fusion
  572.3 9.2 reshape.490
  581.5 3.0 constant_dynamic-slice_fusion
  584.4 3.2 copy.309
  588.3 10.1 fusion.6
  598.4 4.6 copy-done.9
  606.5 6.5 copy.289
  616.1 3.5 fusion.17
  624.9 3.0 constant_dynamic-slice_fusion.1
  627.8 4.0 copy.281
  631.8 72.0 %collective-permute-done.10 = bf16[2,2,256,256]{3,2,1,0:T(8,128)(2,1)} collective-permute-done((bf16[2,2,256,256]{3,2,1,0:T(8,128)(2,1)}, bf16[2,2,256,256]{3,2,1,0:T(8,128)(2,1)}, u32[]{:S(2)}, u32[]{:S(2)}) %collective-permute-start.10) | collective-permute-done | bytes 524320 | tf_op jit(solution)/shard_map/ppermute | solution.py:306
  712.8 24.4 %collective-permute-done.11 = bf16[2,256,256]{2,1,0:T(8,128)(2,1)S(1)} collective-permute-done((bf16[2,256,256]{2,1,0:T(8,128)(2,1)S(1)}, bf16[2,256,256]{2,1,0:T(8,128)(2,1)S(1)}, u32[]{:S(2)}, u32[]{:S(2)}) %collective-permute-start.11) | collective-permute-done | bytes 262176 | tf_op jit(solution)/shard_map/ppermute | solution.py:306
  737.9 3.4 all-to-all-start.7
  741.4 2.9 bitcast_add_fusion.1
  746.6 24.4 %collective-permute-done.9 = bf16[2,256,768]{2,1,0:T(8,128)(2,1)} collective-permute-done((bf16[2,256,768]{2,1,0:T(8,128)(2,1)}, bf16[2,256,768]{2,1,0:T(8,128)(2,1)}, u32[]{:S(2)}, u32[]{:S(2)}) %collective-permute-start.9) | collective-permute-done | bytes 786464 | tf_op jit(solution)/shard_map/ppermute | solution.py:306
  773.2 4.2 all-to-all-start.5
  777.5 5.0 bitcast_add_fusion
  789.4 7.8 all-to-all-done.5
  797.2 3.5 all-to-all-start.9
  800.7 5.9 convolution_convert_fusion.2
  806.6 57.5 %shard_map.168 = f32[128,2048]{1,0:T(8,128)S(1)} custom-call(bf16[8,128,2048]{2,1,0:T(8,128)(2,1)S(1)} %bitcast.313), custom_call_target="tpu_custom_call" | custom-call | bytes 41943040 | tf_op jit(solution)/shard_map/pallas_call | solution.py:253
  864.4 4.0 fusion.8
  868.4 4.4 all-to-all-start.8
  875.7 135.1 %reduce-scatter.4.cloned.1.call-done = f32[64,9]{1,0:T(8,128)} async-done(((f32[2048,9]{1,0:T(8,128)}), f32[64,9]{1,0:T(8,128)}) %reduce-scatter.4.cloned.1.call-update) | async-done | bytes 2320
  (328 shorter events, 142.3 us)
Async XLA Ops:
  8.9 12.2 %all-to-all-start.1 = ((bf16[8,64,256]{2,1,0:T(8,128)(2,1)}), bf16[8,64,256]{2,1,0:T(8,128)(2,1)S(1)}, u32[]{:S(2)}, u32[]{:S(2)}) async-start(bf16[8,64,256]{2,1,0:T(8,128)(2,1)} %copy.261), calls=%async_computation.1 | async-start | bytes 524288 | tf_op jit(solution)/shard_map/all_to_all | solution.py:292
  14.2 10.5 %copy-start.45 = (bf16[64,6144]{1,0:T(8,128)(2,1)S(1)}, bf16[64,6144]{1,0:T(8,128)(2,1)}, u32[]{:S(2)}) copy-start(bf16[64,6144]{1,0:T(8,128)(2,1)} %param.14) | copy-start | bytes 2359300
  16.6 10.4 %copy-start.39 = (bf16[64,10922]{1,0:T(8,128)(2,1)S(1)}, bf16[64,10922]{1,0:T(8,128)(2,1)}, u32[]{:S(2)}) copy-start(bf16[64,10922]{1,0:T(8,128)(2,1)} %param.16) | copy-start | bytes 4194052
  21.1 16.1 %all-to-all-start.4 = ((bf16[8,64,768]{2,1,0:T(8,128)(2,1)}), bf16[8,64,768]{2,1,0:T(8,128)(2,1)S(1)}, u32[]{:S(2)}, u32[]{:S(2)}) async-start(bf16[8,64,768]{2,1,0:T(8,128)(2,1)} %copy.266), calls=%async_computation.4 | async-start | bytes 1572864 | tf_op jit(solution)/shard_map/all_to_all | solution.py:292
  26.9 13.8 %copy-start.64 = (pred[6144]{0:T(1024)(128)(4,1)S(1)}, pred[6144]{0:T(1024)(128)(4,1)}, u32[]{:S(2)}) copy-start(pred[6144]{0:T(1024)(128)(4,1)} %constant.165.clone.1) | copy-start | bytes 18436
  37.2 99.7 %copy-start.26 = (bf16[8,64,768]{2,1,0:T(8,128)(2,1)}, bf16[8,64,768]{2,1,0:T(8,128)(2,1)S(1)}, u32[]{:S(2)}) copy-start(bf16[8,64,768]{2,1,0:T(8,128)(2,1)S(1)} %all-to-all-done.4) | copy-start | bytes 2359300
  37.2 16.1 %all-to-all-start = ((bf16[8,64,768]{2,1,0:T(8,128)(2,1)}), bf16[8,64,768]{2,1,0:T(8,128)(2,1)S(1)}, u32[]{:S(2)}, u32[]{:S(2)}) async-start(bf16[8,64,768]{2,1,0:T(8,128)(2,1)} %reshape.462), calls=%async_computation | async-start | bytes 1572864 | tf_op jit(solution)/shard_map/all_to_all | solution.py:292
  42.2 15.3 %copy-start.73 = (s32[1,4]{1,0:T(1,128)S(1)}, s32[1,4]{1,0:T(1,128)}, u32[]{:S(2)}) copy-start(s32[1,4]{1,0:T(1,128)} %param.13) | copy-start | bytes 52
  42.2 15.3 %copy-start.74 = (s32[1,4]{1,0:T(1,128)S(1)}, s32[1,4]{1,0:T(1,128)}, u32[]{:S(2)}) copy-start(s32[1,4]{1,0:T(1,128)} %param.12) | copy-start | bytes 52
  42.3 39.5 %copy-start.67 = (bf16[64,7]{0,1:T(8,128)(2,1)S(1)}, bf16[64,7]{0,1:T(8,128)(2,1)}, u32[]{:S(2)}) copy-start(bf16[64,7]{0,1:T(8,128)(2,1)} %param.18) | copy-start | bytes 2692
  42.3 39.4 %copy-start.72 = (bf16[64,2]{0,1:T(2,128)(2,1)S(1)}, bf16[64,2]{0,1:T(2,128)(2,1)}, u32[]{:S(2)}) copy-start(bf16[64,2]{0,1:T(2,128)(2,1)} %param.19) | copy-start | bytes 772
  53.3 97.3 %copy-start.27 = (bf16[8,64,768]{2,1,0:T(8,128)(2,1)}, bf16[8,64,768]{2,1,0:T(8,128)(2,1)S(1)}, u32[]{:S(2)}) copy-start(bf16[8,64,768]{2,1,0:T(8,128)(2,1)S(1)} %all-to-all-done) | copy-start | bytes 2359300
  53.3 98.4 %all-to-all-start.3 = ((bf16[8,64,1536]{2,1,0:T(8,128)(2,1)}), bf16[8,64,1536]{2,1,0:T(8,128)(2,1)}, u32[]{:S(2)}, u32[]{:S(2)}) async-start(bf16[8,64,1536]{2,1,0:T(8,128)(2,1)} %copy.264), calls=%async_computation.3 | async-start | bytes 3145728 | tf_op jit(solution)/shard_map/all_to_all | solution.py:292
  123.0 12.3 %collective-permute-start.2 = (bf16[2,256,256]{2,1,0:T(8,128)(2,1)S(1)}, bf16[2,256,256]{2,1,0:T(8,128)(2,1)S(1)}, u32[]{:S(2)}, u32[]{:S(2)}) collective-permute-start(bf16[2,256,256]{2,1,0:T(8,128)(2,1)S(1)} %bitcast.368), channel_id=1, source_target_pairs={{0,4},{4,0},{1,5},{5,1},{2,6},{6,2},{3,7},{7,3},{8,12},{12,8},{9,1... | collective-permute-start | bytes 786440 | tf_op jit(solution)/shard_map/ppermute | solution.py:282
  123.4 13.5 %copy-start.50 = (f32[2048,9]{0,1:T(8,128)}, f32[2048,9]{0,1:T(8,128)S(1)}, u32[]{:S(2)}) copy-start(f32[2048,9]{0,1:T(8,128)S(1)} %reshape.509) | copy-start | bytes 221188
  135.4 14.1 %collective-permute-start.3 = (bf16[2,2,256,256]{3,2,0,1:T(8,128)(2,1)S(1)}, bf16[2,2,256,256]{3,2,0,1:T(8,128)(2,1)}, u32[]{:S(2)}, u32[]{:S(2)}) collective-permute-start(bf16[2,2,256,256]{3,2,0,1:T(8,128)(2,1)S(1)} %pad_maximum_fusion.10), channel_id=1, source_target_pairs={{0,16},{16,0},{1,17},{17,1},{2,18},{18,2},{3,19},{19,3},{4,20},{20... | collective-permute-start | bytes 1572872 | tf_op jit(solution)/shard_map/ppermute | solution.py:282
  136.8 51.4 %collective-permute-start.6 = (bf16[2,256,768]{2,1,0:T(8,128)(2,1)S(1)}, bf16[2,256,768]{2,1,0:T(8,128)(2,1)S(1)}, u32[]{:S(2)}, u32[]{:S(2)}) collective-permute-start(bf16[2,256,768]{2,1,0:T(8,128)(2,1)S(1)} %bitcast.338), channel_id=1, source_target_pairs={{0,4},{4,0},{1,5},{5,1},{2,6},{6,2},{3,7},{7,3},{8,12},{12,8},{9,1... | collective-permute-start | bytes 2359304 | tf_op jit(solution)/shard_map/ppermute | solution.py:282
  136.8 68.2 %collective-permute-start = (bf16[2,256,768]{2,1,0:T(8,128)(2,1)S(1)}, bf16[2,256,768]{2,1,0:T(8,128)(2,1)}, u32[]{:S(2)}, u32[]{:S(2)}) collective-permute-start(bf16[2,256,768]{2,1,0:T(8,128)(2,1)S(1)} %bitcast.340), channel_id=1, source_target_pairs={{0,4},{4,0},{1,5},{5,1},{2,6},{6,2},{3,7},{7,3},{8,12},{12,8},{9,1... | collective-permute-start | bytes 2359304 | tf_op jit(solution)/shard_map/ppermute | solution.py:282
  151.7 92.9 %all-to-all-start.2 = ((bf16[8,256,256]{2,1,0:T(8,128)(2,1)}), bf16[8,256,256]{2,1,0:T(8,128)(2,1)S(1)}, u32[]{:S(2)}, u32[]{:S(2)}) async-start(bf16[8,256,256]{2,1,0:T(8,128)(2,1)} %bitcast.24), calls=%async_computation.2 | async-start | bytes 2097152 | tf_op jit(solution)/shard_map/all_to_all | solution.py:371
  188.2 16.9 %copy-start.44 = (bf16[2,256,768]{2,1,0:T(8,128)(2,1)}, bf16[2,256,768]{2,1,0:T(8,128)(2,1)S(1)}, u32[]{:S(2)}) copy-start(bf16[2,256,768]{2,1,0:T(8,128)(2,1)S(1)} %collective-permute-done.6) | copy-start | bytes 2359300
  207.1 32.5 %copy-start.10 = (bf16[2,1,256,768]{3,2,1,0:T(8,128)(2,1)}, bf16[2,1,256,768]{3,2,1,0:T(8,128)(2,1)S(1)}, u32[]{:S(2)}) copy-start(bf16[2,1,256,768]{3,2,1,0:T(8,128)(2,1)S(1)} %get-tuple-element.56) | copy-start | bytes 2359300
  209.3 40.7 %collective-permute-start.1 = (bf16[2,2,256,768]{3,2,1,0:T(8,128)(2,1)}, bf16[2,2,256,768]{3,2,1,0:T(8,128)(2,1)}, u32[]{:S(2)}, u32[]{:S(2)}) collective-permute-start(bf16[2,2,256,768]{3,2,1,0:T(8,128)(2,1)} %pad_maximum_fusion.4), channel_id=1, source_target_pairs={{0,16},{16,0},{1,17},{17,1},{2,18},{18,2},{3,19},{19,3},{4,20},{20... | collective-permute-start | bytes 4718600 | tf_op jit(solution)/shard_map/ppermute | solution.py:282
  240.9 144.7 %collective-permute-start.7 = (bf16[2,2,256,768]{3,2,1,0:T(8,128)(2,1)}, bf16[2,2,256,768]{3,2,1,0:T(8,128)(2,1)}, u32[]{:S(2)}, u32[]{:S(2)}) collective-permute-start(bf16[2,2,256,768]{3,2,1,0:T(8,128)(2,1)} %pad_maximum_fusion.6), channel_id=1, source_target_pairs={{0,16},{16,0},{1,17},{17,1},{2,18},{18,2},{3,19},{19,3},{4,20},{20... | collective-permute-start | bytes 4718600 | tf_op jit(solution)/shard_map/ppermute | solution.py:282
  242.4 71.3 %collective-permute-start.4 = (bf16[2,256,1536]{2,1,0:T(8,128)(2,1)}, bf16[2,256,1536]{2,1,0:T(8,128)(2,1)}, u32[]{:S(2)}, u32[]{:S(2)}) collective-permute-start(bf16[2,256,1536]{2,1,0:T(8,128)(2,1)} %bitcast.34), channel_id=1, source_target_pairs={{0,4},{4,0},{1,5},{5,1},{2,6},{6,2},{3,7},{7,3},{8,12},{12,8},{9,1... | collective-permute-start | bytes 4718600 | tf_op jit(solution)/shard_map/ppermute | solution.py:282
  244.6 5.4 copy-start.12
  251.9 6.6 copy-start.28
  318.2 69.9 %collective-permute-start.5 = (bf16[2,2,256,1536]{3,2,0,1:T(8,128)(2,1)}, bf16[2,2,256,1536]{3,2,0,1:T(8,128)(2,1)}, u32[]{:S(2)}, u32[]{:S(2)}) collective-permute-start(bf16[2,2,256,1536]{3,2,0,1:T(8,128)(2,1)} %pad_maximum_fusion.2), channel_id=1, source_target_pairs={{0,16},{16,0},{1,17},{17,1},{2,18},{18,2},{3,19},{19,3},{4,20},{20... | collective-permute-start | bytes 9437192 | tf_op jit(solution)/shard_map/ppermute | solution.py:282
  325.6 5.0 copy-start.22
  331.9 22.2 %copy-start.36 = (bf16[1,128,2048]{2,1,0:T(8,128)(2,1)S(1)}, bf16[1,128,2048]{2,1,0:T(8,128)(2,1)}, u32[]{:S(2)}) copy-start(bf16[1,128,2048]{2,1,0:T(8,128)(2,1)} %param.10) | copy-start | bytes 1572868
  332.0 22.2 %copy-start.55 = (f32[2048,1]{0,1:T(1,128)S(1)}, f32[2048,1]{0,1:T(1,128)}, u32[]{:S(2)}) copy-start(f32[2048,1]{0,1:T(1,128)} %get-tuple-element.77) | copy-start | bytes 24580
  387.7 24.3 %copy-start.29 = (bf16[2,2,2,256,768]{4,3,2,1,0:T(8,128)(2,1)}, bf16[2,2,2,256,768]{4,3,2,1,0:T(8,128)(2,1)S(1)}, u32[]{:S(2)}) copy-start(bf16[2,2,2,256,768]{4,3,2,1,0:T(8,128)(2,1)S(1)} %pad_maximum_fusion.3) | copy-start | bytes 9437188
  404.3 7.8 copy-start.14
  415.7 23.0 %copy-start.52 = (f32[2048,1]{0,1:T(1,128)S(1)}, f32[2048,1]{0,1:T(1,128)}, u32[]{:S(2)}) copy-start(f32[2048,1]{0,1:T(1,128)} %get-tuple-element.75) | copy-start | bytes 24580
  415.8 23.0 %copy-start.54 = (f32[2048,1]{0,1:T(1,128)S(1)}, f32[2048,1]{0,1:T(1,128)}, u32[]{:S(2)}) copy-start(f32[2048,1]{0,1:T(1,128)} %get-tuple-element.74) | copy-start | bytes 24580
  415.8 23.0 %copy-start.61 = (f32[128]{0:T(128)S(1)}, f32[128]{0:T(128)}, u32[]{:S(2)}) copy-start(f32[128]{0:T(128)} %copy-done.60) | copy-start | bytes 1540
  415.8 23.0 %copy-start.63 = (f32[128]{0:T(128)S(1)}, f32[128]{0:T(128)}, u32[]{:S(2)}) copy-start(f32[128]{0:T(128)} %copy-done.62) | copy-start | bytes 1540
  475.0 11.1 %copy-start.76 = (f32[1024,768]{1,0:T(8,128)}, f32[1024,768]{1,0:T(8,128)S(1)}, u32[]{:S(2)}) copy-start(f32[1024,768]{1,0:T(8,128)S(1)} %get-tuple-element.33) | copy-start | bytes 9437188
  475.0 11.1 %copy-start.77 = (f32[1024,768]{1,0:T(8,128)}, f32[1024,768]{1,0:T(8,128)S(1)}, u32[]{:S(2)}) copy-start(f32[1024,768]{1,0:T(8,128)S(1)} %get-tuple-element.34) | copy-start | bytes 9437188
  511.5 22.6 %copy-start.42 = (bf16[2,128,2048,1]{2,1,0,3:T(8,128)(2,1)S(1)}, bf16[2,128,2048,1]{2,1,0,3:T(8,128)(2,1)}, u32[]{:S(2)}) copy-start(bf16[2,128,2048,1]{2,1,0,3:T(8,128)(2,1)} %reshape.511) | copy-start | bytes 3145732
  534.1 5.4 copy-start.46
  534.1 5.4 copy-start.75
  558.2 4.8 copy-start.30
  559.2 53.8 %all-to-all-start.6 = ((bf16[8,256,256]{2,1,0:T(8,128)(2,1)}), bf16[8,256,256]{2,1,0:T(8,128)(2,1)S(1)}, u32[]{:S(2)}, u32[]{:S(2)}) async-start(bf16[8,256,256]{2,1,0:T(8,128)(2,1)} %bitcast.304), calls=%async_computation.6 | async-start | bytes 2097152 | tf_op jit(solution)/shard_map/all_to_all | solution.py:462
  564.2 8.0 copy-start.31
  587.7 120.0 %collective-permute-start.8 = (bf16[2,2,256,768]{3,2,0,1:T(8,128)(2,1)}, bf16[2,2,256,768]{3,2,0,1:T(8,128)(2,1)}, u32[]{:S(2)}, u32[]{:S(2)}) collective-permute-start(bf16[2,2,256,768]{3,2,0,1:T(8,128)(2,1)} %bitcast.364), channel_id=1, source_target_pairs={{0,16},{16,0},{1,17},{17,1},{2,18},{18,2},{3,19},{19,3},{4,20},{20... | collective-permute-start | bytes 4718600 | tf_op jit(solution)/shard_map/ppermute | solution.py:306
  605.1 172.4 %collective-permute-start.12 = (bf16[2,2,256,1536]{3,2,1,0:T(8,128)(2,1)}, bf16[2,2,256,1536]{3,2,1,0:T(8,128)(2,1)}, u32[]{:S(2)}, u32[]{:S(2)}) collective-permute-start(bf16[2,2,256,1536]{3,2,1,0:T(8,128)(2,1)} %fusion.5), channel_id=1, source_target_pairs={{0,16},{16,0},{1,17},{17,1},{2,18},{18,2},{3,19},{19,3},{4,20},{20... | collective-permute-start | bytes 9437192 | tf_op jit(solution)/shard_map/ppermute | solution.py:306
  606.5 9.5 copy-start.41
  615.4 88.5 %collective-permute-start.10 = (bf16[2,2,256,256]{3,2,1,0:T(8,128)(2,1)}, bf16[2,2,256,256]{3,2,1,0:T(8,128)(2,1)}, u32[]{:S(2)}, u32[]{:S(2)}) collective-permute-start(bf16[2,2,256,256]{3,2,1,0:T(8,128)(2,1)} %fusion.51), channel_id=1, source_target_pairs={{0,16},{16,0},{1,17},{17,1},{2,18},{18,2},{3,19},{19,3},{4,20},{20... | collective-permute-start | bytes 1572872 | tf_op jit(solution)/shard_map/ppermute | solution.py:306
  623.6 117.7 %collective-permute-start.14 = (bf16[2,2,256,768]{3,2,1,0:T(8,128)(2,1)}, bf16[2,2,256,768]{3,2,1,0:T(8,128)(2,1)}, u32[]{:S(2)}, u32[]{:S(2)}) collective-permute-start(bf16[2,2,256,768]{3,2,1,0:T(8,128)(2,1)} %fusion.16), channel_id=1, source_target_pairs={{0,16},{16,0},{1,17},{17,1},{2,18},{18,2},{3,19},{19,3},{4,20},{20... | collective-permute-start | bytes 4718600 | tf_op jit(solution)/shard_map/ppermute | solution.py:306
  631.8 75.8 %copy-start.4 = (f32[1,2,2,256,768]{4,3,1,2,0:T(8,128)S(1)}, f32[1,2,2,256,768]{4,3,1,2,0:T(8,128)}, u32[]{:S(2)}) copy-start(f32[1,2,2,256,768]{4,3,1,2,0:T(8,128)} %copy.281) | copy-start | bytes 9437188
  705.4 31.8 %collective-permute-start.11 = (bf16[2,256,256]{2,1,0:T(8,128)(2,1)S(1)}, bf16[2,256,256]{2,1,0:T(8,128)(2,1)S(1)}, u32[]{:S(2)}, u32[]{:S(2)}) collective-permute-start(bf16[2,256,256]{2,1,0:T(8,128)(2,1)S(1)} %fusion.62), channel_id=1, source_target_pairs={{0,4},{4,0},{1,5},{5,1},{2,6},{6,2},{3,7},{7,3},{8,12},{12,8},{9,1... | collective-permute-start | bytes 786440 | tf_op jit(solution)/shard_map/ppermute | solution.py:306
  712.0 59.0 %collective-permute-start.9 = (bf16[2,256,768]{2,1,0:T(8,128)(2,1)}, bf16[2,256,768]{2,1,0:T(8,128)(2,1)}, u32[]{:S(2)}, u32[]{:S(2)}) collective-permute-start(bf16[2,256,768]{2,1,0:T(8,128)(2,1)} %fusion.48), channel_id=1, source_target_pairs={{0,4},{4,0},{1,5},{5,1},{2,6},{6,2},{3,7},{7,3},{8,12},{12,8},{9,1... | collective-permute-start | bytes 2359304 | tf_op jit(solution)/shard_map/ppermute | solution.py:306
  737.9 35.3 %all-to-all-start.7 = ((bf16[8,64,256]{2,1,0:T(8,128)(2,1)}), bf16[8,64,256]{2,1,0:T(8,128)(2,1)S(1)}, u32[]{:S(2)}, u32[]{:S(2)}) async-start(bf16[8,64,256]{2,1,0:T(8,128)(2,1)} %bitcast.78), calls=%async_computation.7 | async-start | bytes 524288 | tf_op jit(solution)/shard_map/all_to_all | solution.py:319
  741.3 29.7 %copy-start.6 = (f32[2,2,256,768]{3,2,0,1:T(8,128)S(1)}, f32[2,2,256,768]{3,2,0,1:T(8,128)}, u32[]{:S(2)}) copy-start(f32[2,2,256,768]{3,2,0,1:T(8,128)} %copy-done.5) | copy-start | bytes 9437188
  745.2 42.0 %collective-permute-start.15 = (bf16[2,256,768]{2,1,0:T(8,128)(2,1)}, bf16[2,256,768]{2,1,0:T(8,128)(2,1)}, u32[]{:S(2)}, u32[]{:S(2)}) collective-permute-start(bf16[2,256,768]{2,1,0:T(8,128)(2,1)} %fusion.49), channel_id=1, source_target_pairs={{0,4},{4,0},{1,5},{5,1},{2,6},{6,2},{3,7},{7,3},{8,12},{12,8},{9,1... | collective-permute-start | bytes 2359304 | tf_op jit(solution)/shard_map/ppermute | solution.py:306
  773.2 23.9 %all-to-all-start.5 = ((bf16[8,64,768]{2,1,0:T(8,128)(2,1)}), bf16[8,64,768]{2,1,0:T(8,128)(2,1)}, u32[]{:S(2)}, u32[]{:S(2)}) async-start(bf16[8,64,768]{2,1,0:T(8,128)(2,1)} %bitcast.354), calls=%async_computation.5 | async-start | bytes 1572864 | tf_op jit(solution)/shard_map/all_to_all | solution.py:319
  786.5 78.0 %collective-permute-start.13 = (bf16[2,256,1536]{2,1,0:T(8,128)(2,1)}, bf16[2,256,1536]{2,1,0:T(8,128)(2,1)}, u32[]{:S(2)}, u32[]{:S(2)}) collective-permute-start(bf16[2,256,1536]{2,1,0:T(8,128)(2,1)} %fusion.15), channel_id=1, source_target_pairs={{0,4},{4,0},{1,5},{5,1},{2,6},{6,2},{3,7},{7,3},{8,12},{12,8},{9,1... | collective-permute-start | bytes 4718600 | tf_op jit(solution)/shard_map/ppermute | solution.py:306
  797.2 71.3 %all-to-all-start.9 = ((bf16[8,64,768]{2,1,0:T(8,128)(2,1)}), bf16[8,64,768]{2,1,0:T(8,128)(2,1)S(1)}, u32[]{:S(2)}, u32[]{:S(2)}) async-start(bf16[8,64,768]{2,1,0:T(8,128)(2,1)} %bitcast.355), calls=%async_computation.9 | async-start | bytes 1572864 | tf_op jit(solution)/shard_map/all_to_all | solution.py:319
  806.6 57.5 %copy-start.32 = (bf16[1024,768]{0,1:T(8,128)(2,1)S(1)}, bf16[1024,768]{0,1:T(8,128)(2,1)}, u32[]{:S(2)}) copy-start(bf16[1024,768]{0,1:T(8,128)(2,1)} %copy-done.31) | copy-start | bytes 4718596
  868.4 4.6 copy-start.59
  868.4 6.1 copy-start.8
  868.4 6.1 copy-start.69
  868.4 152.7 %all-to-all-start.8 = ((bf16[8,64,1536]{2,1,0:T(8,128)(2,1)}), bf16[8,64,1536]{2,1,0:T(8,128)(2,1)}, u32[]{:S(2)}, u32[]{:S(2)}) async-start(bf16[8,64,1536]{2,1,0:T(8,128)(2,1)} %bitcast.325), calls=%async_computation.8 | async-start | bytes 3145728 | tf_op jit(solution)/shard_map/all_to_all | solution.py:319
  872.9 137.9 %reduce-scatter.4.cloned.1.call-start = ((), (), s32[]{:S(2)}) async-start(), calls=%async_computation.11 | async-start | bytes 1081344
  (41 other events, 98.7 us)
Sparse Core Ops, SparseCore 0:
  876.6 134.1 reduce-scatter.3

commit v2 on v0

v2 whole, which is shorter than its diff:
```python
import functools
import math

import jax
import jax.numpy as jnp
import numpy as np
from jax import lax
from jax.experimental import pallas as pl
from jax.experimental.pallas import tpu as pltpu
from jax.sharding import Mesh
from jax.sharding import PartitionSpec as P

HEADS = 16
LAYERS = 24
MASKED_SCORE = -1e30
EPSILON = 1e-05
ROPE_BASE = 10000.0

AXES = ("a", "b", "e", "f", "c")
GROUP = 8
LANES = 128
DEVICE_MESH = pl.DeviceIdType.MESH
BF16 = jnp.bfloat16
F32 = jnp.float32
NT = (((1,), (1,)), ((), ()))
TN = (((0,), (0,)), ((), ()))


def dot(left, right, dims=(((1,), (0,)), ((), ()))):
    return lax.dot_general(left, right, dims, preferred_element_type=F32)


def span(start, size):
    return pl.ds(pl.multiple_of(start, size), size)


class Wires:
    def __init__(self, send_sem, recv_sem):
        self.send_sem, self.recv_sem, self.count = send_sem, recv_sem, 0

    def take(self, numbers=1):
        first = self.count
        self.count += numbers
        return first

    def send(self, number, source, target, device):
        one = pltpu.make_async_remote_copy(
            src_ref=source,
            dst_ref=target,
            send_sem=self.send_sem.at[number],
            recv_sem=self.recv_sem.at[number],
            device_id=device,
            device_id_type=DEVICE_MESH,
        )
        one.start()
        return one

    def arrived(self, number, landing):
        pltpu.make_async_copy(landing, landing, self.recv_sem.at[number]).wait()


def sent(copies):
    for one in copies:
        one.wait_send()
    copies.clear()


def layer_kernel(
    sizes,
    x_ref,
    cot_ref,
    table_ref,
    qp_ref,
    dp_ref,
    ip_ref,
    op_ref,
    out_ref,
    gx_ref,
    oq_ref,
    od_ref,
    oi_ref,
    oo_ref,
    yq_ref,
    yi_ref,
    yo_ref,
    zq_ref,
    zi_ref,
    zo_ref,
    wq_ref,
    wd_ref,
    wi_ref,
    wo_ref,
    xg_ref,
    hg_ref,
    dg_ref,
    uf_ref,
    mb_ref,
    du_ref,
    qk_ref,
    cx_ref,
    dc_ref,
    pb_ref,
    core_ref,
    stage_ref,
    relay_ref,
    land_ref,
    sum_ref,
    xh_ref,
    dr_ref,
    rstd_ref,
    bt_ref,
    sg_ref,
    qb_ref,
    tm_ref,
    local_sem,
    send_sem,
    recv_sem,
):
    A, E, R, rows, width, sw, uc, alpha, scale = sizes
    a, b, e, f, c = (lax.axis_index(axis) for axis in AXES)
    qc = 3 * sw
    all_rows = GROUP * rows
    half_rows = all_rows // 2
    slot = lambda bb, ff, cc: cc * 4 + bb * 2 + ff
    me = slot(b, f, c)
    my_rows = span(me * rows, rows)
    flip = lambda v, d: lax.rem(v + d, 2)
    rank = lambda aa, bb, ee, ff, cc: (((aa * 2 + bb) * E + ee) * 2 + ff) * 2 + cc
    line = lambda aa, bb, ee, ff, cc: span(rank(aa, bb, ee, ff, cc) * R, R)
    block = lambda aa, bb, ee: span(((aa * 2 + bb) * E + ee) * 4 * R, 4 * R)
    half = lambda aa, bb: span((aa * 2 + bb) * E * 4 * R, E * 4 * R)
    wires = Wires(send_sem, recv_sem)
    peers = [(r // 4, r // 2 % 2, r % 2) for r in range(GROUP)]

    barrier = pltpu.get_barrier_semaphore()
    others = 0
    for da in range(A):
        for de in range(E):
            for db, df, dc in peers:
                if da + de + db + df + dc:
                    pl.semaphore_signal(
                        barrier,
                        inc=1,
                        device_id={
                            "a": lax.rem(a + da, A),
                            "b": flip(b, db),
                            "e": lax.rem(e + de, E),
                            "f": flip(f, df),
                            "c": flip(c, dc),
                        },
                        device_id_type=DEVICE_MESH,
                    )
                    others += 1
    pl.semaphore_wait(barrier, others)

    class Weight:
        def __init__(self, index, pieces, buf, out, ylanding, zlanding):
            self.index, self.pieces, self.buf, self.out = index, pieces, buf, out
            self.ylanding, self.zlanding = ylanding, zlanding
            self.copies = []
            self.tp, self.z, self.y = (
                wires.take(GROUP),
                wires.take(2 * (E - 1)),
                wires.take(2 * E * (A - 1)),
            )
            self.gtp, self.gz, self.gy = (
                wires.take(GROUP),
                wires.take(2 * (E - 1)),
                wires.take(2 * (A - 1)),
            )

        def send(self, *copy):
            self.copies.append(wires.send(*copy))

        def own(self):
            return pltpu.make_async_copy(
                self.pieces.at[me], self.buf.at[line(a, b, e, f, c)], local_sem.at[self.index]
            )

        def tp_send(self):
            self.own().start()
            for r in range(1, GROUP):
                db, df, dc = peers[r]
                bb, ff, cc = flip(b, db), flip(f, df), flip(c, dc)
                self.send(
                    self.tp + r,
                    self.pieces.at[slot(bb, ff, cc)],
                    self.buf.at[line(a, b, e, f, c)],
                    {"b": bb, "f": ff, "c": cc},
                )

        def tp_arrive(self, db):
            for r in range(4 * db, 4 * db + 4):
                if r == 0:
                    self.own().wait()
                else:
                    _, df, dc = peers[r]
                    wires.arrived(
                        self.tp + r, self.buf.at[line(a, flip(b, db), e, flip(f, df), flip(c, dc))]
                    )
            for s in range(1, E):
                rows_ = self.buf.at[block(a, flip(b, db), e)]
                self.send(
                    self.z + db * (E - 1) + s - 1, rows_, rows_, {"e": lax.rem(e + s, E)}
                )
            self.y_send(db, 0)

        def y_send(self, db, s):
            rows_ = self.buf.at[block(a, flip(b, db), lax.rem(e + E - s, E))]
            for t in range(1, A):
                self.send(
                    self.y + (db * E + s) * (A - 1) + t - 1, rows_, rows_, {"a": lax.rem(a + t, A)}
                )

        def z_arrive(self, db):
            for s in range(1, E):
                wires.arrived(
                    self.z + db * (E - 1) + s - 1,
                    self.buf.at[block(a, flip(b, db), lax.rem(e + E - s, E))],
                )
                self.y_send(db, s)

        def y_arrive(self):
            for db in range(2):
                for s in range(E):
                    for t in range(1, A):
                        wires.arrived(
                            self.y + (db * E + s) * (A - 1) + t - 1,
                            self.buf.at[
                                block(lax.rem(a + A - t, A), flip(b, db), lax.rem(e + E - s, E))
                            ],
                        )

        def add(self, landing, base, count):
            cols = self.buf.shape[1]
            temp = tm_ref.at[pl.ds(0, count), pl.ds(0, cols)]
            load = pltpu.make_async_copy(landing, temp, local_sem.at[3])
            load.start()
            load.wait()

            @pl.loop(0, count // 16)
            def _(i):
                here = pl.ds(pl.multiple_of(base + i * 16, 16), 16)
                there = span(i * 16, 16)
                self.buf[here, :] = (
                    self.buf[here, :].astype(F32) + tm_ref[there, 0:cols].astype(F32)
                ).astype(BF16)

        def gy_send(self, db):
            bb = flip(b, db)
            for t in range(1, A):
                to = lax.rem(a + t, A)
                self.send(
                    self.gy + db * (A - 1) + t - 1,
                    self.buf.at[half(to, bb)],
                    self.ylanding.at[t - 1, db],
                    {"a": to},
                )

        def gy_add(self, db):
            bb = flip(b, db)
            for t in range(1, A):
                landing = self.ylanding.at[t - 1, db]
                wires.arrived(self.gy + db * (A - 1) + t - 1, landing)
                self.add(landing, (a * 2 + bb) * E * 4 * R, E * 4 * R)
            for s in range(1, E):
                to = lax.rem(e + s, E)
                self.send(
                    self.gz + db * (E - 1) + s - 1,
                    self.buf.at[block(a, bb, to)],
                    self.zlanding.at[s - 1, db],
                    {"e": to},
                )

        def gz_add(self, db):
            bb = flip(b, db)
            for s in range(1, E):
                landing = self.zlanding.at[s - 1, db]
                wires.arrived(self.gz + db * (E - 1) + s - 1, landing)
                self.add(landing, ((a * 2 + bb) * E + e) * 4 * R, 4 * R)
            for r in range(4 * db, 4 * db + 4):
                _, df, dc = peers[r]
                ff, cc = flip(f, df), flip(c, dc)
                rows_ = self.buf.at[line(a, bb, e, ff, cc)]
                if r == 0:
                    pltpu.make_async_copy(rows_, self.out.at[me], local_sem.at[self.index]).start()
                else:
                    self.send(
                        self.gtp + r, rows_, self.out.at[me], {"b": bb, "f": ff, "c": cc}
                    )

        def g_end(self):
            for r in range(GROUP):
                db, df, dc = peers[r]
                if r == 0:
                    pltpu.make_async_copy(
                        self.buf.at[line(a, b, e, f, c)],
                        self.out.at[me],
                        local_sem.at[self.index],
                    ).wait()
                else:
                    wires.arrived(
                        self.gtp + r, self.out.at[slot(flip(b, db), flip(f, df), flip(c, dc))]
                    )

    q_w = Weight(0, qp_ref, wq_ref, oq_ref, yq_ref, zq_ref)
    i_w = Weight(1, ip_ref, wi_ref, oi_ref, yi_ref, zi_ref)
    o_w = Weight(2, op_ref, wo_ref, oo_ref, yo_ref, zo_ref)

    dense_pieces = wd_ref.shape[0] // R
    dense_first = wires.take(dense_pieces)
    dense_sends = wires.take(A * E)
    dense_back = wires.take(A * E)
    dense_back_sends = wires.take(dense_pieces)
    first_row = rank(a, b, e, f, c) * R
    head = first_row // LANES

    def dense_route(aa, ee):
        piece = (head // 8) * (LANES // R) + lax.rem(first_row, LANES) // R
        target = {
            "a": aa,
            "b": lax.rem(head // 4, 2),
            "e": ee,
            "f": lax.rem(head, 2),
            "c": lax.rem(head // 2, 2),
        }
        return piece, target

    def is_me(target):
        same = target["a"] == a
        for axis, mine in (("b", b), ("e", e), ("f", f), ("c", c)):
            same = same & (target[axis] == mine)
        return same

    def remote(source, landing, send, recv, target):
        return pltpu.make_async_remote_copy(
            src_ref=source,
            dst_ref=landing,
            send_sem=send_sem.at[send],
            recv_sem=recv_sem.at[recv],
            device_id=target,
            device_id_type=DEVICE_MESH,
        )

    def dense_out(start):
        for da in range(A):
            for de in range(E):
                piece, target = dense_route(lax.rem(a + da, A), lax.rem(e + de, E))
                landing = wd_ref.at[span(piece * R, R)]
                away = remote(
                    dp_ref, landing, dense_sends + da * E + de, dense_first + piece, target
                )
                if da + de:
                    away.start() if start else away.wait_send()
                else:
                    here = is_me(target)

                    @pl.when(here)
                    def _():
                        if start:
                            pltpu.make_async_copy(
                                dp_ref, landing, recv_sem.at[dense_first + piece]
                            ).start()

                    @pl.when(jnp.logical_not(here))
                    def _():
                        away.start() if start else away.wait_send()

    def dense_arrive():
        for piece in range(dense_pieces):
            wires.arrived(dense_first + piece, wd_ref.at[pl.ds(piece * R, R)])

    def dense_grad_out(start):
        for piece in range(dense_pieces):
            i, offset = piece * R // LANES, piece * R % LANES
            owner = ((i * 8 + b * 4 + c * 2 + f) * LANES + offset) // R
            target = {
                "a": owner // (8 * E),
                "b": lax.rem(owner // (4 * E), 2),
                "e": lax.rem(owner // 4, E),
                "f": lax.rem(owner // 2, 2),
                "c": lax.rem(owner, 2),
            }
            from_ = a * E + e
            source = wd_ref.at[pl.ds(piece * R, R)]
            away = remote(
                source, od_ref.at[from_], dense_back_sends + piece, dense_back + from_, target
            )
            here = is_me(target)

            @pl.when(here)
            def _():
                if start:
                    pltpu.make_async_copy(
                        source, od_ref.at[from_], recv_sem.at[dense_back + from_]
                    ).start()

            @pl.when(jnp.logical_not(here))
            def _():
                away.start() if start else away.wait_send()

    def dense_grad_arrive():
        for k in range(A * E):
            wires.arrived(dense_back + k, od_ref.at[k])

    to_b, to_f, to_c = {"b": 1 - b}, {"f": 1 - f}, {"c": 1 - c}
    nb, nf, dg = slot(1 - b, f, c), slot(b, 1 - f, c), slot(1 - b, 1 - f, c)

    class Gather:
        def __init__(self, buf):
            self.buf, self.first, self.copies = buf, wires.take(10), []

        def part(self, place, which):
            if which is None:
                return self.buf.at[span(place * rows, rows)]
            return self.buf.at[span(place * rows + which * (rows // 2), rows // 2)]

        def copy(self, number, place, which, device):
            here = self.part(place, which)
            self.copies.append(wires.send(self.first + number, here, here, device))

        def landed(self, number, place, which):
            wires.arrived(self.first + number, self.part(place, which))

        def start(self):
            self.copy(0, me, 0, to_b)
            self.copy(1, me, 1, to_f)
            self.copy(2, me, 1, to_b)
            self.copy(3, me, 0, to_f)
            self.copy(4, me, None, to_c)

        def relay(self):
            self.landed(0, nb, 0)
            self.copy(5, nb, 0, to_f)
            self.landed(1, nf, 1)
            self.copy(6, nf, 1, to_b)
            self.landed(2, nb, 1)
            self.copy(7, nb, None, to_c)
            self.landed(3, nf, 0)
            self.copy(8, nf, None, to_c)

        def finish(self):
            self.landed(5, dg, 0)
            self.landed(6, dg, 1)
            self.copy(9, dg, None, to_c)
            other = 1 - c
            self.landed(4, slot(b, f, other), None)
            self.landed(7, slot(1 - b, f, other), None)
            self.landed(8, slot(b, 1 - f, other), None)
            self.landed(9, slot(1 - b, 1 - f, other), None)

    step = 16
    places = [(1 - b, 1 - f), (1 - b, f), (b, 1 - f), (b, f)]

    def accumulate(target, at, count, terms):
        @pl.loop(0, count // step)
        def _(i):
            window = pl.ds(pl.multiple_of(at + i * step, step), step)
            total = terms[0][window, :].astype(F32)
            for term in terms[1:]:
                total = total + term[window, :].astype(F32)
            target[window, :] = total.astype(target.dtype)

    def scatter(multiply, meanwhile=None):
        first, copies = wires.take(10), []

        def send(*copy):
            copies.append(wires.send(*copy))

        multiply((1 - c) * half_rows, half_rows)
        for k, (bb, ff) in enumerate(places):
            send(
                first + k,
                pb_ref.at[span(slot(bb, ff, 1 - c) * rows, rows)],
                core_ref.at[pl.ds(k * rows, rows)],
                to_c,
            )
        multiply(c * half_rows, half_rows)
        own = [pb_ref.at[span(slot(bb, ff, c) * rows, rows)] for bb, ff in places]
        core = [core_ref.at[pl.ds(k * rows, rows)] for k in range(4)]
        mid = rows // 2
        low, high = pl.ds(0, mid), pl.ds(mid, mid)
        if meanwhile is not None:
            meanwhile()
        wires.arrived(first, core[0])
        accumulate(stage_ref.at[0], 0, rows, [own[0], core[0]])
        send(first + 4, stage_ref.at[0, low], relay_ref.at[low], to_b)
        send(first + 5, stage_ref.at[0, high], relay_ref.at[high], to_f)
        wires.arrived(first + 1, core[1])
        accumulate(stage_ref.at[1], 0, mid, [own[1], core[1]])
        send(first + 6, stage_ref.at[1, low], land_ref.at[0, low], to_b)
        wires.arrived(first + 2, core[2])
        accumulate(stage_ref.at[2], mid, mid, [own[2], core[2]])
        send(first + 7, stage_ref.at[2, high], land_ref.at[1, high], to_f)
        wires.arrived(first + 5, relay_ref.at[high])
        accumulate(stage_ref.at[1], mid, mid, [own[1], core[1], relay_ref])
        send(first + 8, stage_ref.at[1, high], land_ref.at[0, high], to_b)
        wires.arrived(first + 4, relay_ref.at[low])
        accumulate(stage_ref.at[2], 0, mid, [own[2], core[2], relay_ref])
        send(first + 9, stage_ref.at[2, low], land_ref.at[1, low], to_f)
        wires.arrived(first + 3, core[3])
        wires.arrived(first + 6, land_ref.at[0, low])
        wires.arrived(first + 7, land_ref.at[1, high])
        wires.arrived(first + 8, land_ref.at[0, high])
        wires.arrived(first + 9, land_ref.at[1, low])
        accumulate(sum_ref, 0, rows, [own[3], core[3], land_ref.at[0], land_ref.at[1]])
        sent(copies)

    def blocks(count_m, count_n, body):
        @pl.loop(0, count_m * count_n)
        def _(k):
            body(k // count_n, lax.rem(k, count_n))

    def onto_partial(left, weight, cols):
        def multiply(first, count):
            def body(m, n):
                here = pl.ds(pl.multiple_of(first, half_rows) + m * 512, 512)
                pb_ref[here, span(n * 512, 512)] = dot(
                    left[here, :], weight[span(n * 512, 512), 0:cols], NT
                ).astype(BF16)

            blocks(count // 512, width // 512, body)

        return multiply

    q_w.tp_send()
    own_x = pltpu.make_async_copy(x_ref, xg_ref.at[my_rows], local_sem.at[4])
    own_x.start()
    dense_out(True)
    sg_ref[...] = jnp.zeros_like(sg_ref)
    q_w.tp_arrive(0)
    q_w.tp_arrive(1)
    own_x.wait()
    tokens = Gather(xg_ref)
    tokens.start()
    i_w.tp_send()
    tokens.relay()
    q_w.z_arrive(0)
    tokens.finish()
    q_w.z_arrive(1)
    i_w.tp_arrive(0)
    i_w.tp_arrive(1)
    o_w.tp_send()
    q_w.y_arrive()

    @pl.loop(0, width // LANES)
    def _(k):
        here = span(k * LANES, LANES)
        turned = wq_ref[here, qc : qc + LANES].astype(F32).T
        bt_ref[:, here] = turned[0:16, :]

    heads = [i * 8 + b * 4 + c * 2 + f for i in range(sw // LANES)]
    for t in range(3):
        for i, number in enumerate(heads):
            at = t * sw + i * LANES
            qb_ref[0:1, at : at + LANES] = bt_ref[t : t + 1, span(number * LANES, LANES)]

    def projection(m, n):
        here, cols = span(m * 512, 512), span(n * sw, sw)
        uf_ref[here, cols] = (
            dot(xg_ref[here, 0:width], wq_ref[:, cols]) + qb_ref[0:1, cols]
        )

    blocks(all_rows // 512, 3, projection)

    row_at = lax.broadcasted_iota(jnp.int32, (rows, rows), 0)
    col_at = lax.broadcasted_iota(jnp.int32, (rows, rows), 1)

    def sequence(s):
        here = span(s * rows, rows)
        info = xg_ref[here, width : width + LANES].astype(F32)
        turned = info.T
        allowed = (info[:, 0:1] == turned[0:1, :]) & (
            (turned[2:3, :] < info[:, 1:2]) | (col_at <= row_at)
        )
        picked = (info[:, 2:3] == col_at.astype(F32)).astype(BF16)
        parts = dot(picked, table_ref[...])
        cos_sin = parts[:, 0:LANES] + parts[:, LANES : 2 * LANES] + parts[:, 2 * LANES :]
        swapped = pltpu.roll(cos_sin, LANES // 2, axis=1)
        first = col_at < LANES // 2
        cosine = jnp.where(first, cos_sin, swapped)
        sine = jnp.where(first, -swapped, cos_sin)
        return here, allowed, cosine, sine

    def turn(value, cosine, sine):
        return value * cosine + pltpu.roll(value, LANES // 2, axis=1) * sine

    def softmax(q, k, allowed):
        scores = jnp.where(allowed, scale * dot(q, k, NT), MASKED_SCORE)
        power = jnp.exp(scores - jnp.max(scores, axis=1, keepdims=True))
        return power / jnp.sum(power, axis=1, keepdims=True)

    @pl.loop(0, GROUP)
    def _(s):
        here, allowed, cosine, sine = sequence(s)
        for i in range(sw // LANES):
            cols = [pl.ds(t * sw + i * LANES, LANES) for t in range(3)]
            q = turn(uf_ref[here, cols[0]], cosine, sine).astype(BF16)
            k = turn(uf_ref[here, cols[1]], cosine, sine).astype(BF16)
            v = uf_ref[here, cols[2]].astype(BF16)
            qk_ref[here, cols[0]] = q
            qk_ref[here, cols[1]] = k
            qk_ref[here, cols[2]] = v
            probs = softmax(q, k, allowed).astype(BF16)
            cx_ref[here, i * LANES : (i + 1) * LANES] = dot(probs, v).astype(BF16)

    dense_arrive()

    def dense_partial(first, count):
        def body(m, n):
            here = pl.ds(pl.multiple_of(first, half_rows) + m * 512, 512)
            cols = span(n * 512, 512)
            pb_ref[here, cols] = dot(cx_ref[here, :], wd_ref[:, cols]).astype(BF16)

        blocks(count // 512, width // 512, body)

    scatter(dense_partial, lambda: i_w.z_arrive(0))

    def row_loop(body):
        @pl.loop(0, rows // 16)
        def _(i):
            body(span(i * 16, 16), span(me * rows + i * 16, 16))

    def normalize(value):
        centered = value - jnp.mean(value, axis=1, keepdims=True)
        rstd = lax.rsqrt(jnp.mean(centered * centered, axis=1, keepdims=True) + EPSILON)
        return centered * rstd, rstd

    def first_norm(here, there):
        value = (
            alpha * xg_ref[there, 0:width].astype(F32) + sum_ref[here, :] + bt_ref[3:4, :]
        )
        unit, rstd = normalize(value)
        xh_ref[here, :] = unit
        rstd_ref[here, :] = jnp.broadcast_to(rstd, (16, LANES))
        hg_ref[there, :] = (unit * bt_ref[7:8, :] + bt_ref[4:5, :]).astype(BF16)

    row_loop(first_norm)
    normed = Gather(hg_ref)
    normed.start()
    normed.relay()
    normed.finish()
    i_w.z_arrive(1)
    o_w.tp_arrive(0)
    o_w.tp_arrive(1)
    i_w.y_arrive()

    def units(m, n):
        here = span(m * 512, 512)
        gate_cols = span(n * 256, 256)
        up_cols = span(uc + n * 256, 256)
        left = hg_ref[here, :]
        gate = dot(left, wi_ref[:, gate_cols])
        up = dot(left, wi_ref[:, up_cols])
        cdf = 0.5 * (1.0 + lax.erf(gate * (0.5**0.5)))
        density = jnp.exp(-0.5 * gate * gate) * (1.0 / math.sqrt(2.0 * math.pi))
        act = gate * cdf
        mb_ref[here, gate_cols] = (act * up).astype(BF16)
        uf_ref[here, gate_cols] = (cdf + gate * density) * up
        uf_ref[here, up_cols] = act

    blocks(all_rows // 512, uc // 256, units)
    o_w.z_arrive(0)
    o_w.z_arrive(1)
    o_w.y_arrive()
    scatter(onto_partial(mb_ref, wo_ref, uc))

    def add_row(row, value):
        sg_ref[row : row + 1, :] += jnp.sum(value, axis=0, keepdims=True)

    def norm_back(grad, gain, unit, rstd):
        scaled = grad * gain
        return rstd * (
            scaled
            - jnp.mean(scaled, axis=1, keepdims=True)
            - unit * jnp.mean(scaled * unit, axis=1, keepdims=True)
        )

    def second_norm(here, there):
        normed_one = xh_ref[here, :] * bt_ref[7:8, :] + bt_ref[4:5, :]
        unit, rstd = normalize(alpha * normed_one + sum_ref[here, :] + bt_ref[5:6, :])
        out_ref[here, :] = (unit * bt_ref[8:9, :] + bt_ref[6:7, :]).astype(BF16)
        grad = cot_ref[here, :].astype(F32)
        back = norm_back(grad, bt_ref[8:9, :], unit, rstd)
        low = back.astype(BF16)
        dr_ref[here, :] = back
        dg_ref[there, :] = low
        add_row(5, low.astype(F32))
        add_row(6, grad)
        add_row(8, grad * unit)

    row_loop(second_norm)
    branch = Gather(dg_ref)
    branch.start()
    branch.relay()
    branch.finish()

    def units_back(m, n):
        here = span(m * 512, 512)
        gate_cols, up_cols = span(n * 256, 256), span(uc + n * 256, 256)
        grad = dot(dg_ref[here, :], wo_ref[:, gate_cols])
        du_ref[here, gate_cols] = (uf_ref[here, gate_cols] * grad).astype(BF16)
        du_ref[here, up_cols] = (uf_ref[here, up_cols] * grad).astype(BF16)

    blocks(all_rows // 512, uc // 256, units_back)

    def weight_grad(left, right, target, cols, bn):
        def body(m, n):
            here, there = span(m * 512, 512), span(n * bn, bn)
            target[here, there] = dot(left[:, here], right[:, there], TN).astype(BF16)

        blocks(width // 512, cols // bn, body)

    sent(o_w.copies)
    weight_grad(dg_ref, mb_ref, wo_ref, uc, uc)
    o_w.gy_send(0)
    o_w.gy_send(1)

    def in_grad():
        sent(i_w.copies)
        weight_grad(hg_ref, du_ref, wi_ref, 2 * uc, uc)
        i_w.gy_send(0)
        i_w.gy_send(1)

    sent(branch.copies)
    scatter(onto_partial(du_ref, wi_ref, 2 * uc), in_grad)

    def first_norm_back(here, there):
        grad = alpha * dr_ref[here, :] + sum_ref[here, :]
        unit = xh_ref[here, :]
        back = norm_back(grad, bt_ref[7:8, :], unit, rstd_ref[here, 0:1])
        low = back.astype(BF16)
        dr_ref[here, :] = back
        dg_ref[there, :] = low
        add_row(3, low.astype(F32))
        add_row(4, grad)
        add_row(7, grad * unit)

    row_loop(first_norm_back)
    attended = Gather(dg_ref)
    attended.start()
    o_w.gy_add(0)
    attended.relay()
    attended.finish()

    def context_back(m, n):
        here = span(m * 512, 512)
        dc_ref[here, :] = dot(dg_ref[here, :], wd_ref[...], NT).astype(BF16)

    blocks(all_rows // 512, 1, context_back)

    def dense_grad(m, n):
        cols = span(n * 512, 512)
        wd_ref[:, cols] = dot(cx_ref[...], dg_ref[:, cols], TN).astype(BF16)

    dense_out(False)
    blocks(1, width // 512, dense_grad)
    dense_grad_out(True)
    o_w.gy_add(1)

    @pl.loop(0, GROUP)
    def _(s):
        here, allowed, cosine, sine = sequence(s)
        for i, number in enumerate(heads):
            cols = [pl.ds(t * sw + i * LANES, LANES) for t in range(3)]
            q, k, v = (qk_ref[here, one] for one in cols)
            grad = dc_ref[here, i * LANES : (i + 1) * LANES]
            probs = softmax(q, k, allowed)
            d_probs = dot(grad, v, NT)
            d_value = dot(probs.astype(BF16), grad, TN)
            d_scores = probs * (d_probs - jnp.sum(probs * d_probs, axis=1, keepdims=True))
            low = jnp.where(allowed, d_scores, 0.0).astype(BF16)
            d_query = turn(scale * dot(low, k), cosine, -sine)
            d_key = turn(scale * dot(low, q, TN), cosine, -sine)
            for t, value in enumerate((d_query, d_key, d_value)):
                value = value.astype(BF16)
                mb_ref[here, cols[t]] = value
                lanes = span(number * LANES, LANES)
                sg_ref[t : t + 1, lanes] += jnp.sum(value.astype(F32), axis=0, keepdims=True)

    o_w.gz_add(0)
    o_w.gz_add(1)
    i_w.gy_add(0)

    def qkv_grad():
        sent(q_w.copies)
        weight_grad(xg_ref, mb_ref, wq_ref, qc, qc)

        @pl.loop(0, width // LANES)
        def _(k):
            here = span(k * LANES, LANES)
            wq_ref[here, qc : qc + LANES] = sg_ref[:, here].T.astype(BF16)

        q_w.gy_send(0)
        q_w.gy_send(1)

    scatter(onto_partial(mb_ref, wq_ref, qc), qkv_grad)

    def tokens_back(here, there):
        gx_ref[here, :] = alpha * dr_ref[here, :] + sum_ref[here, :]

    row_loop(tokens_back)

    i_w.gz_add(0)
    i_w.gy_add(1)
    i_w.gz_add(1)
    q_w.gy_add(0)
    q_w.gy_add(1)
    q_w.gz_add(0)
    q_w.gz_add(1)
    for weight in (o_w, i_w, q_w):
        weight.g_end()
    dense_grad_out(False)
    dense_grad_arrive()
    for flow in (q_w, i_w, o_w, tokens, normed, attended):
        sent(flow.copies)


def on_device(
    tokens,
    cotangent,
    lengths,
    prefix,
    qkv_weight,
    dense_weight,
    ffin_weight,
    ffout_weight,
    biases,
    norm_gains,
):
    _, rows, width = tokens.shape
    A, E = lax.axis_size("a"), lax.axis_size("e")
    R = qkv_weight.shape[0]
    head_dim = width // HEADS
    my_heads = HEADS // GROUP
    hidden = ffout_weight.shape[1]
    uc = -(-hidden // (GROUP * 256)) * 256
    padded = uc * GROUP
    sw = my_heads * head_dim
    qc = 3 * sw
    qe = qc + LANES
    docs = lengths.shape[1]

    ends = jnp.cumsum(lengths, axis=1)
    positions = jnp.arange(rows, dtype=jnp.int32)[:, None]
    index = jnp.sum((positions >= ends).astype(jnp.int32), axis=1, keepdims=True)
    member = index == jnp.arange(docs, dtype=jnp.int32)[None, :]
    start_at = jnp.sum(jnp.where(member, ends - lengths, 0), axis=1, keepdims=True)
    prefix_at = jnp.sum(jnp.where(member, prefix, 0), axis=1, keepdims=True)
    valid = positions < ends[:, -1:]
    key = jnp.where(valid, index, docs + positions)
    local_pos = jnp.where(valid, positions - start_at, 0)
    info = jnp.concatenate([key, prefix_at, local_pos], axis=1).astype(BF16)
    x_ext = jnp.concatenate(
        [tokens.reshape(rows, width), jnp.pad(info, ((0, 0), (0, LANES - 3)))], axis=1
    )
    cot = jnp.where(valid, cotangent.reshape(rows, width), 0).astype(BF16)

    inverse = np.float32(ROPE_BASE) ** (
        -np.arange(head_dim // 2, dtype=np.float32) * np.float32(2.0 / head_dim)
    )
    angles = np.arange(rows, dtype=np.float32)[:, None] * inverse.astype(np.float32)
    rest = np.concatenate([np.cos(angles), np.sin(angles)], axis=1).astype(np.float32)
    terms = []
    for _ in range(3):
        terms.append(rest.astype(BF16))
        rest = rest - terms[-1].astype(np.float32)
    table = jnp.asarray(np.concatenate(terms, axis=1))

    qkv_pieces = (
        qkv_weight.reshape(R, 3, my_heads, 2, 2, 2, head_dim)
        .transpose(4, 3, 5, 0, 1, 2, 6)
        .reshape(GROUP, R, qc)
    )
    small = jnp.concatenate([biases, norm_gains], axis=1)
    small = jnp.pad(small, ((0, 0), (0, LANES - small.shape[1])))
    qkv_pieces = jnp.concatenate(
        [qkv_pieces, jnp.broadcast_to(small, (GROUP, R, LANES))], axis=2
    )

    def unit_pieces(weight):
        wide = jnp.pad(weight, ((0, 0), (0, padded - hidden)))
        return wide.reshape(R, GROUP, uc).transpose(1, 0, 2)

    ffin_pieces = jnp.concatenate(
        [unit_pieces(ffin_weight[:, :hidden]), unit_pieces(ffin_weight[:, hidden:])], axis=2
    )
    ffout_pieces = unit_pieces(ffout_weight)

    wires = 3 * (2 * GROUP + 4 * (E - 1) + 2 * E * (A - 1) + 2 * (A - 1))
    wires += 2 * (sw // R) + 2 * A * E + 8 * 10
    group_rows = GROUP * rows
    sizes = (A, E, R, rows, width, sw, uc, (2.0 * LAYERS) ** 0.5, head_dim ** (-0.5))
    shape = jax.ShapeDtypeStruct
    anywhere, vmem = pl.BlockSpec(memory_space=pl.ANY), pl.BlockSpec(memory_space=pltpu.VMEM)
    cols = (qe, 2 * uc, uc)
    results = pl.pallas_call(
        functools.partial(layer_kernel, sizes),
        out_shape=[
            shape((rows, width), BF16),
            shape((rows, width), F32),
            shape((GROUP, R, qe), BF16),
            shape((A * E, R, width), BF16),
            shape((GROUP, R, 2 * uc), BF16),
            shape((GROUP, R, uc), BF16),
        ]
        + [shape((A - 1, 2, E * 4 * R, n), BF16) for n in cols]
        + [shape((E - 1, 2, 4 * R, n), BF16) for n in cols],
        in_specs=[anywhere, vmem, vmem] + [anywhere] * 4,
        out_specs=[vmem, vmem] + [anywhere] * 10,
        scratch_shapes=[
            pltpu.VMEM((width, qe), BF16),
            pltpu.VMEM((sw, width), BF16),
            pltpu.VMEM((width, 2 * uc), BF16),
            pltpu.VMEM((width, uc), BF16),
            pltpu.VMEM((group_rows, width + LANES), BF16),
            pltpu.VMEM((group_rows, width), BF16),
            pltpu.VMEM((group_rows, width), BF16),
            pltpu.VMEM((group_rows, 2 * uc), F32),
            pltpu.VMEM((group_rows, uc), BF16),
            pltpu.VMEM((group_rows, 2 * uc), BF16),
            pltpu.VMEM((group_rows, qc), BF16),
            pltpu.VMEM((group_rows, sw), BF16),
            pltpu.VMEM((group_rows, sw), BF16),
            pltpu.VMEM((group_rows, width), BF16),
            pltpu.VMEM((4 * rows, width), BF16),
            pltpu.VMEM((3, rows, width), BF16),
            pltpu.VMEM((rows, width), BF16),
            pltpu.VMEM((2, rows, width), BF16),
            pltpu.VMEM((rows, width), F32),
            pltpu.VMEM((rows, width), F32),
            pltpu.VMEM((rows, width), F32),
            pltpu.VMEM((rows, LANES), F32),
            pltpu.VMEM((16, width), F32),
            pltpu.VMEM((LANES, width), F32),
            pltpu.VMEM((8, qc), F32),
            pltpu.VMEM((E * 4 * R, 2 * uc), BF16),
            pltpu.SemaphoreType.DMA((5,)),
            pltpu.SemaphoreType.DMA((wires,)),
            pltpu.SemaphoreType.DMA((wires,)),
        ],
        compiler_params=pltpu.CompilerParams(
            collective_id=0, has_side_effects=True, vmem_limit_bytes=63 << 20
        ),
    )(x_ext, cot, table, qkv_pieces, dense_weight, ffin_pieces, ffout_pieces)
    result, d_tokens, qkv_grad, dense_grad, ffin_grad, ffout_grad = results[:6]

    def unit_columns(pieces):
        return pieces.transpose(1, 0, 2).reshape(R, padded)[:, :hidden].astype(F32)

    grad_qkv = (
        qkv_grad[:, :, :qc]
        .reshape(2, 2, 2, R, 3, my_heads, head_dim)
        .transpose(3, 4, 5, 1, 0, 2, 6)
        .reshape(R, 3 * width)
        .astype(F32)
    )
    small_grads = jnp.sum(qkv_grad[:, :, qc:].astype(F32), axis=0)
    return (
        result.reshape(tokens.shape),
        d_tokens.reshape(tokens.shape),
        grad_qkv,
        jnp.sum(dense_grad.astype(F32), axis=0),
        jnp.concatenate(
            [unit_columns(ffin_grad[:, :, :uc]), unit_columns(ffin_grad[:, :, uc:])], axis=1
        ),
        unit_columns(ffout_grad),
        small_grads[:, :7],
        small_grads[:, 7:9],
    )


def solution(mesh):
    dp, fsdp = mesh.shape["dp"], mesh.shape["fsdp"]
    fine = Mesh(mesh.devices.reshape(dp // 2, 2, fsdp // 4, 2, 2), AXES)
    cube, flat = P(AXES, None, None), P(AXES, None)
    return jax.shard_map(
        on_device,
        mesh=fine,
        in_specs=(cube, cube) + (flat,) * 8,
        out_specs=(cube, cube) + (flat,) * 6,
        check_vma=False,
    )
```

time: 2880 us -> 578 us (0.20)
  waiting for transfers between devices: 2410 us -> 0 us
  Pallas kernels: 0 us -> 545 us
  matrix products: 216 us -> 0 us
  local copies, waits for them, and re-layouts: 125 us -> 14.7 us
  blocking collectives: 80.9 us -> 0 us
    reduce_scatter x2 -> x0, waiting for transfers between devices: 1430 us -> none  [owner_rows(): lax.psum_scatter(term, ('dp', 'fsdp'), scatter_dimension=0, tiled=True)]
    pallas_call x0 -> x1, Pallas kernels: none -> 545 us  [on_device(): pl.pallas_call(functools.partial(layer_kernel, sizes), out_shape=[shape((...]
    all_gather x4 -> x0, waiting for transfers between devices: 493 us -> none  [the longest x1 247 us: on_device(): lax.all_gather(ffin_weight, ('dp', 'fsdp'), axis=0, tiled=True)]
    unnamed x10 -> x0, waiting for transfers between devices: 482 us -> none
    dot_general x18 -> x0, matrix products: 216 us -> none  [the longest x4 83.5 us: contract_rows(): lax.dot_general(left_rows, right_rows, (((0,), (0,)), ((), ())), preferre...]
    all_gather x2 -> x0, blocking collectives: 80.9 us -> none  [the longest x1 43.2 us: on_device(): lax.all_gather(norm_gains, ('dp', 'fsdp'), axis=0, tiled=True)]
    unnamed x81 -> x26, local copies, waits for them, and re-layouts: 74.6 us -> 6.12 us
    concatenate x3 -> x1, local copies, waits for them, and re-layouts: 41.9 us -> 0.13 us  [on_device(): info = jnp.concatenate([key, prefix_at, local_pos], axis=1).astype(BF16)]
  transfers between devices with their start and end apart: 8 -> 0, of which waited for: 8 -> 0; matrix products, arithmetic and copies ran while one was open for 7% -> 0% of each run, Pallas kernels for 0% -> 0%
where the time goes in v2:
time: 578 us; the launch traced here: 577 us
  Pallas kernels  545 us (94%)
  other arithmetic  17.1 us (3%)
  local copies, waits for them, and re-layouts  14.7 us (3%)
    pallas_call x1, Pallas kernels, on_device(): pl.pallas_call(functools.partial(layer_kernel, sizes), out_shape=[shape((...  545 us

profile of v2, /device:TPU:0, one launch (start us, length us, event | category | flops | bytes accessed | tf_op | source)
XLA Modules:
  0.0 577.2 jit_solution(6961241242734032584)
XLA Ops:
  0.6 0.0 copy-start
  0.6 0.9 reduce_window_sum.11
  1.6 0.6 slice.37
  2.2 0.1 convert_reduce_fusion.2
  2.2 0.6 iota_compare_fusion.3
  2.9 0.7 subtract_bitcast_fusion
  3.6 0.7 select_reduce_fusion.1
  4.3 0.7 fusion.2
  5.0 0.7 pad_maximum_fusion.2
  5.7 0.1 copy.61
  5.8 0.1 copy.49
  6.0 1.9 bitcast_select_fusion.cot_ref
  7.9 1.9 fusion.1.x_ref
  9.8 0.0 copy-done
  9.8 0.0 copy-start.5
  9.8 0.3 slice.39
  10.1 0.1 pad.21
  10.1 0.8 copy-done.5
  11.0 0.6 reshape.104
  11.5 0.6 copy.73
  12.1 0.0 copy-start.7
  12.1 0.4 reshape.105
  12.5 1.0 pad_maximum_fusion.1.qp_ref
  13.6 0.0 copy-done.7
  13.6 0.0 copy-start.1
  13.6 0.0 copy-start.9
  13.6 0.1 pad.22
  13.6 0.9 copy.72
  14.6 0.6 copy-done.1
  15.2 0.0 copy-done.9
  15.2 0.1 slice_select_fusion
  15.3 0.2 bitcast_bitcast_fusion.1
  15.5 1.3 pad_maximum_fusion.ip_ref
  16.7 544.7 %shard_map.170 = (bf16[128,2048]{1,0:T(8,128)(2,1)}, f32[128,2048]{1,0:T(8,128)}, bf16[8,64,896]{2,1,0:T(8,128)(2,1)}, bf16[4,64,2048]{2,1,0:T(8,128)(2,1)}, bf1...) custom-call(bf16[128,2176]{1,0:T(8,128)(2,1)} %fusion.1.x_ref, ...), custom_call_target="tpu_custom_call" | custom-call | tf_op jit(solution)/shard_map/pallas_call | solution.py:897
  561.4 0.0 copy-start.4
  561.4 1.0 convert_reduce_fusion.1
  562.4 0.7 copy.59
  563.1 0.1 slice.53
  563.2 0.6 copy.60
  563.8 2.2 convert_reduce_fusion
  566.1 0.0 copy-done.4
  566.1 0.1 slice_convert_fusion
  566.2 0.8 reshape.115
  567.0 1.2 copy.55
  568.2 0.0 copy-start.6
  568.3 2.4 reshape.114
  570.7 0.0 copy-done.6
  570.7 0.0 copy-start.2
  570.7 0.1 copy.67
  570.7 1.2 slice_convert_fusion.1
  571.9 0.7 copy-done.2
  572.6 0.2 slice_bitcast_fusion.1
  572.7 0.1 copy.65
  572.9 0.1 copy.66
  573.0 0.0 copy-start.8
  573.0 1.9 maximum_convert_fusion
  574.9 0.0 copy-done.8
  574.9 0.0 copy-start.3
  574.9 0.8 copy.76
  575.7 0.6 copy-done.3
  576.3 1.0 copy.77
  (6 shorter events, 0.1 us)
Async XLA Ops:
  0.6 9.2 %copy-start = (bf16[64,10922]{1,0:T(8,128)(2,1)S(1)}, bf16[64,10922]{1,0:T(8,128)(2,1)}, u32[]{:S(2)}) copy-start(bf16[64,10922]{1,0:T(8,128)(2,1)} %param.17) | copy-start | bytes 4194052
  9.8 1.1 copy-start.5
  12.1 1.4 copy-start.7
  13.6 1.6 copy-start.1
  13.6 1.6 copy-start.9
  561.4 4.6 copy-start.4
  568.2 2.4 copy-start.6
  570.7 1.9 copy-start.2
  573.0 1.9 copy-start.8
  574.9 1.4 copy-start.3

commit v3 on v2

--- a/solution.py
+++ b/solution.py
@@ -70,26 +70,34 @@
     x_ref,
     cot_ref,
     table_ref,
+    sp_ref,
     qp_ref,
     dp_ref,
     ip_ref,
     op_ref,
     out_ref,
     gx_ref,
+    os_ref,
     oq_ref,
     od_ref,
     oi_ref,
     oo_ref,
+    ys_ref,
     yq_ref,
+    yd_ref,
     yi_ref,
     yo_ref,
+    zs_ref,
     zq_ref,
+    zd_ref,
     zi_ref,
     zo_ref,
+    ws_ref,
     wq_ref,
     wd_ref,
     wi_ref,
     wo_ref,
+    go_ref,
     xg_ref,
     hg_ref,
     dg_ref,
@@ -112,6 +120,7 @@
     sg_ref,
     qb_ref,
     tm_ref,
+    td_ref,
     local_sem,
     send_sem,
     recv_sem,
@@ -126,9 +135,6 @@
     my_rows = span(me * rows, rows)
     flip = lambda v, d: lax.rem(v + d, 2)
     rank = lambda aa, bb, ee, ff, cc: (((aa * 2 + bb) * E + ee) * 2 + ff) * 2 + cc
-    line = lambda aa, bb, ee, ff, cc: span(rank(aa, bb, ee, ff, cc) * R, R)
-    block = lambda aa, bb, ee: span(((aa * 2 + bb) * E + ee) * 4 * R, 4 * R)
-    half = lambda aa, bb: span((aa * 2 + bb) * E * 4 * R, E * 4 * R)
     wires = Wires(send_sem, recv_sem)
     peers = [(r // 4, r // 2 % 2, r % 2) for r in range(GROUP)]
 
@@ -157,6 +163,7 @@
         def __init__(self, index, pieces, buf, out, ylanding, zlanding):
             self.index, self.pieces, self.buf, self.out = index, pieces, buf, out
             self.ylanding, self.zlanding = ylanding, zlanding
+            self.R = pieces.shape[1]
             self.copies = []
             self.tp, self.z, self.y = (
                 wires.take(GROUP),
@@ -172,9 +179,18 @@
         def send(self, *copy):
             self.copies.append(wires.send(*copy))
 
+        def line(self, aa, bb, ee, ff, cc):
+            return span(rank(aa, bb, ee, ff, cc) * self.R, self.R)
+
+        def block(self, aa, bb, ee):
+            return span(((aa * 2 + bb) * E + ee) * 4 * self.R, 4 * self.R)
+
+        def half(self, aa, bb):
+            return span((aa * 2 + bb) * E * 4 * self.R, E * 4 * self.R)
+
         def own(self):
             return pltpu.make_async_copy(
-                self.pieces.at[me], self.buf.at[line(a, b, e, f, c)], local_sem.at[self.index]
+                self.pieces.at[me], self.buf.at[self.line(a, b, e, f, c)], local_sem.at[self.index]
             )
 
         def tp_send(self):
@@ -185,28 +201,29 @@
                 self.send(
                     self.tp + r,
                     self.pieces.at[slot(bb, ff, cc)],
-                    self.buf.at[line(a, b, e, f, c)],
+                    self.buf.at[self.line(a, b, e, f, c)],
                     {"b": bb, "f": ff, "c": cc},
                 )
 
-        def tp_arrive(self, db):
+        def tp_wait(self, db):
             for r in range(4 * db, 4 * db + 4):
                 if r == 0:
                     self.own().wait()
                 else:
                     _, df, dc = peers[r]
                     wires.arrived(
-                        self.tp + r, self.buf.at[line(a, flip(b, db), e, flip(f, df), flip(c, dc))]
+                        self.tp + r, self.buf.at[self.line(a, flip(b, db), e, flip(f, df), flip(c, dc))]
                     )
+
+        def z_send(self, db):
+            rows_ = self.buf.at[self.block(a, flip(b, db), e)]
             for s in range(1, E):
-                rows_ = self.buf.at[block(a, flip(b, db), e)]
                 self.send(
                     self.z + db * (E - 1) + s - 1, rows_, rows_, {"e": lax.rem(e + s, E)}
                 )
-            self.y_send(db, 0)
 
         def y_send(self, db, s):
-            rows_ = self.buf.at[block(a, flip(b, db), lax.rem(e + E - s, E))]
+            rows_ = self.buf.at[self.block(a, flip(b, db), lax.rem(e + E - s, E))]
             for t in range(1, A):
                 self.send(
                     self.y + (db * E + s) * (A - 1) + t - 1, rows_, rows_, {"a": lax.rem(a + t, A)}
@@ -216,7 +233,7 @@
             for s in range(1, E):
                 wires.arrived(
                     self.z + db * (E - 1) + s - 1,
-                    self.buf.at[block(a, flip(b, db), lax.rem(e + E - s, E))],
+                    self.buf.at[self.block(a, flip(b, db), lax.rem(e + E - s, E))],
                 )
                 self.y_send(db, s)
 
@@ -227,14 +244,14 @@
                         wires.arrived(
                             self.y + (db * E + s) * (A - 1) + t - 1,
                             self.buf.at[
-                                block(lax.rem(a + A - t, A), flip(b, db), lax.rem(e + E - s, E))
+                                self.block(lax.rem(a + A - t, A), flip(b, db), lax.rem(e + E - s, E))
                             ],
                         )
 
         def add(self, landing, base, count):
             cols = self.buf.shape[1]
             temp = tm_ref.at[pl.ds(0, count), pl.ds(0, cols)]
-            load = pltpu.make_async_copy(landing, temp, local_sem.at[3])
+            load = pltpu.make_async_copy(landing, temp, local_sem.at[4])
             load.start()
             load.wait()
 
@@ -252,7 +269,7 @@
                 to = lax.rem(a + t, A)
                 self.send(
                     self.gy + db * (A - 1) + t - 1,
-                    self.buf.at[half(to, bb)],
+                    self.buf.at[self.half(to, bb)],
                     self.ylanding.at[t - 1, db],
                     {"a": to},
                 )
@@ -262,12 +279,12 @@
             for t in range(1, A):
                 landing = self.ylanding.at[t - 1, db]
                 wires.arrived(self.gy + db * (A - 1) + t - 1, landing)
-                self.add(landing, (a * 2 + bb) * E * 4 * R, E * 4 * R)
+                self.add(landing, (a * 2 + bb) * E * 4 * self.R, E * 4 * self.R)
             for s in range(1, E):
                 to = lax.rem(e + s, E)
                 self.send(
                     self.gz + db * (E - 1) + s - 1,
-                    self.buf.at[block(a, bb, to)],
+                    self.buf.at[self.block(a, bb, to)],
                     self.zlanding.at[s - 1, db],
                     {"e": to},
                 )
@@ -277,11 +294,11 @@
             for s in range(1, E):
                 landing = self.zlanding.at[s - 1, db]
                 wires.arrived(self.gz + db * (E - 1) + s - 1, landing)
-                self.add(landing, ((a * 2 + bb) * E + e) * 4 * R, 4 * R)
+                self.add(landing, ((a * 2 + bb) * E + e) * 4 * self.R, 4 * self.R)
             for r in range(4 * db, 4 * db + 4):
                 _, df, dc = peers[r]
                 ff, cc = flip(f, df), flip(c, dc)
-                rows_ = self.buf.at[line(a, bb, e, ff, cc)]
+                rows_ = self.buf.at[self.line(a, bb, e, ff, cc)]
                 if r == 0:
                     pltpu.make_async_copy(rows_, self.out.at[me], local_sem.at[self.index]).start()
                 else:
@@ -294,7 +311,7 @@
                 db, df, dc = peers[r]
                 if r == 0:
                     pltpu.make_async_copy(
-                        self.buf.at[line(a, b, e, f, c)],
+                        self.buf.at[self.line(a, b, e, f, c)],
                         self.out.at[me],
                         local_sem.at[self.index],
                     ).wait()
@@ -303,34 +320,10 @@
                         self.gtp + r, self.out.at[slot(flip(b, db), flip(f, df), flip(c, dc))]
                     )
 
+    s_w = Weight(3, sp_ref, ws_ref, os_ref, ys_ref, zs_ref)
     q_w = Weight(0, qp_ref, wq_ref, oq_ref, yq_ref, zq_ref)
     i_w = Weight(1, ip_ref, wi_ref, oi_ref, yi_ref, zi_ref)
     o_w = Weight(2, op_ref, wo_ref, oo_ref, yo_ref, zo_ref)
-
-    dense_pieces = wd_ref.shape[0] // R
-    dense_first = wires.take(dense_pieces)
-    dense_sends = wires.take(A * E)
-    dense_back = wires.take(A * E)
-    dense_back_sends = wires.take(dense_pieces)
-    first_row = rank(a, b, e, f, c) * R
-    head = first_row // LANES
-
-    def dense_route(aa, ee):
-        piece = (head // 8) * (LANES // R) + lax.rem(first_row, LANES) // R
-        target = {
-            "a": aa,
-            "b": lax.rem(head // 4, 2),
-            "e": ee,
-            "f": lax.rem(head, 2),
-            "c": lax.rem(head // 2, 2),
-        }
-        return piece, target
-
-    def is_me(target):
-        same = target["a"] == a
-        for axis, mine in (("b", b), ("e", e), ("f", f), ("c", c)):
-            same = same & (target[axis] == mine)
-        return same
 
     def remote(source, landing, send, recv, target):
         return pltpu.make_async_remote_copy(
@@ -342,73 +335,201 @@
             device_id_type=DEVICE_MESH,
         )
 
-    def dense_out(start):
-        for da in range(A):
-            for de in range(E):
-                piece, target = dense_route(lax.rem(a + da, A), lax.rem(e + de, E))
-                landing = wd_ref.at[span(piece * R, R)]
-                away = remote(
-                    dp_ref, landing, dense_sends + da * E + de, dense_first + piece, target
+    class Dense:
+        def __init__(self):
+            self.pieces = wd_ref.shape[0] // R
+            self.first = wires.take(self.pieces)
+            self.push = wires.take(1)
+            self.zs = wires.take(self.pieces * (E - 1))
+            self.ys = wires.take(self.pieces * (A - 1))
+            self.gy = wires.take(self.pieces * (A - 1))
+            self.gz = wires.take(self.pieces * (E - 1))
+            self.back = wires.take(1)
+            self.back_sends = wires.take(self.pieces)
+            self.owners = []
+            for piece in range(self.pieces):
+                i, offset = piece * R // LANES, piece * R % LANES
+                owner = ((i * 8 + b * 4 + c * 2 + f) * LANES + offset) // R
+                self.owners.append(
+                    {
+                        "a": owner // (8 * E),
+                        "b": lax.rem(owner // (4 * E), 2),
+                        "e": lax.rem(owner // 4, E),
+                        "f": lax.rem(owner // 2, 2),
+                        "c": lax.rem(owner, 2),
+                    }
                 )
-                if da + de:
-                    away.start() if start else away.wait_send()
-                else:
-                    here = is_me(target)
-
-                    @pl.when(here)
-                    def _():
-                        if start:
-                            pltpu.make_async_copy(
-                                dp_ref, landing, recv_sem.at[dense_first + piece]
-                            ).start()
-
-                    @pl.when(jnp.logical_not(here))
-                    def _():
-                        away.start() if start else away.wait_send()
-
-    def dense_arrive():
-        for piece in range(dense_pieces):
-            wires.arrived(dense_first + piece, wd_ref.at[pl.ds(piece * R, R)])
-
-    def dense_grad_out(start):
-        for piece in range(dense_pieces):
-            i, offset = piece * R // LANES, piece * R % LANES
-            owner = ((i * 8 + b * 4 + c * 2 + f) * LANES + offset) // R
-            target = {
-                "a": owner // (8 * E),
-                "b": lax.rem(owner // (4 * E), 2),
-                "e": lax.rem(owner // 4, E),
-                "f": lax.rem(owner // 2, 2),
-                "c": lax.rem(owner, 2),
-            }
-            from_ = a * E + e
-            source = wd_ref.at[pl.ds(piece * R, R)]
-            away = remote(
-                source, od_ref.at[from_], dense_back_sends + piece, dense_back + from_, target
-            )
-            here = is_me(target)
+
+        def rows(self, piece):
+            return wd_ref.at[pl.ds(piece * R, R)]
+
+        def each(self, test, body):
+            for piece, owner in enumerate(self.owners):
+                same_a, same_e = owner["a"] == a, owner["e"] == e
+
+                @pl.when(test(same_a, same_e))
+                def _():
+                    body(piece, owner)
+
+        def local_or_remote(self, target, source, landing, send, recv, start):
+            here = target["b"] == b
+            for axis, mine in (("f", f), ("c", c)):
+                here = here & (target[axis] == mine)
+            away = remote(source, landing, send, recv, target)
 
             @pl.when(here)
             def _():
                 if start:
-                    pltpu.make_async_copy(
-                        source, od_ref.at[from_], recv_sem.at[dense_back + from_]
-                    ).start()
+                    pltpu.make_async_copy(source, landing, recv_sem.at[recv]).start()
 
             @pl.when(jnp.logical_not(here))
             def _():
                 away.start() if start else away.wait_send()
 
-    def dense_grad_arrive():
-        for k in range(A * E):
-            wires.arrived(dense_back + k, od_ref.at[k])
+        def out(self, start):
+            first_row = rank(a, b, e, f, c) * R
+            head = first_row // LANES
+            piece = (head // 8) * (LANES // R) + lax.rem(first_row, LANES) // R
+            target = {
+                "b": lax.rem(head // 4, 2),
+                "f": lax.rem(head, 2),
+                "c": lax.rem(head // 2, 2),
+            }
+            landing = wd_ref.at[span(piece * R, R)]
+            self.local_or_remote(target, dp_ref, landing, self.push, self.first + piece, start)
+
+        def z(self, piece, s):
+            rows_ = self.rows(piece)
+            number = self.zs + piece * (E - 1) + s - 1
+            return remote(rows_, rows_, number, self.first + piece, {"e": lax.rem(e + s, E)})
+
+        def y(self, piece, t):
+            rows_ = self.rows(piece)
+            number = self.ys + piece * (A - 1) + t - 1
+            return remote(rows_, rows_, number, self.first + piece, {"a": lax.rem(a + t, A)})
+
+        def arrived(self, piece, _=None):
+            wires.arrived(self.first + piece, self.rows(piece))
+
+        def z_send(self):
+            def body(piece, owner):
+                self.arrived(piece)
+                for s in range(1, E):
+                    self.z(piece, s).start()
+
+            self.each(lambda same_a, same_e: same_a & same_e, body)
+
+        def y_send(self):
+            self.each(lambda same_a, same_e: same_a & jnp.logical_not(same_e), self.arrived)
+
+            def body(piece, owner):
+                for t in range(1, A):
+                    self.y(piece, t).start()
+
+            self.each(lambda same_a, same_e: same_a, body)
+
+        def y_arrive(self):
+            self.each(lambda same_a, same_e: jnp.logical_not(same_a), self.arrived)
+
+        def sent(self):
+            self.out(False)
+
+            def over_z(piece, owner):
+                for s in range(1, E):
+                    self.z(piece, s).wait_send()
+
+            def over_y(piece, owner):
+                for t in range(1, A):
+                    self.y(piece, t).wait_send()
+
+            self.each(lambda same_a, same_e: same_a & same_e, over_z)
+            self.each(lambda same_a, same_e: same_a, over_y)
+
+        def g_y(self, piece, t):
+            to = lax.rem(a + t, A)
+            number = self.gy + piece * (A - 1) + t - 1
+            copy = remote(self.rows(piece), yd_ref.at[t - 1, piece], number, number, {"a": to})
+            return to, copy
+
+        def gy_send(self, start=True):
+            for piece, owner in enumerate(self.owners):
+                for t in range(1, A):
+                    to, copy = self.g_y(piece, t)
+
+                    @pl.when(owner["a"] == to)
+                    def _():
+                        copy.start() if start else copy.wait_send()
+
+        def add(self, landing, piece):
+            load = pltpu.make_async_copy(landing, td_ref, local_sem.at[4])
+            load.start()
+            load.wait()
+
+            @pl.loop(0, R // 16)
+            def _(i):
+                here, there = span(piece * R + i * 16, 16), span(i * 16, 16)
+                wd_ref[here, :] = (
+                    wd_ref[here, :].astype(F32) + td_ref[there, :].astype(F32)
+                ).astype(BF16)
+
+        def g_z(self, piece, s):
+            to = lax.rem(e + s, E)
+            number = self.gz + piece * (E - 1) + s - 1
+            copy = remote(self.rows(piece), zd_ref.at[s - 1, piece], number, number, {"e": to})
+            return to, copy
+
+        def gz_send(self, start=True):
+            for piece, owner in enumerate(self.owners):
+                for s in range(1, E):
+                    to, copy = self.g_z(piece, s)
+
+                    @pl.when((owner["a"] == a) & (owner["e"] == to))
+                    def _():
+                        copy.start() if start else copy.wait_send()
+
+        def gy_add(self):
+            def body(piece, owner):
+                for t in range(1, A):
+                    landing = yd_ref.at[t - 1, piece]
+                    wires.arrived(self.gy + piece * (A - 1) + t - 1, landing)
+                    self.add(landing, piece)
+
+            self.each(lambda same_a, same_e: same_a, body)
+            self.gz_send()
+
+        def home(self, piece, owner, start):
+            target = {axis: owner[axis] for axis in ("b", "f", "c")}
+            self.local_or_remote(
+                target, self.rows(piece), od_ref, self.back_sends + piece, self.back, start
+            )
+
+        def gz_add(self):
+            def body(piece, owner):
+                for s in range(1, E):
+                    landing = zd_ref.at[s - 1, piece]
+                    wires.arrived(self.gz + piece * (E - 1) + s - 1, landing)
+                    self.add(landing, piece)
+                self.home(piece, owner, True)
+
+            self.each(lambda same_a, same_e: same_a & same_e, body)
+
+        def g_end(self):
+            wires.arrived(self.back, od_ref)
+            self.gy_send(False)
+            self.gz_send(False)
+            self.each(
+                lambda same_a, same_e: same_a & same_e,
+                lambda piece, owner: self.home(piece, owner, False),
+            )
+
+    dense = Dense()
 
     to_b, to_f, to_c = {"b": 1 - b}, {"f": 1 - f}, {"c": 1 - c}
     nb, nf, dg = slot(1 - b, f, c), slot(b, 1 - f, c), slot(1 - b, 1 - f, c)
 
     class Gather:
-        def __init__(self, buf):
-            self.buf, self.first, self.copies = buf, wires.take(10), []
+        def __init__(self, buf, lean):
+            self.buf, self.first, self.copies, self.lean = buf, wires.take(10), [], lean
 
         def part(self, place, which):
             if which is None:
@@ -430,6 +551,16 @@
             self.copy(4, me, None, to_c)
 
         def relay(self):
+            if self.lean:
+                self.landed(1, nf, 1)
+                self.copy(6, nf, 1, to_b)
+                self.landed(3, nf, 0)
+                self.copy(5, nf, 0, to_b)
+                self.copy(8, nf, None, to_c)
+                self.landed(0, nb, 0)
+                self.landed(2, nb, 1)
+                self.copy(7, nb, None, to_c)
+                return
             self.landed(0, nb, 0)
             self.copy(5, nb, 0, to_f)
             self.landed(1, nf, 1)
@@ -461,7 +592,7 @@
                 total = total + term[window, :].astype(F32)
             target[window, :] = total.astype(target.dtype)
 
-    def scatter(multiply, meanwhile=None):
+    def scatter(multiply, lean, early=None, late=None):
         first, copies = wires.take(10), []
 
         def send(*copy):
@@ -480,29 +611,45 @@
         core = [core_ref.at[pl.ds(k * rows, rows)] for k in range(4)]
         mid = rows // 2
         low, high = pl.ds(0, mid), pl.ds(mid, mid)
-        if meanwhile is not None:
-            meanwhile()
+        early, late = (hook or (lambda: None) for hook in (early, late))
         wires.arrived(first, core[0])
         accumulate(stage_ref.at[0], 0, rows, [own[0], core[0]])
-        send(first + 4, stage_ref.at[0, low], relay_ref.at[low], to_b)
-        send(first + 5, stage_ref.at[0, high], relay_ref.at[high], to_f)
-        wires.arrived(first + 1, core[1])
-        accumulate(stage_ref.at[1], 0, mid, [own[1], core[1]])
-        send(first + 6, stage_ref.at[1, low], land_ref.at[0, low], to_b)
-        wires.arrived(first + 2, core[2])
-        accumulate(stage_ref.at[2], mid, mid, [own[2], core[2]])
-        send(first + 7, stage_ref.at[2, high], land_ref.at[1, high], to_f)
-        wires.arrived(first + 5, relay_ref.at[high])
-        accumulate(stage_ref.at[1], mid, mid, [own[1], core[1], relay_ref])
-        send(first + 8, stage_ref.at[1, high], land_ref.at[0, high], to_b)
-        wires.arrived(first + 4, relay_ref.at[low])
-        accumulate(stage_ref.at[2], 0, mid, [own[2], core[2], relay_ref])
-        send(first + 9, stage_ref.at[2, low], land_ref.at[1, low], to_f)
-        wires.arrived(first + 3, core[3])
-        wires.arrived(first + 6, land_ref.at[0, low])
-        wires.arrived(first + 7, land_ref.at[1, high])
-        wires.arrived(first + 8, land_ref.at[0, high])
-        wires.arrived(first + 9, land_ref.at[1, low])
+        if lean:
+            send(first + 4, stage_ref.at[0], relay_ref, to_b)
+            wires.arrived(first + 1, core[1])
+            accumulate(stage_ref.at[1], 0, rows, [own[1], core[1]])
+            send(first + 6, stage_ref.at[1], land_ref.at[0], to_b)
+            early()
+            wires.arrived(first + 2, core[2])
+            wires.arrived(first + 4, relay_ref)
+            accumulate(stage_ref.at[2], 0, rows, [own[2], core[2], relay_ref])
+            send(first + 7, stage_ref.at[2], land_ref.at[1], to_f)
+            late()
+            wires.arrived(first + 3, core[3])
+            wires.arrived(first + 6, land_ref.at[0])
+            wires.arrived(first + 7, land_ref.at[1])
+        else:
+            send(first + 4, stage_ref.at[0, low], relay_ref.at[low], to_b)
+            send(first + 5, stage_ref.at[0, high], relay_ref.at[high], to_f)
+            wires.arrived(first + 1, core[1])
+            accumulate(stage_ref.at[1], 0, mid, [own[1], core[1]])
+            send(first + 6, stage_ref.at[1, low], land_ref.at[0, low], to_b)
+            wires.arrived(first + 2, core[2])
+            accumulate(stage_ref.at[2], mid, mid, [own[2], core[2]])
+            send(first + 7, stage_ref.at[2, high], land_ref.at[1, high], to_f)
+            early()
+            wires.arrived(first + 5, relay_ref.at[high])
+            accumulate(stage_ref.at[1], mid, mid, [own[1], core[1], relay_ref])
+            send(first + 8, stage_ref.at[1, high], land_ref.at[0, high], to_b)
+            wires.arrived(first + 4, relay_ref.at[low])
+            accumulate(stage_ref.at[2], 0, mid, [own[2], core[2], relay_ref])
+            send(first + 9, stage_ref.at[2, low], land_ref.at[1, low], to_f)
+            late()
+            wires.arrived(first + 3, core[3])
+            wires.arrived(first + 6, land_ref.at[0, low])
+            wires.arrived(first + 7, land_ref.at[1, high])
+            wires.arrived(first + 8, land_ref.at[0, high])
+            wires.arrived(first + 9, land_ref.at[1, low])
         accumulate(sum_ref, 0, rows, [own[3], core[3], land_ref.at[0], land_ref.at[1]])
         sent(copies)
 
@@ -524,30 +671,51 @@
         return multiply
 
     q_w.tp_send()
-    own_x = pltpu.make_async_copy(x_ref, xg_ref.at[my_rows], local_sem.at[4])
+    s_w.tp_send()
+    dense.out(True)
+    own_x = pltpu.make_async_copy(x_ref, xg_ref.at[my_rows], local_sem.at[5])
     own_x.start()
-    dense_out(True)
     sg_ref[...] = jnp.zeros_like(sg_ref)
-    q_w.tp_arrive(0)
-    q_w.tp_arrive(1)
+    tokens = Gather(xg_ref, True)
+    for db in range(2):
+        q_w.tp_wait(db)
+        q_w.z_send(db)
+        q_w.y_send(db, 0)
     own_x.wait()
-    tokens = Gather(xg_ref)
     tokens.start()
     i_w.tp_send()
+    for db in range(2):
+        s_w.tp_wait(db)
+        s_w.z_send(db)
+        s_w.y_send(db, 0)
+    dense.z_send()
+    q_w.z_arrive(0)
     tokens.relay()
-    q_w.z_arrive(0)
+    i_w.tp_wait(0)
+    i_w.z_send(0)
+    i_w.y_send(0, 0)
+    q_w.z_arrive(1)
+    s_w.z_arrive(0)
+    s_w.z_arrive(1)
+    i_w.tp_wait(1)
+    dense.y_send()
+    i_w.y_send(1, 0)
     tokens.finish()
-    q_w.z_arrive(1)
-    i_w.tp_arrive(0)
-    i_w.tp_arrive(1)
     o_w.tp_send()
+    s_w.y_arrive()
     q_w.y_arrive()
+
+    lane = lax.broadcasted_iota(jnp.int32, (16, LANES), 1)
 
     @pl.loop(0, width // LANES)
     def _(k):
-        here = span(k * LANES, LANES)
-        turned = wq_ref[here, qc : qc + LANES].astype(F32).T
-        bt_ref[:, here] = turned[0:16, :]
+        line = jnp.zeros((16, LANES), F32)
+        for j in range(LANES // R):
+            part = ws_ref[span((k * (LANES // R) + j) * 16, 16), :].astype(F32)
+            if j:
+                part = pltpu.roll(part, j * R, axis=1)
+            line = jnp.where(lane // R == j, part, line)
+        bt_ref[:, span(k * LANES, LANES)] = line
 
     heads = [i * 8 + b * 4 + c * 2 + f for i in range(sw // LANES)]
     for t in range(3):
@@ -604,7 +772,8 @@
             probs = softmax(q, k, allowed).astype(BF16)
             cx_ref[here, i * LANES : (i + 1) * LANES] = dot(probs, v).astype(BF16)
 
-    dense_arrive()
+    i_w.z_send(1)
+    dense.y_arrive()
 
     def dense_partial(first, count):
         def body(m, n):
@@ -614,7 +783,10 @@
 
         blocks(count // 512, width // 512, body)
 
-    scatter(dense_partial, lambda: i_w.z_arrive(0))
+    scatter(dense_partial, True, lambda: i_w.z_arrive(0))
+    for db in range(2):
+        o_w.tp_wait(db)
+        o_w.z_send(db)
 
     def row_loop(body):
         @pl.loop(0, rows // 16)
@@ -636,13 +808,13 @@
         hg_ref[there, :] = (unit * bt_ref[7:8, :] + bt_ref[4:5, :]).astype(BF16)
 
     row_loop(first_norm)
-    normed = Gather(hg_ref)
+    normed = Gather(hg_ref, True)
     normed.start()
+    o_w.y_send(0, 0)
+    o_w.y_send(1, 0)
     normed.relay()
+    i_w.z_arrive(1)
     normed.finish()
-    i_w.z_arrive(1)
-    o_w.tp_arrive(0)
-    o_w.tp_arrive(1)
     i_w.y_arrive()
 
     def units(m, n):
@@ -663,7 +835,7 @@
     o_w.z_arrive(0)
     o_w.z_arrive(1)
     o_w.y_arrive()
-    scatter(onto_partial(mb_ref, wo_ref, uc))
+    scatter(onto_partial(mb_ref, wo_ref, uc), False)
 
     def add_row(row, value):
         sg_ref[row : row + 1, :] += jnp.sum(value, axis=0, keepdims=True)
@@ -690,7 +862,7 @@
         add_row(8, grad * unit)
 
     row_loop(second_norm)
-    branch = Gather(dg_ref)
+    branch = Gather(dg_ref, False)
     branch.start()
     branch.relay()
     branch.finish()
@@ -702,8 +874,6 @@
         du_ref[here, gate_cols] = (uf_ref[here, gate_cols] * grad).astype(BF16)
         du_ref[here, up_cols] = (uf_ref[here, up_cols] * grad).astype(BF16)
 
-    blocks(all_rows // 512, uc // 256, units_back)
-
     def weight_grad(left, right, target, cols, bn):
         def body(m, n):
             here, there = span(m * 512, 512), span(n * bn, bn)
@@ -712,9 +882,11 @@
         blocks(width // 512, cols // bn, body)
 
     sent(o_w.copies)
-    weight_grad(dg_ref, mb_ref, wo_ref, uc, uc)
+    weight_grad(dg_ref, mb_ref, go_ref, uc, uc)
+    o_w.buf = go_ref
     o_w.gy_send(0)
     o_w.gy_send(1)
+    blocks(all_rows // 512, uc // 256, units_back)
 
     def in_grad():
         sent(i_w.copies)
@@ -723,7 +895,7 @@
         i_w.gy_send(1)
 
     sent(branch.copies)
-    scatter(onto_partial(du_ref, wi_ref, 2 * uc), in_grad)
+    scatter(onto_partial(du_ref, wi_ref, 2 * uc), False, in_grad, lambda: o_w.gy_add(0))
 
     def first_norm_back(here, there):
         grad = alpha * dr_ref[here, :] + sum_ref[here, :]
@@ -737,9 +909,9 @@
         add_row(7, grad * unit)
 
     row_loop(first_norm_back)
-    attended = Gather(dg_ref)
+    attended = Gather(dg_ref, True)
     attended.start()
-    o_w.gy_add(0)
+    o_w.gy_add(1)
     attended.relay()
     attended.finish()
 
@@ -753,10 +925,9 @@
         cols = span(n * 512, 512)
         wd_ref[:, cols] = dot(cx_ref[...], dg_ref[:, cols], TN).astype(BF16)
 
-    dense_out(False)
+    dense.sent()
     blocks(1, width // 512, dense_grad)
-    dense_grad_out(True)
-    o_w.gy_add(1)
+    dense.gy_send()
 
     @pl.loop(0, GROUP)
     def _(s):
@@ -778,41 +949,53 @@
                 lanes = span(number * LANES, LANES)
                 sg_ref[t : t + 1, lanes] += jnp.sum(value.astype(F32), axis=0, keepdims=True)
 
-    o_w.gz_add(0)
-    o_w.gz_add(1)
     i_w.gy_add(0)
 
     def qkv_grad():
         sent(q_w.copies)
         weight_grad(xg_ref, mb_ref, wq_ref, qc, qc)
 
+        q_w.gy_send(0)
+        q_w.gy_send(1)
+        sent(s_w.copies)
+
         @pl.loop(0, width // LANES)
         def _(k):
-            here = span(k * LANES, LANES)
-            wq_ref[here, qc : qc + LANES] = sg_ref[:, here].T.astype(BF16)
-
-        q_w.gy_send(0)
-        q_w.gy_send(1)
-
-    scatter(onto_partial(mb_ref, wq_ref, qc), qkv_grad)
+            line = sg_ref[:, span(k * LANES, LANES)]
+            for j in range(LANES // R):
+                part = line if j == 0 else pltpu.roll(line, LANES - j * R, axis=1)
+                ws_ref[span((k * (LANES // R) + j) * 16, 16), :] = part.astype(BF16)
+
+        s_w.gy_send(0)
+        s_w.gy_send(1)
+
+    def late_adds():
+        i_w.gy_add(1)
+
+    scatter(onto_partial(mb_ref, wq_ref, qc), True, qkv_grad, late_adds)
 
     def tokens_back(here, there):
         gx_ref[here, :] = alpha * dr_ref[here, :] + sum_ref[here, :]
 
     row_loop(tokens_back)
 
-    i_w.gz_add(0)
-    i_w.gy_add(1)
-    i_w.gz_add(1)
+    dense.gy_add()
+    o_w.gz_add(0)
+    o_w.gz_add(1)
     q_w.gy_add(0)
     q_w.gy_add(1)
+    s_w.gy_add(0)
+    s_w.gy_add(1)
+    dense.gz_add()
+    i_w.gz_add(0)
+    i_w.gz_add(1)
     q_w.gz_add(0)
     q_w.gz_add(1)
-    for weight in (o_w, i_w, q_w):
+    s_w.gz_add(0)
+    s_w.gz_add(1)
+    for weight in (dense, o_w, i_w, q_w, s_w):
         weight.g_end()
-    dense_grad_out(False)
-    dense_grad_arrive()
-    for flow in (q_w, i_w, o_w, tokens, normed, attended):
+    for flow in (q_w, i_w, o_w, s_w, tokens, normed, attended):
         sent(flow.copies)
 
 
@@ -838,7 +1021,6 @@
     padded = uc * GROUP
     sw = my_heads * head_dim
     qc = 3 * sw
-    qe = qc + LANES
     docs = lengths.shape[1]
 
     ends = jnp.cumsum(lengths, axis=1)
@@ -872,11 +1054,9 @@
         .transpose(4, 3, 5, 0, 1, 2, 6)
         .reshape(GROUP, R, qc)
     )
-    small = jnp.concatenate([biases, norm_gains], axis=1)
-    small = jnp.pad(small, ((0, 0), (0, LANES - small.shape[1])))
-    qkv_pieces = jnp.concatenate(
-        [qkv_pieces, jnp.broadcast_to(small, (GROUP, R, LANES))], axis=2
-    )
+    small = jnp.concatenate([biases, norm_gains], axis=1).T
+    small = jnp.pad(small, ((0, 16 - small.shape[0]), (0, LANES - R)))
+    small_pieces = jnp.broadcast_to(small, (GROUP, 16, LANES))
 
     def unit_pieces(weight):
         wide = jnp.pad(weight, ((0, 0), (0, padded - hidden)))
@@ -887,31 +1067,41 @@
     )
     ffout_pieces = unit_pieces(ffout_weight)
 
-    wires = 3 * (2 * GROUP + 4 * (E - 1) + 2 * E * (A - 1) + 2 * (A - 1))
-    wires += 2 * (sw // R) + 2 * A * E + 8 * 10
+    wires = 4 * (2 * GROUP + 4 * (E - 1) + 2 * E * (A - 1) + 2 * (A - 1))
+    wires += (sw // R) * 2 * (A + E) + 2 + 8 * 10
     group_rows = GROUP * rows
     sizes = (A, E, R, rows, width, sw, uc, (2.0 * LAYERS) ** 0.5, head_dim ** (-0.5))
     shape = jax.ShapeDtypeStruct
     anywhere, vmem = pl.BlockSpec(memory_space=pl.ANY), pl.BlockSpec(memory_space=pltpu.VMEM)
-    cols = (qe, 2 * uc, uc)
+    landings = [(64, LANES), (4 * R, qc), None, (4 * R, 2 * uc), (4 * R, uc)]
+    dense_landing = (sw // R, R, width)
     results = pl.pallas_call(
         functools.partial(layer_kernel, sizes),
         out_shape=[
             shape((rows, width), BF16),
             shape((rows, width), F32),
-            shape((GROUP, R, qe), BF16),
-            shape((A * E, R, width), BF16),
+            shape((GROUP, 16, LANES), BF16),
+            shape((GROUP, R, qc), BF16),
+            shape((R, width), BF16),
             shape((GROUP, R, 2 * uc), BF16),
             shape((GROUP, R, uc), BF16),
         ]
-        + [shape((A - 1, 2, E * 4 * R, n), BF16) for n in cols]
-        + [shape((E - 1, 2, 4 * R, n), BF16) for n in cols],
-        in_specs=[anywhere, vmem, vmem] + [anywhere] * 4,
-        out_specs=[vmem, vmem] + [anywhere] * 10,
+        + [
+            shape((A - 1,) + ((2, E * one[0], one[1]) if one else dense_landing), BF16)
+            for one in landings
+        ]
+        + [
+            shape((E - 1,) + ((2,) + one if one else dense_landing), BF16)
+            for one in landings
+        ],
+        in_specs=[anywhere, vmem, vmem] + [anywhere] * 5,
+        out_specs=[vmem, vmem] + [anywhere] * 15,
         scratch_shapes=[
-            pltpu.VMEM((width, qe), BF16),
+            pltpu.VMEM((width // R * 16, LANES), BF16),
+            pltpu.VMEM((width, qc), BF16),
             pltpu.VMEM((sw, width), BF16),
             pltpu.VMEM((width, 2 * uc), BF16),
+            pltpu.VMEM((width, uc), BF16),
             pltpu.VMEM((width, uc), BF16),
             pltpu.VMEM((group_rows, width + LANES), BF16),
             pltpu.VMEM((group_rows, width), BF16),
@@ -932,35 +1122,35 @@
             pltpu.VMEM((rows, width), F32),
             pltpu.VMEM((rows, LANES), F32),
             pltpu.VMEM((16, width), F32),
-            pltpu.VMEM((LANES, width), F32),
+            pltpu.VMEM((16, width), F32),
             pltpu.VMEM((8, qc), F32),
             pltpu.VMEM((E * 4 * R, 2 * uc), BF16),
-            pltpu.SemaphoreType.DMA((5,)),
+            pltpu.VMEM((R, width), BF16),
+            pltpu.SemaphoreType.DMA((6,)),
             pltpu.SemaphoreType.DMA((wires,)),
             pltpu.SemaphoreType.DMA((wires,)),
         ],
         compiler_params=pltpu.CompilerParams(
             collective_id=0, has_side_effects=True, vmem_limit_bytes=63 << 20
         ),
-    )(x_ext, cot, table, qkv_pieces, dense_weight, ffin_pieces, ffout_pieces)
-    result, d_tokens, qkv_grad, dense_grad, ffin_grad, ffout_grad = results[:6]
+    )(x_ext, cot, table, small_pieces, qkv_pieces, dense_weight, ffin_pieces, ffout_pieces)
+    result, d_tokens, small_grads, qkv_grad, dense_grad, ffin_grad, ffout_grad = results[:7]
 
     def unit_columns(pieces):
         return pieces.transpose(1, 0, 2).reshape(R, padded)[:, :hidden].astype(F32)
 
     grad_qkv = (
-        qkv_grad[:, :, :qc]
-        .reshape(2, 2, 2, R, 3, my_heads, head_dim)
+        qkv_grad.reshape(2, 2, 2, R, 3, my_heads, head_dim)
         .transpose(3, 4, 5, 1, 0, 2, 6)
         .reshape(R, 3 * width)
         .astype(F32)
     )
-    small_grads = jnp.sum(qkv_grad[:, :, qc:].astype(F32), axis=0)
+    small_grads = jnp.sum(small_grads.astype(F32), axis=0)[:, :R].T
     return (
         result.reshape(tokens.shape),
         d_tokens.reshape(tokens.shape),
         grad_qkv,
-        jnp.sum(dense_grad.astype(F32), axis=0),
+        dense_grad.astype(F32),
         jnp.concatenate(
             [unit_columns(ffin_grad[:, :, :uc]), unit_columns(ffin_grad[:, :, uc:])], axis=1
         ),

time: 578 us -> 510 us (0.88)
  Pallas kernels: 545 us -> 477 us
    pallas_call x1, Pallas kernels: 545 us -> 477 us  [on_device(): pl.pallas_call(functools.partial(layer_kernel, sizes), out_shape=[shape((...]
where the time goes in v3:
time: 510 us; the launch traced here: 509 us
  Pallas kernels  477 us (94%)
  local copies, waits for them, and re-layouts  16.3 us (3%)
  other arithmetic  15.2 us (3%)
    pallas_call x1, Pallas kernels, on_device(): pl.pallas_call(functools.partial(layer_kernel, sizes), out_shape=[shape((...  477 us

profile of v3, /device:TPU:0, one launch (start us, length us, event | category | flops | bytes accessed | tf_op | source)
XLA Modules:
  0.0 508.8 jit_solution(1923510309666080535)
XLA Ops:
  0.6 0.0 copy-start
  0.6 0.9 reduce_window_sum.11
  1.6 0.6 slice.34
  2.2 0.1 convert_reduce_fusion.1
  2.2 0.6 iota_compare_fusion.3
  2.9 0.7 subtract_bitcast_fusion
  3.6 0.7 select_reduce_fusion.1
  4.3 0.7 fusion.2
  5.0 0.7 maximum_bitcast_fusion
  5.7 0.6 broadcast_in_dim.58.sp_ref
  6.3 0.1 copy.44
  6.5 1.9 bitcast_select_fusion.cot_ref
  8.4 1.9 fusion.1.x_ref
  10.3 0.0 copy-done
  10.3 0.0 copy-start.4
  10.3 0.3 slice.36
  10.6 0.1 pad.21
  10.6 0.8 copy-done.4
  11.4 0.6 reshape.104
  12.0 0.0 copy-start.6
  12.0 0.6 copy.64
  12.6 1.2 reshape.105.qp_ref
  13.9 0.0 copy-done.6
  13.9 0.0 copy-start.1
  13.9 0.0 copy-start.8
  13.9 0.1 pad.22
  13.9 0.9 copy.63
  14.9 0.6 copy-done.1
  15.5 0.0 copy-done.8
  15.5 0.1 slice_select_fusion
  15.6 0.2 bitcast_bitcast_fusion.1
  15.8 1.3 pad_maximum_fusion.ip_ref
  17.1 476.5 %shard_map.170 = (bf16[128,2048]{1,0:T(8,128)(2,1)}, f32[128,2048]{1,0:T(8,128)}, bf16[8,16,128]{2,1,0:T(8,128)(2,1)}, bf16[8,64,768]{2,1,0:T(8,128)(2,1)}, bf16...) custom-call(bf16[128,2176]{1,0:T(8,128)(2,1)} %fusion.1.x_ref, ...), custom_call_target="tpu_custom_call" | custom-call | tf_op jit(solution)/shard_map/pallas_call | solution.py:1078
  493.6 0.8 convert_reduce_fusion
  494.4 0.6 slice.50
  494.9 0.6 slice.49
  495.5 1.8 convert_element_type.42
  497.3 0.0 copy-start.5
  497.3 1.3 copy.58
  498.6 1.2 slice_convert_fusion
  499.8 0.0 copy-done.5
  499.8 0.8 reshape.115
  500.5 1.2 copy.49
  501.8 0.0 copy-start.2
  501.8 2.4 reshape.114
  504.2 0.0 copy-done.2
  504.2 0.2 slice_bitcast_fusion.1
  504.3 0.1 copy.56
  504.5 0.1 copy.57
  504.6 0.0 copy-start.7
  504.6 1.9 maximum_convert_fusion
  506.4 0.0 copy-done.7
  506.4 0.0 copy-start.3
  506.4 0.8 copy.67
  507.2 0.6 copy-done.3
  507.9 1.0 copy.68
  (6 shorter events, 0.1 us)
Async XLA Ops:
  0.6 9.7 %copy-start = (bf16[64,10922]{1,0:T(8,128)(2,1)S(1)}, bf16[64,10922]{1,0:T(8,128)(2,1)}, u32[]{:S(2)}) copy-start(bf16[64,10922]{1,0:T(8,128)(2,1)} %param.17) | copy-start | bytes 4194052
  10.3 1.1 copy-start.4
  12.0 1.9 copy-start.6
  13.9 1.6 copy-start.1
  13.9 1.6 copy-start.8
  497.3 2.5 copy-start.5
  501.8 2.4 copy-start.2
  504.6 1.9 copy-start.7
  506.4 1.4 copy-start.3

commit v4 on v3

--- a/solution.py
+++ b/solution.py
@@ -19,6 +19,7 @@
 AXES = ("a", "b", "e", "f", "c")
 GROUP = 8
 LANES = 128
+SHARED = 6
 DEVICE_MESH = pl.DeviceIdType.MESH
 BF16 = jnp.bfloat16
 F32 = jnp.float32
@@ -43,7 +44,7 @@
         self.count += numbers
         return first
 
-    def send(self, number, source, target, device):
+    def send(self, number, source, target, device, condition=None):
         one = pltpu.make_async_remote_copy(
             src_ref=source,
             dst_ref=target,
@@ -52,50 +53,64 @@
             device_id=device,
             device_id_type=DEVICE_MESH,
         )
-        one.start()
-        return one
-
-    def arrived(self, number, landing):
-        pltpu.make_async_copy(landing, landing, self.recv_sem.at[number]).wait()
+        when(condition, one.start)
+        return condition, one
+
+    def arrived(self, number, landing, condition=None):
+        when(condition, pltpu.make_async_copy(landing, landing, self.recv_sem.at[number]).wait)
+
+
+def when(condition, body):
+    if condition is None:
+        body()
+    else:
+        pl.when(condition)(body)
 
 
 def sent(copies):
-    for one in copies:
-        one.wait_send()
+    for condition, one in copies:
+        when(condition, one.wait_send)
     copies.clear()
 
 
 def layer_kernel(
     sizes,
-    x_ref,
+    len_ref,
+    pre_ref,
     cot_ref,
     table_ref,
+    x_ref,
     sp_ref,
     qp_ref,
     dp_ref,
-    ip_ref,
+    gp_ref,
+    up_ref,
     op_ref,
     out_ref,
     gx_ref,
     os_ref,
     oq_ref,
     od_ref,
-    oi_ref,
+    og_ref,
+    ou_ref,
     oo_ref,
     ys_ref,
     yq_ref,
     yd_ref,
-    yi_ref,
+    yg_ref,
+    yu_ref,
     yo_ref,
     zs_ref,
     zq_ref,
     zd_ref,
-    zi_ref,
+    zg_ref,
+    zu_ref,
     zo_ref,
     ws_ref,
     wq_ref,
     wd_ref,
-    wi_ref,
+    wg_ref,
+    wu_ref,
     wo_ref,
     go_ref,
     xg_ref,
@@ -116,6 +131,7 @@
     xh_ref,
     dr_ref,
     rstd_ref,
+    valid_ref,
     bt_ref,
     sg_ref,
     qb_ref,
@@ -125,7 +141,7 @@
     send_sem,
     recv_sem,
 ):
-    A, E, R, rows, width, sw, uc, alpha, scale = sizes
+    A, E, R, rows, width, sw, uc, larger, alpha, scale = sizes
     a, b, e, f, c = (lax.axis_index(axis) for axis in AXES)
     qc = 3 * sw
     all_rows = GROUP * rows
@@ -160,24 +176,40 @@
     pl.semaphore_wait(barrier, others)
 
     class Weight:
-        def __init__(self, index, pieces, buf, out, ylanding, zlanding):
-            self.index, self.pieces, self.buf, self.out = index, pieces, buf, out
+        def __init__(self, index, parts, pieces, buf, out, ylanding, zlanding):
+            self.index, self.parts, self.pieces, self.buf, self.out = index, parts, pieces, buf, out
             self.ylanding, self.zlanding = ylanding, zlanding
             self.R = pieces.shape[1]
             self.copies = []
-            self.tp, self.z, self.y = (
-                wires.take(GROUP),
-                wires.take(2 * (E - 1)),
-                wires.take(2 * E * (A - 1)),
-            )
-            self.gtp, self.gz, self.gy = (
-                wires.take(GROUP),
-                wires.take(2 * (E - 1)),
-                wires.take(2 * (A - 1)),
-            )
-
-        def send(self, *copy):
-            self.copies.append(wires.send(*copy))
+            take = lambda count: wires.take(count * len(parts))
+            self.tp, self.z, self.y = take(GROUP), take(2 * (E - 1)), take(2 * E * (A - 1))
+            self.gtp, self.gz, self.gy = take(GROUP), take(2 * (E - 1)), take(2 * (A - 1))
+
+        def each(self, member, body):
+            for k, (first, size, extra) in enumerate(self.parts):
+                body(k, pl.ds(first, size), member < larger if extra else None)
+
+        def send(self, first, number, source, target, device, member=me):
+            def body(k, cols, condition):
+                self.copies.append(
+                    wires.send(
+                        first + number * len(self.parts) + k,
+                        source.at[:, cols],
+                        target.at[:, cols],
+                        device,
+                        condition,
+                    )
+                )
+
+            self.each(member, body)
+
+        def arrived(self, first, number, landing, member=me):
+            def body(k, cols, condition):
+                wires.arrived(
+                    first + number * len(self.parts) + k, landing.at[:, cols], condition
+                )
+
+            self.each(member, body)
 
         def line(self, aa, bb, ee, ff, cc):
             return span(rank(aa, bb, ee, ff, cc) * self.R, self.R)
@@ -188,9 +220,12 @@
         def half(self, aa, bb):
             return span((aa * 2 + bb) * E * 4 * self.R, E * 4 * self.R)
 
+        def piece(self, place):
+            return self.pieces.at[place if self.pieces.shape[0] > 1 else 0]
+
         def own(self):
             return pltpu.make_async_copy(
-                self.pieces.at[me], self.buf.at[self.line(a, b, e, f, c)], local_sem.at[self.index]
+                self.piece(me), self.buf.at[self.line(a, b, e, f, c)], local_sem.at[self.index]
             )
 
         def tp_send(self):
@@ -198,11 +233,14 @@
             for r in range(1, GROUP):
                 db, df, dc = peers[r]
                 bb, ff, cc = flip(b, db), flip(f, df), flip(c, dc)
+                place = slot(bb, ff, cc)
                 self.send(
-                    self.tp + r,
-                    self.pieces.at[slot(bb, ff, cc)],
+                    self.tp,
+                    r,
+                    self.piece(place),
                     self.buf.at[self.line(a, b, e, f, c)],
                     {"b": bb, "f": ff, "c": cc},
+                    place,
                 )
 
         def tp_wait(self, db):
@@ -211,65 +249,71 @@
                     self.own().wait()
                 else:
                     _, df, dc = peers[r]
-                    wires.arrived(
-                        self.tp + r, self.buf.at[self.line(a, flip(b, db), e, flip(f, df), flip(c, dc))]
-                    )
+                    rows_ = self.line(a, flip(b, db), e, flip(f, df), flip(c, dc))
+                    self.arrived(self.tp, r, self.buf.at[rows_])
 
         def z_send(self, db):
             rows_ = self.buf.at[self.block(a, flip(b, db), e)]
             for s in range(1, E):
-                self.send(
-                    self.z + db * (E - 1) + s - 1, rows_, rows_, {"e": lax.rem(e + s, E)}
-                )
+                self.send(self.z, db * (E - 1) + s - 1, rows_, rows_, {"e": lax.rem(e + s, E)})
 
         def y_send(self, db, s):
             rows_ = self.buf.at[self.block(a, flip(b, db), lax.rem(e + E - s, E))]
             for t in range(1, A):
-                self.send(
-                    self.y + (db * E + s) * (A - 1) + t - 1, rows_, rows_, {"a": lax.rem(a + t, A)}
-                )
+                number = (db * E + s) * (A - 1) + t - 1
+                self.send(self.y, number, rows_, rows_, {"a": lax.rem(a + t, A)})
 
         def z_arrive(self, db):
             for s in range(1, E):
-                wires.arrived(
-                    self.z + db * (E - 1) + s - 1,
-                    self.buf.at[self.block(a, flip(b, db), lax.rem(e + E - s, E))],
-                )
+                rows_ = self.block(a, flip(b, db), lax.rem(e + E - s, E))
+                self.arrived(self.z, db * (E - 1) + s - 1, self.buf.at[rows_])
                 self.y_send(db, s)
 
         def y_arrive(self):
             for db in range(2):
                 for s in range(E):
                     for t in range(1, A):
-                        wires.arrived(
-                            self.y + (db * E + s) * (A - 1) + t - 1,
-                            self.buf.at[
-                                self.block(lax.rem(a + A - t, A), flip(b, db), lax.rem(e + E - s, E))
-                            ],
+                        rows_ = self.block(
+                            lax.rem(a + A - t, A), flip(b, db), lax.rem(e + E - s, E)
                         )
+                        self.arrived(
+                            self.y, (db * E + s) * (A - 1) + t - 1, self.buf.at[rows_]
+                        )
 
         def add(self, landing, base, count):
-            cols = self.buf.shape[1]
-            temp = tm_ref.at[pl.ds(0, count), pl.ds(0, cols)]
-            load = pltpu.make_async_copy(landing, temp, local_sem.at[4])
-            load.start()
-            load.wait()
-
-            @pl.loop(0, count // 16)
-            def _(i):
-                here = pl.ds(pl.multiple_of(base + i * 16, 16), 16)
-                there = span(i * 16, 16)
-                self.buf[here, :] = (
-                    self.buf[here, :].astype(F32) + tm_ref[there, 0:cols].astype(F32)
-                ).astype(BF16)
+            def load(k, cols, condition):
+                copy = pltpu.make_async_copy(
+                    landing.at[:, cols],
+                    tm_ref.at[pl.ds(0, count), cols],
+                    local_sem.at[SHARED + k],
+                )
+                when(condition, copy.start)
+
+                def total():
+                    copy.wait()
+
+                    @pl.loop(0, count // 16)
+                    def _(i):
+                        here = pl.ds(pl.multiple_of(base + i * 16, 16), 16)
+                        there = span(i * 16, 16)
+                        self.buf[here, cols] = (
+                            self.buf[here, cols].astype(F32) + tm_ref[there, cols].astype(F32)
+                        ).astype(BF16)
+
+                return lambda: when(condition, total)
+
+            totals = []
+            self.each(me, lambda *part: totals.append(load(*part)))
+            for total in totals:
+                total()
 
         def gy_send(self, db):
-            bb = flip(b, db)
             for t in range(1, A):
                 to = lax.rem(a + t, A)
                 self.send(
-                    self.gy + db * (A - 1) + t - 1,
-                    self.buf.at[self.half(to, bb)],
+                    self.gy,
+                    db * (A - 1) + t - 1,
+                    self.buf.at[self.half(to, flip(b, db))],
                     self.ylanding.at[t - 1, db],
                     {"a": to},
                 )
@@ -278,12 +322,13 @@
             bb = flip(b, db)
             for t in range(1, A):
                 landing = self.ylanding.at[t - 1, db]
-                wires.arrived(self.gy + db * (A - 1) + t - 1, landing)
+                self.arrived(self.gy, db * (A - 1) + t - 1, landing)
                 self.add(landing, (a * 2 + bb) * E * 4 * self.R, E * 4 * self.R)
             for s in range(1, E):
                 to = lax.rem(e + s, E)
                 self.send(
-                    self.gz + db * (E - 1) + s - 1,
+                    self.gz,
+                    db * (E - 1) + s - 1,
                     self.buf.at[self.block(a, bb, to)],
                     self.zlanding.at[s - 1, db],
                     {"e": to},
@@ -293,7 +338,7 @@
             bb = flip(b, db)
             for s in range(1, E):
                 landing = self.zlanding.at[s - 1, db]
-                wires.arrived(self.gz + db * (E - 1) + s - 1, landing)
+                self.arrived(self.gz, db * (E - 1) + s - 1, landing)
                 self.add(landing, ((a * 2 + bb) * E + e) * 4 * self.R, 4 * self.R)
             for r in range(4 * db, 4 * db + 4):
                 _, df, dc = peers[r]
@@ -302,9 +347,7 @@
                 if r == 0:
                     pltpu.make_async_copy(rows_, self.out.at[me], local_sem.at[self.index]).start()
                 else:
-                    self.send(
-                        self.gtp + r, rows_, self.out.at[me], {"b": bb, "f": ff, "c": cc}
-                    )
+                    self.send(self.gtp, r, rows_, self.out.at[me], {"b": bb, "f": ff, "c": cc})
 
         def g_end(self):
             for r in range(GROUP):
@@ -316,14 +359,16 @@
                         local_sem.at[self.index],
                     ).wait()
                 else:
-                    wires.arrived(
-                        self.gtp + r, self.out.at[slot(flip(b, db), flip(f, df), flip(c, dc))]
-                    )
-
-    s_w = Weight(3, sp_ref, ws_ref, os_ref, ys_ref, zs_ref)
-    q_w = Weight(0, qp_ref, wq_ref, oq_ref, yq_ref, zq_ref)
-    i_w = Weight(1, ip_ref, wi_ref, oi_ref, yi_ref, zi_ref)
-    o_w = Weight(2, op_ref, wo_ref, oo_ref, yo_ref, zo_ref)
+                    place = slot(flip(b, db), flip(f, df), flip(c, dc))
+                    self.arrived(self.gtp, r, self.out.at[place], place)
+
+    tile = uc - LANES
+    shares = [(0, tile, False), (tile, LANES, True)]
+    s_w = Weight(0, [(0, LANES, False)], sp_ref, ws_ref, os_ref, ys_ref, zs_ref)
+    q_w = Weight(1, [(0, qc, False)], qp_ref, wq_ref, oq_ref, yq_ref, zq_ref)
+    g_w = Weight(2, shares, gp_ref, wg_ref, og_ref, yg_ref, zg_ref)
+    u_w = Weight(3, shares, up_ref, wu_ref, ou_ref, yu_ref, zu_ref)
+    o_w = Weight(4, shares, op_ref, wo_ref, oo_ref, yo_ref, zo_ref)
 
     def remote(source, landing, send, recv, target):
         return pltpu.make_async_remote_copy(
@@ -461,7 +506,7 @@
                         copy.start() if start else copy.wait_send()
 
         def add(self, landing, piece):
-            load = pltpu.make_async_copy(landing, td_ref, local_sem.at[4])
+            load = pltpu.make_async_copy(landing, td_ref, local_sem.at[SHARED])
             load.start()
             load.wait()
 
@@ -658,13 +703,13 @@
         def _(k):
             body(k // count_n, lax.rem(k, count_n))
 
-    def onto_partial(left, weight, cols):
+    def onto_partial(*terms):
         def multiply(first, count):
             def body(m, n):
                 here = pl.ds(pl.multiple_of(first, half_rows) + m * 512, 512)
-                pb_ref[here, span(n * 512, 512)] = dot(
-                    left[here, :], weight[span(n * 512, 512), 0:cols], NT
-                ).astype(BF16)
+                there = span(n * 512, 512)
+                total = sum(dot(left[here, :], weight[there, :], NT) for left, weight in terms)
+                pb_ref[here, there] = total.astype(BF16)
 
             blocks(count // 512, width // 512, body)
 
@@ -673,9 +718,33 @@
     q_w.tp_send()
     s_w.tp_send()
     dense.out(True)
-    own_x = pltpu.make_async_copy(x_ref, xg_ref.at[my_rows], local_sem.at[5])
+    own_x = pltpu.make_async_copy(
+        x_ref.at[0], xg_ref.at[my_rows, pl.ds(0, width)], local_sem.at[5]
+    )
     own_x.start()
     sg_ref[...] = jnp.zeros_like(sg_ref)
+
+    @pl.when(me >= larger)
+    def _():
+        for weight in (g_w, u_w, o_w):
+            weight.buf[:, tile:] = jnp.zeros((width, LANES), BF16)
+
+    at = lax.broadcasted_iota(jnp.int32, (rows, LANES), 0)
+    lane = lax.broadcasted_iota(jnp.int32, (rows, LANES), 1)
+    docs = len_ref.shape[1]
+    key, prefix_at, local_pos, valid, first = at + docs, at * 0, at * 0, at < 0, 0
+    for k in range(docs):
+        last = first + len_ref[0, k]
+        member = (at >= first) & (at < last)
+        key = jnp.where(member, k, key)
+        prefix_at = jnp.where(member, pre_ref[0, k], prefix_at)
+        local_pos = jnp.where(member, at - first, local_pos)
+        valid = valid | member
+        first = last
+    info = jnp.where(lane == 0, key, jnp.where(lane == 1, prefix_at, local_pos))
+    xg_ref[my_rows, width:] = info.astype(F32).astype(BF16)
+    valid_ref[...] = jnp.where(valid, 1.0, 0.0)
+
     tokens = Gather(xg_ref, True)
     for db in range(2):
         q_w.tp_wait(db)
@@ -683,29 +752,31 @@
         q_w.y_send(db, 0)
     own_x.wait()
     tokens.start()
-    i_w.tp_send()
+    g_w.tp_send()
     for db in range(2):
         s_w.tp_wait(db)
         s_w.z_send(db)
         s_w.y_send(db, 0)
     dense.z_send()
+    u_w.tp_send()
     q_w.z_arrive(0)
     tokens.relay()
-    i_w.tp_wait(0)
-    i_w.z_send(0)
-    i_w.y_send(0, 0)
+    g_w.tp_wait(0)
+    g_w.z_send(0)
+    g_w.y_send(0, 0)
     q_w.z_arrive(1)
     s_w.z_arrive(0)
     s_w.z_arrive(1)
-    i_w.tp_wait(1)
     dense.y_send()
-    i_w.y_send(1, 0)
+    g_w.tp_wait(1)
+    g_w.z_send(1)
+    g_w.y_send(1, 0)
     tokens.finish()
     o_w.tp_send()
     s_w.y_arrive()
     q_w.y_arrive()
 
-    lane = lax.broadcasted_iota(jnp.int32, (16, LANES), 1)
+    lane = lane[0:16, :]
 
     @pl.loop(0, width // LANES)
     def _(k):
@@ -772,7 +843,11 @@
             probs = softmax(q, k, allowed).astype(BF16)
             cx_ref[here, i * LANES : (i + 1) * LANES] = dot(probs, v).astype(BF16)
 
-    i_w.z_send(1)
+    u_w.tp_wait(0)
+    u_w.tp_wait(1)
+    u_w.z_send(0)
+    u_w.z_send(1)
+    g_w.z_arrive(0)
     dense.y_arrive()
 
     def dense_partial(first, count):
@@ -783,7 +858,11 @@
 
         blocks(count // 512, width // 512, body)
 
-    scatter(dense_partial, True, lambda: i_w.z_arrive(0))
+    def more_units():
+        u_w.y_send(0, 0)
+        u_w.y_send(1, 0)
+
+    scatter(dense_partial, True, lambda: g_w.z_arrive(1), more_units)
     for db in range(2):
         o_w.tp_wait(db)
         o_w.z_send(db)
@@ -810,20 +889,22 @@
     row_loop(first_norm)
     normed = Gather(hg_ref, True)
     normed.start()
+    u_w.z_arrive(0)
+    normed.relay()
     o_w.y_send(0, 0)
     o_w.y_send(1, 0)
-    normed.relay()
-    i_w.z_arrive(1)
+    u_w.z_arrive(1)
     normed.finish()
-    i_w.y_arrive()
+    g_w.y_arrive()
+    u_w.y_arrive()
 
     def units(m, n):
         here = span(m * 512, 512)
         gate_cols = span(n * 256, 256)
         up_cols = span(uc + n * 256, 256)
         left = hg_ref[here, :]
-        gate = dot(left, wi_ref[:, gate_cols])
-        up = dot(left, wi_ref[:, up_cols])
+        gate = dot(left, wg_ref[:, gate_cols])
+        up = dot(left, wu_ref[:, gate_cols])
         cdf = 0.5 * (1.0 + lax.erf(gate * (0.5**0.5)))
         density = jnp.exp(-0.5 * gate * gate) * (1.0 / math.sqrt(2.0 * math.pi))
         act = gate * cdf
@@ -835,7 +916,7 @@
     o_w.z_arrive(0)
     o_w.z_arrive(1)
     o_w.y_arrive()
-    scatter(onto_partial(mb_ref, wo_ref, uc), False)
+    scatter(onto_partial((mb_ref, wo_ref)), False)
 
     def add_row(row, value):
         sg_ref[row : row + 1, :] += jnp.sum(value, axis=0, keepdims=True)
@@ -852,7 +933,7 @@
         normed_one = xh_ref[here, :] * bt_ref[7:8, :] + bt_ref[4:5, :]
         unit, rstd = normalize(alpha * normed_one + sum_ref[here, :] + bt_ref[5:6, :])
         out_ref[here, :] = (unit * bt_ref[8:9, :] + bt_ref[6:7, :]).astype(BF16)
-        grad = cot_ref[here, :].astype(F32)
+        grad = cot_ref[0, here, :].astype(F32) * valid_ref[here, 0:1]
         back = norm_back(grad, bt_ref[8:9, :], unit, rstd)
         low = back.astype(BF16)
         dr_ref[here, :] = back
@@ -888,14 +969,20 @@
     o_w.gy_send(1)
     blocks(all_rows // 512, uc // 256, units_back)
 
+    du_gate = du_ref.at[:, pl.ds(0, uc)]
+    du_up = du_ref.at[:, pl.ds(uc, uc)]
+
     def in_grad():
-        sent(i_w.copies)
-        weight_grad(hg_ref, du_ref, wi_ref, 2 * uc, uc)
-        i_w.gy_send(0)
-        i_w.gy_send(1)
+        for weight, right in ((g_w, du_gate), (u_w, du_up)):
+            sent(weight.copies)
+            weight_grad(hg_ref, right, weight.buf, uc, uc)
+            weight.gy_send(0)
+            weight.gy_send(1)
 
     sent(branch.copies)
-    scatter(onto_partial(du_ref, wi_ref, 2 * uc), False, in_grad, lambda: o_w.gy_add(0))
+    scatter(
+        onto_partial((du_gate, wg_ref), (du_up, wu_ref)), False, in_grad, lambda: o_w.gy_add(0)
+    )
 
     def first_norm_back(here, there):
         grad = alpha * dr_ref[here, :] + sum_ref[here, :]
@@ -913,6 +1000,7 @@
     attended.start()
     o_w.gy_add(1)
     attended.relay()
+    g_w.gy_add(0)
     attended.finish()
 
     def context_back(m, n):
@@ -928,6 +1016,7 @@
     dense.sent()
     blocks(1, width // 512, dense_grad)
     dense.gy_send()
+    g_w.gy_add(1)
 
     @pl.loop(0, GROUP)
     def _(s):
@@ -949,7 +1038,7 @@
                 lanes = span(number * LANES, LANES)
                 sg_ref[t : t + 1, lanes] += jnp.sum(value.astype(F32), axis=0, keepdims=True)
 
-    i_w.gy_add(0)
+    u_w.gy_add(0)
 
     def qkv_grad():
         sent(q_w.copies)
@@ -969,10 +1058,7 @@
         s_w.gy_send(0)
         s_w.gy_send(1)
 
-    def late_adds():
-        i_w.gy_add(1)
-
-    scatter(onto_partial(mb_ref, wq_ref, qc), True, qkv_grad, late_adds)
+    scatter(onto_partial((mb_ref, wq_ref)), True, qkv_grad, lambda: u_w.gy_add(1))
 
     def tokens_back(here, there):
         gx_ref[here, :] = alpha * dr_ref[here, :] + sum_ref[here, :]
@@ -986,16 +1072,18 @@
     q_w.gy_add(1)
     s_w.gy_add(0)
     s_w.gy_add(1)
+    for db in range(2):
+        g_w.gz_add(db)
+    for db in range(2):
+        u_w.gz_add(db)
     dense.gz_add()
-    i_w.gz_add(0)
-    i_w.gz_add(1)
-    q_w.gz_add(0)
-    q_w.gz_add(1)
-    s_w.gz_add(0)
-    s_w.gz_add(1)
-    for weight in (dense, o_w, i_w, q_w, s_w):
+    for db in range(2):
+        q_w.gz_add(db)
+    for db in range(2):
+        s_w.gz_add(db)
+    for weight in (dense, o_w, g_w, u_w, q_w, s_w):
         weight.g_end()
-    for flow in (q_w, i_w, o_w, s_w, tokens, normed, attended):
+    for flow in (q_w, g_w, u_w, o_w, s_w, tokens, normed, attended):
         sent(flow.copies)
 
 
@@ -1017,26 +1105,12 @@
     head_dim = width // HEADS
     my_heads = HEADS // GROUP
     hidden = ffout_weight.shape[1]
-    uc = -(-hidden // (GROUP * 256)) * 256
-    padded = uc * GROUP
+    tiles = -(-hidden // LANES)
+    larger = tiles % GROUP
+    uc = (tiles // GROUP + 1) * LANES
+    smaller = uc - LANES
     sw = my_heads * head_dim
     qc = 3 * sw
-    docs = lengths.shape[1]
-
-    ends = jnp.cumsum(lengths, axis=1)
-    positions = jnp.arange(rows, dtype=jnp.int32)[:, None]
-    index = jnp.sum((positions >= ends).astype(jnp.int32), axis=1, keepdims=True)
-    member = index == jnp.arange(docs, dtype=jnp.int32)[None, :]
-    start_at = jnp.sum(jnp.where(member, ends - lengths, 0), axis=1, keepdims=True)
-    prefix_at = jnp.sum(jnp.where(member, prefix, 0), axis=1, keepdims=True)
-    valid = positions < ends[:, -1:]
-    key = jnp.where(valid, index, docs + positions)
-    local_pos = jnp.where(valid, positions - start_at, 0)
-    info = jnp.concatenate([key, prefix_at, local_pos], axis=1).astype(BF16)
-    x_ext = jnp.concatenate(
-        [tokens.reshape(rows, width), jnp.pad(info, ((0, 0), (0, LANES - 3)))], axis=1
-    )
-    cot = jnp.where(valid, cotangent.reshape(rows, width), 0).astype(BF16)
 
     inverse = np.float32(ROPE_BASE) ** (
         -np.arange(head_dim // 2, dtype=np.float32) * np.float32(2.0 / head_dim)
@@ -1056,24 +1130,26 @@
     )
     small = jnp.concatenate([biases, norm_gains], axis=1).T
     small = jnp.pad(small, ((0, 16 - small.shape[0]), (0, LANES - R)))
-    small_pieces = jnp.broadcast_to(small, (GROUP, 16, LANES))
+    small_pieces = small[None]
 
     def unit_pieces(weight):
-        wide = jnp.pad(weight, ((0, 0), (0, padded - hidden)))
-        return wide.reshape(R, GROUP, uc).transpose(1, 0, 2)
-
-    ffin_pieces = jnp.concatenate(
-        [unit_pieces(ffin_weight[:, :hidden]), unit_pieces(ffin_weight[:, hidden:])], axis=2
-    )
+        wide = jnp.pad(weight, ((0, 0), (0, tiles * LANES - hidden)))
+        first = wide[:, : larger * uc].reshape(R, larger, uc)
+        rest = wide[:, larger * uc :].reshape(R, GROUP - larger, smaller)
+        rest = jnp.pad(rest, ((0, 0), (0, 0), (0, LANES)))
+        return jnp.concatenate([first, rest], axis=1).transpose(1, 0, 2)
+
+    gate_pieces = unit_pieces(ffin_weight[:, :hidden])
+    up_pieces = unit_pieces(ffin_weight[:, hidden:])
     ffout_pieces = unit_pieces(ffout_weight)
 
-    wires = 4 * (2 * GROUP + 4 * (E - 1) + 2 * E * (A - 1) + 2 * (A - 1))
+    wires = 8 * (2 * GROUP + 4 * (E - 1) + 2 * E * (A - 1) + 2 * (A - 1))
     wires += (sw // R) * 2 * (A + E) + 2 + 8 * 10
     group_rows = GROUP * rows
-    sizes = (A, E, R, rows, width, sw, uc, (2.0 * LAYERS) ** 0.5, head_dim ** (-0.5))
+    sizes = (A, E, R, rows, width, sw, uc, larger, (2.0 * LAYERS) ** 0.5, head_dim ** (-0.5))
     shape = jax.ShapeDtypeStruct
     anywhere, vmem = pl.BlockSpec(memory_space=pl.ANY), pl.BlockSpec(memory_space=pltpu.VMEM)
-    landings = [(64, LANES), (4 * R, qc), None, (4 * R, 2 * uc), (4 * R, uc)]
+    landings = [(64, LANES), (4 * R, qc), None] + [(4 * R, uc)] * 3
     dense_landing = (sw // R, R, width)
     results = pl.pallas_call(
         functools.partial(layer_kernel, sizes),
@@ -1083,9 +1159,8 @@
             shape((GROUP, 16, LANES), BF16),
             shape((GROUP, R, qc), BF16),
             shape((R, width), BF16),
-            shape((GROUP, R, 2 * uc), BF16),
-            shape((GROUP, R, uc), BF16),
         ]
+        + [shape((GROUP, R, uc), BF16)] * 3
         + [
             shape((A - 1,) + ((2, E * one[0], one[1]) if one else dense_landing), BF16)
             for one in landings
@@ -1094,13 +1169,14 @@
             shape((E - 1,) + ((2,) + one if one else dense_landing), BF16)
             for one in landings
         ],
-        in_specs=[anywhere, vmem, vmem] + [anywhere] * 5,
-        out_specs=[vmem, vmem] + [anywhere] * 15,
+        in_specs=[pl.BlockSpec(memory_space=pltpu.SMEM)] * 2 + [vmem] * 2 + [anywhere] * 7,
+        out_specs=[vmem, vmem] + [anywhere] * 18,
         scratch_shapes=[
             pltpu.VMEM((width // R * 16, LANES), BF16),
             pltpu.VMEM((width, qc), BF16),
             pltpu.VMEM((sw, width), BF16),
-            pltpu.VMEM((width, 2 * uc), BF16),
+            pltpu.VMEM((width, uc), BF16),
+            pltpu.VMEM((width, uc), BF16),
             pltpu.VMEM((width, uc), BF16),
             pltpu.VMEM((width, uc), BF16),
             pltpu.VMEM((group_rows, width + LANES), BF16),
@@ -1121,23 +1197,39 @@
             pltpu.VMEM((rows, width), F32),
             pltpu.VMEM((rows, width), F32),
             pltpu.VMEM((rows, LANES), F32),
+            pltpu.VMEM((rows, LANES), F32),
             pltpu.VMEM((16, width), F32),
             pltpu.VMEM((16, width), F32),
             pltpu.VMEM((8, qc), F32),
-            pltpu.VMEM((E * 4 * R, 2 * uc), BF16),
+            pltpu.VMEM((E * 4 * R, max(uc, qc)), BF16),
             pltpu.VMEM((R, width), BF16),
-            pltpu.SemaphoreType.DMA((6,)),
+            pltpu.SemaphoreType.DMA((SHARED + 2,)),
             pltpu.SemaphoreType.DMA((wires,)),
             pltpu.SemaphoreType.DMA((wires,)),
         ],
         compiler_params=pltpu.CompilerParams(
             collective_id=0, has_side_effects=True, vmem_limit_bytes=63 << 20
         ),
-    )(x_ext, cot, table, small_pieces, qkv_pieces, dense_weight, ffin_pieces, ffout_pieces)
-    result, d_tokens, small_grads, qkv_grad, dense_grad, ffin_grad, ffout_grad = results[:7]
+    )(
+        lengths,
+        prefix,
+        cotangent,
+        table,
+        tokens,
+        small_pieces,
+        qkv_pieces,
+        dense_weight,
+        gate_pieces,
+        up_pieces,
+        ffout_pieces,
+    )
+    result, d_tokens, small_grads, qkv_grad, dense_grad, gate_grad, up_grad, ffout_grad = results[:8]
 
     def unit_columns(pieces):
-        return pieces.transpose(1, 0, 2).reshape(R, padded)[:, :hidden].astype(F32)
+        turned = pieces.transpose(1, 0, 2)
+        first = turned[:, :larger].reshape(R, larger * uc)
+        rest = turned[:, larger:, :smaller].reshape(R, (GROUP - larger) * smaller)
+        return jnp.concatenate([first, rest], axis=1)[:, :hidden].astype(F32)
 
     grad_qkv = (
         qkv_grad.reshape(2, 2, 2, R, 3, my_heads, head_dim)
@@ -1152,7 +1244,7 @@
         grad_qkv,
         dense_grad.astype(F32),
         jnp.concatenate(
-            [unit_columns(ffin_grad[:, :, :uc]), unit_columns(ffin_grad[:, :, uc:])], axis=1
+            [unit_columns(gate_grad), unit_columns(up_grad)], axis=1
         ),
         unit_columns(ffout_grad),
         small_grads[:, :7],

time: 510 us -> 482 us (0.945)
  Pallas kernels: 477 us -> 452 us
  other arithmetic: 15.2 us -> 7.81 us
    pallas_call x1, Pallas kernels: 477 us -> 452 us  [on_device(): pl.pallas_call(functools.partial(layer_kernel, sizes), out_shape=[shape((...]
where the time goes in v4:
time: 482 us; the launch traced here: 478 us
  Pallas kernels  452 us (94%)
  local copies, waits for them, and re-layouts  16.9 us (4%)
  other arithmetic  7.81 us (2%)
    pallas_call x1, Pallas kernels, on_device(): pl.pallas_call(functools.partial(layer_kernel, sizes), out_shape=[shape((...  452 us

profile of v4, /device:TPU:0, one launch (start us, length us, event | category | flops | bytes accessed | tf_op | source)
XLA Modules:
  0.0 478.0 jit_solution(8609508262349949899)
XLA Ops:
  0.6 0.0 copy-start.1
  0.6 0.8 maximum_bitcast_fusion
  1.4 0.6 pad_bitcast_fusion.sp_ref
  2.0 1.0 slice.70
  3.0 1.1 slice.67
  4.2 0.0 copy-done.1
  4.2 0.0 copy-start
  4.2 0.0 copy-start.9
  4.3 0.9 fusion.12.op_ref
  5.2 0.6 copy-done
  5.8 0.0 copy-done.9
  5.8 0.1 slice_select_fusion
  6.1 0.3 slice.68
  6.4 0.0 copy-start.3
  6.4 1.3 fusion.8
  7.7 0.0 copy-done.3
  7.8 0.6 reshape.70
  8.3 0.6 copy.54
  8.9 1.2 reshape.71.qp_ref
  10.2 452.4 %shard_map.170 = (bf16[128,2048]{1,0:T(8,128)(2,1)}, f32[128,2048]{1,0:T(8,128)}, bf16[8,16,128]{2,1,0:T(8,128)(2,1)}, bf16[8,64,768]{2,1,0:T(8,128)(2,1)}, bf16...) custom-call(s32[1,4]{1,0:T(1,128)} %len_ref.1, ...), custom_call_target="tpu_custom_call" | custom-call | tf_op jit(solution)/shard_map/pallas_call | solution.py:1154
  462.6 0.0 copy-start.6
  462.6 0.8 convert_reduce_fusion
  463.5 0.6 slice.94
  464.0 0.6 slice.93
  464.6 1.0 slice_bitcast_fusion.5
  465.6 1.0 slice_bitcast_fusion.2
  466.7 0.0 copy-start.5
  466.7 0.0 copy-done.6
  466.9 0.0 copy-start.8
  466.9 0.9 copy-done.5
  468.0 0.0 copy-done.8
  468.0 0.8 convert_element_type.37
  468.8 1.2 fusion.13
  470.0 0.0 copy-start.4
  470.0 1.9 fusion.6
  471.8 0.0 copy-done.4
  471.9 0.8 reshape.87
  472.6 1.2 copy.28
  473.8 0.0 copy-start.7
  473.8 0.0 copy-start.2
  473.9 2.4 reshape.86
  476.3 0.0 copy-done.7
  476.3 0.8 copy.63
  477.1 0.0 copy-done.2
  477.1 1.0 copy.64
  (21 shorter events, 0.6 us)
Async XLA Ops:
  0.6 3.6 copy-start.1
  4.2 1.6 copy-start
  4.2 1.6 copy-start.9
  6.4 1.3 copy-start.3
  462.6 4.1 copy-start.6
  466.7 1.1 copy-start.5
  466.9 1.1 copy-start.8
  470.0 1.9 copy-start.4
  473.8 2.4 copy-start.7
  473.8 3.2 copy-start.2

commit v5 on v4

--- a/solution.py
+++ b/solution.py
@@ -79,21 +79,20 @@
     pre_ref,
     cot_ref,
     table_ref,
+    bias_ref,
+    gain_ref,
     x_ref,
-    sp_ref,
-    qp_ref,
+    rq_ref,
     dp_ref,
-    gp_ref,
-    up_ref,
-    op_ref,
+    ri_ref,
+    ro_ref,
     out_ref,
     gx_ref,
+    fq_ref,
+    fi_ref,
+    fo_ref,
     os_ref,
-    oq_ref,
     od_ref,
-    og_ref,
-    ou_ref,
-    oo_ref,
     ys_ref,
     yq_ref,
     yd_ref,
@@ -106,6 +105,7 @@
     zg_ref,
     zu_ref,
     zo_ref,
+    sp_ref,
     ws_ref,
     wq_ref,
     wd_ref,
@@ -154,6 +154,13 @@
     wires = Wires(send_sem, recv_sem)
     peers = [(r // 4, r // 2 % 2, r % 2) for r in range(GROUP)]
 
+    loads = [
+        pltpu.make_async_copy(raw, final, local_sem.at[SHARED + 2 + k])
+        for k, (raw, final) in enumerate(((rq_ref, fq_ref), (ri_ref, fi_ref), (ro_ref, fo_ref)))
+    ]
+    for load in loads:
+        load.start()
+
     barrier = pltpu.get_barrier_semaphore()
     others = 0
     for da in range(A):
@@ -176,14 +183,14 @@
     pl.semaphore_wait(barrier, others)
 
     class Weight:
-        def __init__(self, index, parts, pieces, buf, out, ylanding, zlanding):
-            self.index, self.parts, self.pieces, self.buf, self.out = index, parts, pieces, buf, out
+        def __init__(self, index, R, parts, piece, buf, out, ylanding, zlanding):
+            self.index, self.R, self.parts, self.buf = index, R, parts, buf
+            self.piece, self.out = piece, out
             self.ylanding, self.zlanding = ylanding, zlanding
-            self.R = pieces.shape[1]
             self.copies = []
             take = lambda count: wires.take(count * len(parts))
             self.tp, self.z, self.y = take(GROUP), take(2 * (E - 1)), take(2 * E * (A - 1))
-            self.gtp, self.gz, self.gy = take(GROUP), take(2 * (E - 1)), take(2 * (A - 1))
+            self.gtp, self.gz, self.gy = take(GROUP), take(2 * (E - 1)), take(2 * E * (A - 1))
 
         def each(self, member, body):
             for k, (first, size, extra) in enumerate(self.parts):
@@ -216,12 +223,6 @@
 
         def block(self, aa, bb, ee):
             return span(((aa * 2 + bb) * E + ee) * 4 * self.R, 4 * self.R)
-
-        def half(self, aa, bb):
-            return span((aa * 2 + bb) * E * 4 * self.R, E * 4 * self.R)
-
-        def piece(self, place):
-            return self.pieces.at[place if self.pieces.shape[0] > 1 else 0]
 
         def own(self):
             return pltpu.make_async_copy(
@@ -307,25 +308,26 @@
             for total in totals:
                 total()
 
-        def gy_send(self, db):
+        def gy_send(self):
+            for s in (*range(1, E), 0):
+                for db in range(2):
+                    for t in range(1, A):
+                        to = lax.rem(a + t, A)
+                        self.send(
+                            self.gy,
+                            (db * E + s) * (A - 1) + t - 1,
+                            self.buf.at[self.block(to, flip(b, db), lax.rem(e + s, E))],
+                            self.ylanding.at[t - 1, db, s],
+                            {"a": to},
+                        )
+
+        def gy_add(self, db, s):
+            bb, to = flip(b, db), lax.rem(e + s, E)
             for t in range(1, A):
-                to = lax.rem(a + t, A)
-                self.send(
-                    self.gy,
-                    db * (A - 1) + t - 1,
-                    self.buf.at[self.half(to, flip(b, db))],
-                    self.ylanding.at[t - 1, db],
-                    {"a": to},
-                )
-
-        def gy_add(self, db):
-            bb = flip(b, db)
-            for t in range(1, A):
-                landing = self.ylanding.at[t - 1, db]
-                self.arrived(self.gy, db * (A - 1) + t - 1, landing)
-                self.add(landing, (a * 2 + bb) * E * 4 * self.R, E * 4 * self.R)
-            for s in range(1, E):
-                to = lax.rem(e + s, E)
+                landing = self.ylanding.at[t - 1, db, s]
+                self.arrived(self.gy, (db * E + s) * (A - 1) + t - 1, landing)
+                self.add(landing, ((a * 2 + bb) * E + to) * 4 * self.R, 4 * self.R)
+            if s:
                 self.send(
                     self.gz,
                     db * (E - 1) + s - 1,
@@ -333,6 +335,16 @@
                     self.zlanding.at[s - 1, db],
                     {"e": to},
                 )
+
+        def gy_away(self, db):
+            for s in range(1, E):
+                self.gy_add(db, s)
+
+        def home(self):
+            for db in range(2):
+                self.gy_add(db, 0)
+            for db in range(2):
+                self.gz_add(db)
 
         def gz_add(self, db):
             bb = flip(b, db)
@@ -345,9 +357,9 @@
                 ff, cc = flip(f, df), flip(c, dc)
                 rows_ = self.buf.at[self.line(a, bb, e, ff, cc)]
                 if r == 0:
-                    pltpu.make_async_copy(rows_, self.out.at[me], local_sem.at[self.index]).start()
+                    pltpu.make_async_copy(rows_, self.out(me), local_sem.at[self.index]).start()
                 else:
-                    self.send(self.gtp, r, rows_, self.out.at[me], {"b": bb, "f": ff, "c": cc})
+                    self.send(self.gtp, r, rows_, self.out(me), {"b": bb, "f": ff, "c": cc})
 
         def g_end(self):
             for r in range(GROUP):
@@ -355,20 +367,130 @@
                 if r == 0:
                     pltpu.make_async_copy(
                         self.buf.at[self.line(a, b, e, f, c)],
-                        self.out.at[me],
+                        self.out(me),
                         local_sem.at[self.index],
                     ).wait()
                 else:
                     place = slot(flip(b, db), flip(f, df), flip(c, dc))
-                    self.arrived(self.gtp, r, self.out.at[place], place)
+                    self.arrived(self.gtp, r, self.out(place), place)
 
     tile = uc - LANES
     shares = [(0, tile, False), (tile, LANES, True)]
-    s_w = Weight(0, [(0, LANES, False)], sp_ref, ws_ref, os_ref, ys_ref, zs_ref)
-    q_w = Weight(1, [(0, qc, False)], qp_ref, wq_ref, oq_ref, yq_ref, zq_ref)
-    g_w = Weight(2, shares, gp_ref, wg_ref, og_ref, yg_ref, zg_ref)
-    u_w = Weight(3, shares, up_ref, wu_ref, ou_ref, yu_ref, zu_ref)
-    o_w = Weight(4, shares, op_ref, wo_ref, oo_ref, yo_ref, zo_ref)
+
+    def quarter(ref, down, right):
+        return lambda place: ref.at[
+            span((down * GROUP + place) * R, R), pl.ds(right * uc, uc)
+        ]
+
+    def weight(index, parts, down, right, *rest):
+        buf, ylanding, zlanding = rest
+        piece, out = quarter(du_ref, down, right), quarter(hg_ref, down, right)
+        return Weight(index, R, parts, piece, buf, out, ylanding, zlanding)
+
+    s_w = Weight(
+        0,
+        16,
+        [(0, LANES, False)],
+        lambda place: sp_ref,
+        ws_ref,
+        lambda place: os_ref.at[place],
+        ys_ref,
+        zs_ref,
+    )
+    q_w = weight(1, [(0, qc, False)], 0, 0, wq_ref, yq_ref, zq_ref)
+    g_w = weight(2, shares, 0, 1, wg_ref, yg_ref, zg_ref)
+    u_w = weight(3, shares, 1, 0, wu_ref, yu_ref, zu_ref)
+    o_w = weight(4, shares, 1, 1, wo_ref, yo_ref, zo_ref)
+
+    hidden = fo_ref.shape[1]
+    tiles = -(-hidden // LANES)
+    tile_lane = lax.broadcasted_iota(jnp.int32, (R, LANES), 1)
+
+    def lanes_of(ref, start, valid=LANES):
+        def aligned(m):
+            width_ = min(LANES, ref.shape[1] - m * LANES)
+            part = ref[:, m * LANES : m * LANES + max(width_, 0)].astype(F32) if width_ > 0 else None
+            if width_ >= LANES:
+                return part
+            if part is None:
+                return jnp.zeros((R, LANES), F32)
+            return jnp.concatenate([part, jnp.zeros((R, LANES - width_), F32)], axis=1)
+
+        base, off = divmod(start, LANES)
+        value = aligned(base)
+        if off:
+            back = LANES - off
+            value = jnp.where(
+                tile_lane < back,
+                pltpu.roll(value, back, axis=1),
+                pltpu.roll(aligned(base + 1), back, axis=1),
+            )
+        return jnp.where(tile_lane < valid, value, 0.0) if valid < LANES else value
+
+    def member_tiles():
+        for place in range(GROUP):
+            first = place * (uc // LANES - 1) + min(place, larger)
+            for k in range(uc // LANES - (place >= larger)):
+                yield place, k, first + k
+
+    def cut(ref, start, down, right):
+        for place, k, number in member_tiles():
+            at = (down * GROUP + place) * R, right * uc + k * LANES
+            du_ref[at[0] : at[0] + R, at[1] : at[1] + LANES] = lanes_of(
+                ref, start + number * LANES, min(LANES, hidden - number * LANES)
+            ).astype(BF16)
+        for place in range(larger, GROUP):
+            at = (down * GROUP + place) * R, (right + 1) * uc - LANES
+            du_ref[at[0] : at[0] + R, at[1] : at[1] + LANES] = jnp.zeros((R, LANES), BF16)
+
+    def home_tiles(down, right):
+        found = {}
+        for place, k, number in member_tiles():
+            at = (down * GROUP + place) * R, right * uc + k * LANES
+            found[number] = at
+        return lambda number: hg_ref[
+            found[number][0] : found[number][0] + R, found[number][1] : found[number][1] + LANES
+        ].astype(F32)
+
+    def join(ref, groups):
+        total = hidden * len(groups)
+        for number in range(-(-total // LANES)):
+            value = None
+            for k, tile_of in enumerate(groups):
+                shift = k * hidden % LANES
+                first = number - k * hidden // LANES
+                for piece in (first, first - 1) if shift else (first,):
+                    if not 0 <= piece < tiles:
+                        continue
+                    start = k * hidden + piece * LANES - number * LANES
+                    end = min(start + LANES, (k + 1) * hidden - number * LANES)
+                    if start >= LANES or end <= 0:
+                        continue
+                    part = tile_of(piece)
+                    if shift:
+                        part = pltpu.roll(part, shift, axis=1)
+                    if value is None:
+                        value = part
+                    else:
+                        value = jnp.where((tile_lane >= start) & (tile_lane < end), part, value)
+            size = min(LANES, total - number * LANES)
+            ref[:, number * LANES : number * LANES + size] = value[:, :size].astype(BF16)
+
+    def qkv_places():
+        for place in range(GROUP):
+            cc, bb, ff = place // 4, place // 2 % 2, place % 2
+            for t in range(3):
+                for i in range(sw // LANES):
+                    number = i * 8 + bb * 4 + cc * 2 + ff
+                    yield place * R, t * sw + i * LANES, t * width + number * LANES
+
+    def cut_qkv():
+        for row, col, start in qkv_places():
+            du_ref[row : row + R, col : col + LANES] = fq_ref[:, start : start + LANES]
+
+    def join_qkv():
+        for row, col, start in qkv_places():
+            fq_ref[:, start : start + LANES] = hg_ref[row : row + R, col : col + LANES]
 
     def remote(source, landing, send, recv, target):
         return pltpu.make_async_remote_copy(
@@ -715,7 +837,15 @@
 
         return multiply
 
+    loads[0].wait()
+    cut_qkv()
     q_w.tp_send()
+    columns = [bias_ref[...].astype(F32), gain_ref[...].astype(F32)]
+    columns.append(jnp.zeros((R, LANES - sum(one.shape[1] for one in columns)), F32))
+    turned = jnp.concatenate(columns, axis=1).T[0:16, :]
+    if R < LANES:
+        turned = jnp.concatenate([turned, jnp.zeros((16, LANES - R), F32)], axis=1)
+    sp_ref[...] = turned.astype(BF16)
     s_w.tp_send()
     dense.out(True)
     own_x = pltpu.make_async_copy(
@@ -745,6 +875,8 @@
     xg_ref[my_rows, width:] = info.astype(F32).astype(BF16)
     valid_ref[...] = jnp.where(valid, 1.0, 0.0)
 
+    loads[1].wait()
+    cut(fi_ref, 0, 0, 1)
     tokens = Gather(xg_ref, True)
     for db in range(2):
         q_w.tp_wait(db)
@@ -753,6 +885,9 @@
     own_x.wait()
     tokens.start()
     g_w.tp_send()
+    cut(fi_ref, hidden, 1, 0)
+    loads[2].wait()
+    cut(fo_ref, 0, 1, 1)
     for db in range(2):
         s_w.tp_wait(db)
         s_w.z_send(db)
@@ -846,7 +981,6 @@
     u_w.tp_wait(0)
     u_w.tp_wait(1)
     u_w.z_send(0)
-    u_w.z_send(1)
     g_w.z_arrive(0)
     dense.y_arrive()
 
@@ -859,13 +993,11 @@
         blocks(count // 512, width // 512, body)
 
     def more_units():
+        u_w.z_send(1)
         u_w.y_send(0, 0)
         u_w.y_send(1, 0)
 
     scatter(dense_partial, True, lambda: g_w.z_arrive(1), more_units)
-    for db in range(2):
-        o_w.tp_wait(db)
-        o_w.z_send(db)
 
     def row_loop(body):
         @pl.loop(0, rows // 16)
@@ -889,10 +1021,13 @@
     row_loop(first_norm)
     normed = Gather(hg_ref, True)
     normed.start()
+    for db in range(2):
+        o_w.tp_wait(db)
+        o_w.z_send(db)
     u_w.z_arrive(0)
-    normed.relay()
     o_w.y_send(0, 0)
     o_w.y_send(1, 0)
+    normed.relay()
     u_w.z_arrive(1)
     normed.finish()
     g_w.y_arrive()
@@ -962,11 +1097,11 @@
 
         blocks(width // 512, cols // bn, body)
 
-    sent(o_w.copies)
+    for flow in (normed, q_w, g_w, u_w, o_w):
+        sent(flow.copies)
     weight_grad(dg_ref, mb_ref, go_ref, uc, uc)
     o_w.buf = go_ref
-    o_w.gy_send(0)
-    o_w.gy_send(1)
+    o_w.gy_send()
     blocks(all_rows // 512, uc // 256, units_back)
 
     du_gate = du_ref.at[:, pl.ds(0, uc)]
@@ -974,14 +1109,14 @@
 
     def in_grad():
         for weight, right in ((g_w, du_gate), (u_w, du_up)):
-            sent(weight.copies)
             weight_grad(hg_ref, right, weight.buf, uc, uc)
-            weight.gy_send(0)
-            weight.gy_send(1)
+            weight.gy_send()
+            if weight is g_w:
+                o_w.gy_away(0)
 
     sent(branch.copies)
     scatter(
-        onto_partial((du_gate, wg_ref), (du_up, wu_ref)), False, in_grad, lambda: o_w.gy_add(0)
+        onto_partial((du_gate, wg_ref), (du_up, wu_ref)), False, in_grad, lambda: o_w.gy_away(1)
     )
 
     def first_norm_back(here, there):
@@ -998,9 +1133,9 @@
     row_loop(first_norm_back)
     attended = Gather(dg_ref, True)
     attended.start()
-    o_w.gy_add(1)
+    g_w.gy_away(0)
     attended.relay()
-    g_w.gy_add(0)
+    g_w.gy_away(1)
     attended.finish()
 
     def context_back(m, n):
@@ -1016,7 +1151,8 @@
     dense.sent()
     blocks(1, width // 512, dense_grad)
     dense.gy_send()
-    g_w.gy_add(1)
+    u_w.gy_away(0)
+    o_w.home()
 
     @pl.loop(0, GROUP)
     def _(s):
@@ -1038,14 +1174,16 @@
                 lanes = span(number * LANES, LANES)
                 sg_ref[t : t + 1, lanes] += jnp.sum(value.astype(F32), axis=0, keepdims=True)
 
-    u_w.gy_add(0)
+    u_w.gy_away(1)
+
+    def late_adds():
+        q_w.gy_away(0)
+        g_w.home()
 
     def qkv_grad():
-        sent(q_w.copies)
         weight_grad(xg_ref, mb_ref, wq_ref, qc, qc)
 
-        q_w.gy_send(0)
-        q_w.gy_send(1)
+        q_w.gy_send()
         sent(s_w.copies)
 
         @pl.loop(0, width // LANES)
@@ -1055,35 +1193,38 @@
                 part = line if j == 0 else pltpu.roll(line, LANES - j * R, axis=1)
                 ws_ref[span((k * (LANES // R) + j) * 16, 16), :] = part.astype(BF16)
 
-        s_w.gy_send(0)
-        s_w.gy_send(1)
-
-    scatter(onto_partial((mb_ref, wq_ref)), True, qkv_grad, lambda: u_w.gy_add(1))
+        s_w.gy_send()
+
+    scatter(onto_partial((mb_ref, wq_ref)), True, qkv_grad, late_adds)
 
     def tokens_back(here, there):
         gx_ref[here, :] = alpha * dr_ref[here, :] + sum_ref[here, :]
 
     row_loop(tokens_back)
 
+    q_w.gy_away(1)
     dense.gy_add()
-    o_w.gz_add(0)
-    o_w.gz_add(1)
-    q_w.gy_add(0)
-    q_w.gy_add(1)
-    s_w.gy_add(0)
-    s_w.gy_add(1)
     for db in range(2):
-        g_w.gz_add(db)
+        s_w.gy_away(db)
+    u_w.home()
     for db in range(2):
-        u_w.gz_add(db)
-    dense.gz_add()
+        q_w.gy_add(db, 0)
+        s_w.gy_add(db, 0)
     for db in range(2):
         q_w.gz_add(db)
     for db in range(2):
         s_w.gz_add(db)
-    for weight in (dense, o_w, g_w, u_w, q_w, s_w):
-        weight.g_end()
-    for flow in (q_w, g_w, u_w, o_w, s_w, tokens, normed, attended):
+    dense.gz_add()
+    o_w.g_end()
+    join(fo_ref, [home_tiles(1, 1)])
+    g_w.g_end()
+    u_w.g_end()
+    join(fi_ref, [home_tiles(0, 1), home_tiles(1, 0)])
+    q_w.g_end()
+    join_qkv()
+    s_w.g_end()
+    dense.g_end()
+    for flow in (q_w, g_w, u_w, o_w, s_w, tokens, attended):
         sent(flow.copies)
 
 
@@ -1105,10 +1246,6 @@
     head_dim = width // HEADS
     my_heads = HEADS // GROUP
     hidden = ffout_weight.shape[1]
-    tiles = -(-hidden // LANES)
-    larger = tiles % GROUP
-    uc = (tiles // GROUP + 1) * LANES
-    smaller = uc - LANES
     sw = my_heads * head_dim
     qc = 3 * sw
 
@@ -1123,27 +1260,10 @@
         rest = rest - terms[-1].astype(np.float32)
     table = jnp.asarray(np.concatenate(terms, axis=1))
 
-    qkv_pieces = (
-        qkv_weight.reshape(R, 3, my_heads, 2, 2, 2, head_dim)
-        .transpose(4, 3, 5, 0, 1, 2, 6)
-        .reshape(GROUP, R, qc)
-    )
-    small = jnp.concatenate([biases, norm_gains], axis=1).T
-    small = jnp.pad(small, ((0, 16 - small.shape[0]), (0, LANES - R)))
-    small_pieces = small[None]
-
-    def unit_pieces(weight):
-        wide = jnp.pad(weight, ((0, 0), (0, tiles * LANES - hidden)))
-        first = wide[:, : larger * uc].reshape(R, larger, uc)
-        rest = wide[:, larger * uc :].reshape(R, GROUP - larger, smaller)
-        rest = jnp.pad(rest, ((0, 0), (0, 0), (0, LANES)))
-        return jnp.concatenate([first, rest], axis=1).transpose(1, 0, 2)
-
-    gate_pieces = unit_pieces(ffin_weight[:, :hidden])
-    up_pieces = unit_pieces(ffin_weight[:, hidden:])
-    ffout_pieces = unit_pieces(ffout_weight)
-
-    wires = 8 * (2 * GROUP + 4 * (E - 1) + 2 * E * (A - 1) + 2 * (A - 1))
+    tiles = -(-hidden // LANES)
+    larger = tiles % GROUP
+    uc = (tiles // GROUP + 1) * LANES
+    wires = 8 * (2 * GROUP + 4 * (E - 1) + 4 * E * (A - 1))
     wires += (sw // R) * 2 * (A + E) + 2 + 8 * 10
     group_rows = GROUP * rows
     sizes = (A, E, R, rows, width, sw, uc, larger, (2.0 * LAYERS) ** 0.5, head_dim ** (-0.5))
@@ -1156,22 +1276,24 @@
         out_shape=[
             shape((rows, width), BF16),
             shape((rows, width), F32),
+            shape((R, 3 * width), BF16),
+            shape((R, 2 * hidden), BF16),
+            shape((R, hidden), BF16),
             shape((GROUP, 16, LANES), BF16),
-            shape((GROUP, R, qc), BF16),
             shape((R, width), BF16),
         ]
-        + [shape((GROUP, R, uc), BF16)] * 3
         + [
-            shape((A - 1,) + ((2, E * one[0], one[1]) if one else dense_landing), BF16)
+            shape((A - 1,) + ((2, E) + one if one else dense_landing), BF16)
             for one in landings
         ]
         + [
             shape((E - 1,) + ((2,) + one if one else dense_landing), BF16)
             for one in landings
         ],
-        in_specs=[pl.BlockSpec(memory_space=pltpu.SMEM)] * 2 + [vmem] * 2 + [anywhere] * 7,
-        out_specs=[vmem, vmem] + [anywhere] * 18,
+        in_specs=[pl.BlockSpec(memory_space=pltpu.SMEM)] * 2 + [vmem] * 4 + [anywhere] * 5,
+        out_specs=[vmem] * 5 + [anywhere] * 14,
         scratch_shapes=[
+            pltpu.VMEM((16, LANES), BF16),
             pltpu.VMEM((width // R * 16, LANES), BF16),
             pltpu.VMEM((width, qc), BF16),
             pltpu.VMEM((sw, width), BF16),
@@ -1201,9 +1323,9 @@
             pltpu.VMEM((16, width), F32),
             pltpu.VMEM((16, width), F32),
             pltpu.VMEM((8, qc), F32),
-            pltpu.VMEM((E * 4 * R, max(uc, qc)), BF16),
+            pltpu.VMEM((4 * R, max(uc, qc)), BF16),
             pltpu.VMEM((R, width), BF16),
-            pltpu.SemaphoreType.DMA((SHARED + 2,)),
+            pltpu.SemaphoreType.DMA((SHARED + 5,)),
             pltpu.SemaphoreType.DMA((wires,)),
             pltpu.SemaphoreType.DMA((wires,)),
         ],
@@ -1215,38 +1337,23 @@
         prefix,
         cotangent,
         table,
+        biases,
+        norm_gains,
         tokens,
-        small_pieces,
-        qkv_pieces,
+        qkv_weight,
         dense_weight,
-        gate_pieces,
-        up_pieces,
-        ffout_pieces,
+        ffin_weight,
+        ffout_weight,
     )
-    result, d_tokens, small_grads, qkv_grad, dense_grad, gate_grad, up_grad, ffout_grad = results[:8]
-
-    def unit_columns(pieces):
-        turned = pieces.transpose(1, 0, 2)
-        first = turned[:, :larger].reshape(R, larger * uc)
-        rest = turned[:, larger:, :smaller].reshape(R, (GROUP - larger) * smaller)
-        return jnp.concatenate([first, rest], axis=1)[:, :hidden].astype(F32)
-
-    grad_qkv = (
-        qkv_grad.reshape(2, 2, 2, R, 3, my_heads, head_dim)
-        .transpose(3, 4, 5, 1, 0, 2, 6)
-        .reshape(R, 3 * width)
-        .astype(F32)
-    )
+    result, d_tokens, qkv_grad, ffin_grad, ffout_grad, small_grads, dense_grad = results[:7]
     small_grads = jnp.sum(small_grads.astype(F32), axis=0)[:, :R].T
     return (
         result.reshape(tokens.shape),
         d_tokens.reshape(tokens.shape),
-        grad_qkv,
+        qkv_grad.astype(F32),
         dense_grad.astype(F32),
-        jnp.concatenate(
-            [unit_columns(gate_grad), unit_columns(up_grad)], axis=1
-        ),
-        unit_columns(ffout_grad),
+        ffin_grad.astype(F32),
+        ffout_grad.astype(F32),
         small_grads[:, :7],
         small_grads[:, 7:9],
     )

time: 482 us -> 438 us (0.909)
  Pallas kernels: 452 us -> 419 us
  local copies, waits for them, and re-layouts: 16.9 us -> 6.97 us
    pallas_call x1, Pallas kernels: 452 us -> 419 us  [on_device(): pl.pallas_call(functools.partial(layer_kernel, sizes), out_shape=[shape((...]
where the time goes in v5:
time: 438 us; the launch traced here: 435 us
  Pallas kernels  419 us (96%)
  other arithmetic  7.89 us (2%)
  local copies, waits for them, and re-layouts  6.97 us (2%)
    pallas_call x1, Pallas kernels, on_device(): pl.pallas_call(functools.partial(layer_kernel, sizes), out_shape=[shape((...  419 us

profile of v5, /device:TPU:0, one launch (start us, length us, event | category | flops | bytes accessed | tf_op | source)
XLA Modules:
  0.0 434.9 jit_solution(6659466797981624080)
XLA Ops:
  0.6 1.4 copy.19.bias_ref
  2.0 1.4 copy.20.gain_ref
  3.4 419.3 %shard_map.170 = (bf16[128,2048]{1,0:T(8,128)(2,1)}, f32[128,2048]{1,0:T(8,128)}, bf16[64,6144]{1,0:T(8,128)(2,1)}, bf16[64,10922]{1,0:T(8,128)(2,1)}, bf16[64,5...) custom-call(s32[1,4]{1,0:T(1,128)} %len_ref.1, ...), custom_call_target="tpu_custom_call" | custom-call | tf_op jit(solution)/shard_map/pallas_call | solution.py:1274
  422.7 0.0 copy-start.2
  422.7 0.8 convert_reduce_fusion
  423.6 0.6 slice.14
  424.1 0.6 slice.13
  424.7 1.8 convert_element_type.16
  426.5 2.3 convert_element_type.18
  428.8 0.0 copy-done.2
  428.8 0.0 copy-start
  428.8 1.2 convert_element_type.15
  430.1 0.7 copy-done
  430.7 0.0 copy-start.3
  430.7 1.7 convert_element_type.17
  432.5 0.0 copy-done.3
  432.5 0.0 copy-start.1
  432.5 0.8 copy.23
  433.3 0.6 copy-done.1
  433.9 1.0 copy.24
  (1 shorter events, 0.0 us)
Async XLA Ops:
  422.7 6.1 %copy-start.2 = (bf16[64,6144]{1,0:T(8,128)(2,1)S(1)}, bf16[64,6144]{1,0:T(8,128)(2,1)}, u32[]{:S(2)}) copy-start(bf16[64,6144]{1,0:T(8,128)(2,1)} %get-tuple-element.17) | copy-start | bytes 2359300
  428.8 1.9 copy-start
  430.7 1.7 copy-start.3
  432.5 1.4 copy-start.1

commit v6 on v5

--- a/solution.py
+++ b/solution.py
@@ -77,21 +77,20 @@
     sizes,
     len_ref,
     pre_ref,
-    cot_ref,
-    table_ref,
-    bias_ref,
-    gain_ref,
+    ct_ref,
+    tb_ref,
+    sp_ref,
     x_ref,
     rq_ref,
     dp_ref,
     ri_ref,
     ro_ref,
-    out_ref,
-    gx_ref,
-    fq_ref,
-    fi_ref,
-    fo_ref,
-    os_ref,
+    small_ref,
+    eo_ref,
+    ex_ref,
+    eq_ref,
+    ei_ref,
+    ef_ref,
     od_ref,
     ys_ref,
     yq_ref,
@@ -105,7 +104,14 @@
     zg_ref,
     zu_ref,
     zo_ref,
-    sp_ref,
+    out_ref,
+    gx_ref,
+    fq_ref,
+    fi_ref,
+    fo_ref,
+    cot_ref,
+    table_ref,
+    os_ref,
     ws_ref,
     wq_ref,
     wd_ref,
@@ -156,7 +162,27 @@
 
     loads = [
         pltpu.make_async_copy(raw, final, local_sem.at[SHARED + 2 + k])
-        for k, (raw, final) in enumerate(((rq_ref, fq_ref), (ri_ref, fi_ref), (ro_ref, fo_ref)))
+        for k, (raw, final) in enumerate(
+            (
+                (rq_ref, fq_ref),
+                (ri_ref, fi_ref),
+                (ro_ref, fo_ref),
+                (tb_ref, table_ref),
+                (ct_ref.at[0], cot_ref),
+            )
+        )
+    ]
+    results = [
+        pltpu.make_async_copy(found, result, local_sem.at[SHARED + 7 + k])
+        for k, (found, result) in enumerate(
+            (
+                (out_ref, eo_ref),
+                (gx_ref, ex_ref),
+                (fo_ref, ef_ref),
+                (fi_ref, ei_ref),
+                (fq_ref, eq_ref),
+            )
+        )
     ]
     for load in loads:
         load.start()
@@ -691,12 +717,13 @@
 
     dense = Dense()
 
+    chain = wires.take(10), wires.take(10)
     to_b, to_f, to_c = {"b": 1 - b}, {"f": 1 - f}, {"c": 1 - c}
     nb, nf, dg = slot(1 - b, f, c), slot(b, 1 - f, c), slot(1 - b, 1 - f, c)
 
     class Gather:
         def __init__(self, buf, lean):
-            self.buf, self.first, self.copies, self.lean = buf, wires.take(10), [], lean
+            self.buf, self.first, self.copies, self.lean = buf, chain[0], [], lean
 
         def part(self, place, which):
             if which is None:
@@ -760,7 +787,7 @@
             target[window, :] = total.astype(target.dtype)
 
     def scatter(multiply, lean, early=None, late=None):
-        first, copies = wires.take(10), []
+        first, copies = chain[1], []
 
         def send(*copy):
             copies.append(wires.send(*copy))
@@ -840,12 +867,6 @@
     loads[0].wait()
     cut_qkv()
     q_w.tp_send()
-    columns = [bias_ref[...].astype(F32), gain_ref[...].astype(F32)]
-    columns.append(jnp.zeros((R, LANES - sum(one.shape[1] for one in columns)), F32))
-    turned = jnp.concatenate(columns, axis=1).T[0:16, :]
-    if R < LANES:
-        turned = jnp.concatenate([turned, jnp.zeros((16, LANES - R), F32)], axis=1)
-    sp_ref[...] = turned.astype(BF16)
     s_w.tp_send()
     dense.out(True)
     own_x = pltpu.make_async_copy(
@@ -908,6 +929,9 @@
     g_w.y_send(1, 0)
     tokens.finish()
     o_w.tp_send()
+    for db in range(2):
+        u_w.tp_wait(db)
+        u_w.y_send(db, 0)
     s_w.y_arrive()
     q_w.y_arrive()
 
@@ -937,6 +961,7 @@
 
     blocks(all_rows // 512, 3, projection)
 
+    loads[3].wait()
     row_at = lax.broadcasted_iota(jnp.int32, (rows, rows), 0)
     col_at = lax.broadcasted_iota(jnp.int32, (rows, rows), 1)
 
@@ -978,8 +1003,6 @@
             probs = softmax(q, k, allowed).astype(BF16)
             cx_ref[here, i * LANES : (i + 1) * LANES] = dot(probs, v).astype(BF16)
 
-    u_w.tp_wait(0)
-    u_w.tp_wait(1)
     u_w.z_send(0)
     g_w.z_arrive(0)
     dense.y_arrive()
@@ -994,8 +1017,9 @@
 
     def more_units():
         u_w.z_send(1)
-        u_w.y_send(0, 0)
-        u_w.y_send(1, 0)
+        for db in range(2):
+            o_w.tp_wait(db)
+            o_w.y_send(db, 0)
 
     scatter(dense_partial, True, lambda: g_w.z_arrive(1), more_units)
 
@@ -1020,21 +1044,20 @@
 
     row_loop(first_norm)
     normed = Gather(hg_ref, True)
+    sent(tokens.copies)
     normed.start()
     for db in range(2):
-        o_w.tp_wait(db)
         o_w.z_send(db)
     u_w.z_arrive(0)
-    o_w.y_send(0, 0)
-    o_w.y_send(1, 0)
     normed.relay()
     u_w.z_arrive(1)
     normed.finish()
+    o_w.z_arrive(0)
     g_w.y_arrive()
     u_w.y_arrive()
 
     def units(m, n):
-        here = span(m * 512, 512)
+        here = pl.ds(m * 512, 512)
         gate_cols = span(n * 256, 256)
         up_cols = span(uc + n * 256, 256)
         left = hg_ref[here, :]
@@ -1047,9 +1070,10 @@
         uf_ref[here, gate_cols] = (cdf + gate * density) * up
         uf_ref[here, up_cols] = act
 
-    blocks(all_rows // 512, uc // 256, units)
-    o_w.z_arrive(0)
-    o_w.z_arrive(1)
+    for m in range(all_rows // 512):
+        blocks(1, uc // 256, lambda _, n: units(m, n))
+        if m == 0:
+            o_w.z_arrive(1)
     o_w.y_arrive()
     scatter(onto_partial((mb_ref, wo_ref)), False)
 
@@ -1068,7 +1092,7 @@
         normed_one = xh_ref[here, :] * bt_ref[7:8, :] + bt_ref[4:5, :]
         unit, rstd = normalize(alpha * normed_one + sum_ref[here, :] + bt_ref[5:6, :])
         out_ref[here, :] = (unit * bt_ref[8:9, :] + bt_ref[6:7, :]).astype(BF16)
-        grad = cot_ref[0, here, :].astype(F32) * valid_ref[here, 0:1]
+        grad = cot_ref[here, :].astype(F32) * valid_ref[here, 0:1]
         back = norm_back(grad, bt_ref[8:9, :], unit, rstd)
         low = back.astype(BF16)
         dr_ref[here, :] = back
@@ -1077,8 +1101,11 @@
         add_row(6, grad)
         add_row(8, grad * unit)
 
+    loads[4].wait()
     row_loop(second_norm)
+    results[0].start()
     branch = Gather(dg_ref, False)
+    sent(normed.copies)
     branch.start()
     branch.relay()
     branch.finish()
@@ -1131,7 +1158,7 @@
         add_row(7, grad * unit)
 
     row_loop(first_norm_back)
-    attended = Gather(dg_ref, True)
+    attended = Gather(dg_ref, False)
     attended.start()
     g_w.gy_away(0)
     attended.relay()
@@ -1178,6 +1205,7 @@
 
     def late_adds():
         q_w.gy_away(0)
+        q_w.gy_away(1)
         g_w.home()
 
     def qkv_grad():
@@ -1194,6 +1222,7 @@
                 ws_ref[span((k * (LANES // R) + j) * 16, 16), :] = part.astype(BF16)
 
         s_w.gy_send()
+        dense.gy_add()
 
     scatter(onto_partial((mb_ref, wq_ref)), True, qkv_grad, late_adds)
 
@@ -1201,9 +1230,8 @@
         gx_ref[here, :] = alpha * dr_ref[here, :] + sum_ref[here, :]
 
     row_loop(tokens_back)
-
-    q_w.gy_away(1)
-    dense.gy_add()
+    results[1].start()
+
     for db in range(2):
         s_w.gy_away(db)
     u_w.home()
@@ -1217,15 +1245,68 @@
     dense.gz_add()
     o_w.g_end()
     join(fo_ref, [home_tiles(1, 1)])
+    results[2].start()
     g_w.g_end()
     u_w.g_end()
     join(fi_ref, [home_tiles(0, 1), home_tiles(1, 0)])
+    results[3].start()
     q_w.g_end()
     join_qkv()
+    results[4].start()
     s_w.g_end()
+    small_ref[...] = sum(os_ref[place].astype(F32) for place in range(GROUP))
     dense.g_end()
+    for result in results:
+        result.wait()
     for flow in (q_w, g_w, u_w, o_w, s_w, tokens, attended):
         sent(flow.copies)
+
+
+def final_kernel(count, plain, *refs):
+    small_ref, bias_ref, gain_ref = refs[0], refs[1 + count], refs[2 + count]
+    refs = refs[1 : 1 + count] + refs[3 + count :]
+    sources, targets, held = (refs[k * count : (k + 1) * count] for k in range(3))
+    wide = refs[3 * count : -2]
+    load_sem, store_sem = refs[-2:]
+    loads = [
+        pltpu.make_async_copy(source, one, load_sem.at[k])
+        for k, (source, one) in enumerate(zip(sources, held))
+    ]
+    for one in loads:
+        one.start()
+    cut, own = bias_ref.shape
+    bias_ref[...] = small_ref[0:cut, 0:own]
+    gain_ref[...] = small_ref[cut : cut + gain_ref.shape[0], 0:own]
+    stores = []
+    for k, load in enumerate(loads):
+        load.wait()
+        found = held[k]
+        if k >= plain:
+            found = wide[k - plain]
+            found[...] = held[k][...].astype(F32)
+        stores.append(pltpu.make_async_copy(found, targets[k], store_sem.at[k]))
+        stores[-1].start()
+    for one in stores:
+        one.wait()
+
+
+def finish(small, cuts, plain, narrow):
+    shape, anywhere = jax.ShapeDtypeStruct, pl.BlockSpec(memory_space=pl.ANY)
+    vmem = pl.BlockSpec(memory_space=pltpu.VMEM)
+    arrays = [*plain, *narrow]
+    count = len(arrays)
+    return pl.pallas_call(
+        functools.partial(final_kernel, count, len(plain)),
+        out_shape=[shape(cut, F32) for cut in cuts]
+        + [shape(one.shape, one.dtype) for one in plain]
+        + [shape(one.shape, F32) for one in narrow],
+        in_specs=[vmem] + [anywhere] * count,
+        out_specs=[vmem] * 2 + [anywhere] * count,
+        scratch_shapes=[pltpu.VMEM(one.shape, one.dtype) for one in arrays]
+        + [pltpu.VMEM(one.shape, F32) for one in narrow]
+        + [pltpu.SemaphoreType.DMA((count,)), pltpu.SemaphoreType.DMA((count,))],
+        compiler_params=pltpu.CompilerParams(vmem_limit_bytes=63 << 20),
+    )(small, *arrays)
 
 
 def on_device(
@@ -1260,11 +1341,14 @@
         rest = rest - terms[-1].astype(np.float32)
     table = jnp.asarray(np.concatenate(terms, axis=1))
 
+    small = jnp.concatenate([biases, norm_gains], axis=1).T
+    small = jnp.pad(small, ((0, 16 - small.shape[0]), (0, LANES - R)))
+
     tiles = -(-hidden // LANES)
     larger = tiles % GROUP
     uc = (tiles // GROUP + 1) * LANES
     wires = 8 * (2 * GROUP + 4 * (E - 1) + 4 * E * (A - 1))
-    wires += (sw // R) * 2 * (A + E) + 2 + 8 * 10
+    wires += (sw // R) * 2 * (A + E) + 2 + 2 * 10
     group_rows = GROUP * rows
     sizes = (A, E, R, rows, width, sw, uc, larger, (2.0 * LAYERS) ** 0.5, head_dim ** (-0.5))
     shape = jax.ShapeDtypeStruct
@@ -1274,12 +1358,12 @@
     results = pl.pallas_call(
         functools.partial(layer_kernel, sizes),
         out_shape=[
+            shape((16, LANES), F32),
             shape((rows, width), BF16),
             shape((rows, width), F32),
             shape((R, 3 * width), BF16),
             shape((R, 2 * hidden), BF16),
             shape((R, hidden), BF16),
-            shape((GROUP, 16, LANES), BF16),
             shape((R, width), BF16),
         ]
         + [
@@ -1290,10 +1374,17 @@
             shape((E - 1,) + ((2,) + one if one else dense_landing), BF16)
             for one in landings
         ],
-        in_specs=[pl.BlockSpec(memory_space=pltpu.SMEM)] * 2 + [vmem] * 4 + [anywhere] * 5,
-        out_specs=[vmem] * 5 + [anywhere] * 14,
+        in_specs=[pl.BlockSpec(memory_space=pltpu.SMEM)] * 2 + [anywhere] * 8,
+        out_specs=[vmem] + [anywhere] * 18,
         scratch_shapes=[
-            pltpu.VMEM((16, LANES), BF16),
+            pltpu.VMEM((rows, width), BF16),
+            pltpu.VMEM((rows, width), F32),
+            pltpu.VMEM((R, 3 * width), BF16),
+            pltpu.VMEM((R, 2 * hidden), BF16),
+            pltpu.VMEM((R, hidden), BF16),
+            pltpu.VMEM((rows, width), BF16),
+            pltpu.VMEM((rows, 3 * LANES), BF16),
+            pltpu.VMEM((GROUP, 16, LANES), BF16),
             pltpu.VMEM((width // R * 16, LANES), BF16),
             pltpu.VMEM((width, qc), BF16),
             pltpu.VMEM((sw, width), BF16),
@@ -1325,7 +1416,7 @@
             pltpu.VMEM((8, qc), F32),
             pltpu.VMEM((4 * R, max(uc, qc)), BF16),
             pltpu.VMEM((R, width), BF16),
-            pltpu.SemaphoreType.DMA((SHARED + 5,)),
+            pltpu.SemaphoreType.DMA((SHARED + 12,)),
             pltpu.SemaphoreType.DMA((wires,)),
             pltpu.SemaphoreType.DMA((wires,)),
         ],
@@ -1337,25 +1428,29 @@
         prefix,
         cotangent,
         table,
-        biases,
-        norm_gains,
+        small,
         tokens,
         qkv_weight,
         dense_weight,
         ffin_weight,
         ffout_weight,
     )
-    result, d_tokens, qkv_grad, ffin_grad, ffout_grad, small_grads, dense_grad = results[:7]
-    small_grads = jnp.sum(small_grads.astype(F32), axis=0)[:, :R].T
+    small_grads, result, d_tokens, qkv_grad, ffin_grad, ffout_grad, dense_grad = results[:7]
+    bias_grad, gain_grad, result, d_tokens, ffin_grad, qkv_grad, ffout_grad, dense_grad = finish(
+        small_grads,
+        (biases.shape[::-1], norm_gains.shape[::-1]),
+        [result, d_tokens],
+        [ffin_grad, qkv_grad, ffout_grad, dense_grad],
+    )
     return (
         result.reshape(tokens.shape),
         d_tokens.reshape(tokens.shape),
-        qkv_grad.astype(F32),
-        dense_grad.astype(F32),
-        ffin_grad.astype(F32),
-        ffout_grad.astype(F32),
-        small_grads[:, :7],
-        small_grads[:, 7:9],
+        qkv_grad,
+        dense_grad,
+        ffin_grad,
+        ffout_grad,
+        bias_grad.T,
+        gain_grad.T,
     )
 
 

time: 438 us -> 418 us (0.954)
  other arithmetic: 7.89 us -> 0.71 us
  local copies, waits for them, and re-layouts: 6.97 us -> 0.6 us
  Pallas kernels: 419 us -> 414 us
    pallas_call x1, Pallas kernels: 419 us -> 408 us  [on_device(): pl.pallas_call(functools.partial(layer_kernel, sizes), out_shape=[shape((...]
    convert_element_type x4 -> x0, other arithmetic: 7.05 us -> none  [the longest x1 2.28 us: on_device(): ffout_grad.astype(F32)]
    pallas_call x0 -> x1, Pallas kernels: none -> 6.03 us  [finish(): pl.pallas_call(functools.partial(final_kernel, count, len(plain)), out_sh...]
    unnamed x12 -> x0, local copies, waits for them, and re-layouts: 5.8 us -> none
where the time goes in v6:
time: 418 us; the launch traced here: 416 us
  Pallas kernels  414 us (99%)
    pallas_call x1, Pallas kernels, on_device(): pl.pallas_call(functools.partial(layer_kernel, sizes), out_shape=[shape((...  408 us

profile of v6, /device:TPU:0, one launch (start us, length us, event | category | flops | bytes accessed | tf_op | source)
XLA Modules:
  0.0 416.3 jit_solution(16412486283621242259)
XLA Ops:
  0.6 0.7 maximum_bitcast_fusion
  1.3 0.6 pad.4.sp_ref
  1.9 408.2 %shard_map.170 = (f32[16,128]{1,0:T(8,128)}, bf16[128,2048]{1,0:T(8,128)(2,1)}, f32[128,2048]{1,0:T(8,128)}, bf16[64,6144]{1,0:T(8,128)(2,1)}, bf16[64,10922]{1,...) custom-call(s32[1,4]{1,0:T(1,128)} %len_ref.1, ...), custom_call_target="tpu_custom_call" | custom-call | tf_op jit(solution)/shard_map/pallas_call | solution.py:1358
  410.1 6.0 %shard_map.171 = (f32[7,64]{1,0:T(8,128)}, f32[2,64]{1,0:T(2,128)}, bf16[128,2048]{1,0:T(8,128)(2,1)}, f32[128,2048]{1,0:T(8,128)}, f32[64,10922]{1,0:T(8,128)},...) custom-call(f32[16,128]{1,0:T(8,128)} %get-tuple-element.23.refs_0_, ...), custom_call_target="tpu_custom_call" | custom-call | tf_op jit(solution)/shard_map/pallas_call | solution.py:1298

commit v7 on v6

--- a/solution.py
+++ b/solution.py
@@ -37,18 +37,23 @@
 
 class Wires:
     def __init__(self, send_sem, recv_sem):
-        self.send_sem, self.recv_sem, self.count = send_sem, recv_sem, 0
+        self.send_sem, self.recv_sem, self.count, self.outs = send_sem, recv_sem, 0, 0
 
     def take(self, numbers=1):
         first = self.count
         self.count += numbers
         return first
 
-    def send(self, number, source, target, device, condition=None):
+    def out(self, numbers=1):
+        first = self.outs
+        self.outs += numbers
+        return first
+
+    def send(self, out, number, source, target, device, condition=None):
         one = pltpu.make_async_remote_copy(
             src_ref=source,
             dst_ref=target,
-            send_sem=self.send_sem.at[number],
+            send_sem=self.send_sem.at[out],
             recv_sem=self.recv_sem.at[number],
             device_id=device,
             device_id_type=DEVICE_MESH,
@@ -213,7 +218,7 @@
             self.index, self.R, self.parts, self.buf = index, R, parts, buf
             self.piece, self.out = piece, out
             self.ylanding, self.zlanding = ylanding, zlanding
-            self.copies = []
+            self.copies, self.shared, self.way = [], wires.out(2), 0
             take = lambda count: wires.take(count * len(parts))
             self.tp, self.z, self.y = take(GROUP), take(2 * (E - 1)), take(2 * E * (A - 1))
             self.gtp, self.gz, self.gy = take(GROUP), take(2 * (E - 1)), take(2 * E * (A - 1))
@@ -224,8 +229,13 @@
 
         def send(self, first, number, source, target, device, member=me):
             def body(k, cols, condition):
-                self.copies.append(
+                if condition is None:
+                    out, copies = self.shared + self.way, []
+                else:
+                    out, copies = wires.out(), self.copies
+                copies.append(
                     wires.send(
+                        out,
                         first + number * len(self.parts) + k,
                         source.at[:, cols],
                         target.at[:, cols],
@@ -243,6 +253,13 @@
                 )
 
             self.each(member, body)
+
+        def sent(self):
+            first, size, _ = self.parts[0]
+            rows_ = self.buf.at[pl.ds(0, (A * E * GROUP - 1) * self.R), pl.ds(first, size)]
+            pltpu.make_async_copy(rows_, rows_, send_sem.at[self.shared + self.way]).wait()
+            sent(self.copies)
+            self.way = 1
 
         def line(self, aa, bb, ee, ff, cc):
             return span(rank(aa, bb, ee, ff, cc) * self.R, self.R)
@@ -532,13 +549,14 @@
         def __init__(self):
             self.pieces = wd_ref.shape[0] // R
             self.first = wires.take(self.pieces)
-            self.push = wires.take(1)
-            self.zs = wires.take(self.pieces * (E - 1))
-            self.ys = wires.take(self.pieces * (A - 1))
+            self.push = wires.out()
+            self.zs = wires.out(self.pieces * (E - 1))
+            self.ys = wires.out(self.pieces * (A - 1))
             self.gy = wires.take(self.pieces * (A - 1))
             self.gz = wires.take(self.pieces * (E - 1))
             self.back = wires.take(1)
-            self.back_sends = wires.take(self.pieces)
+            self.back_sends = wires.out(self.pieces)
+            self.gys, self.gzs = wires.out(self.pieces * (A - 1)), wires.out(self.pieces * (E - 1))
             self.owners = []
             for piece in range(self.pieces):
                 i, offset = piece * R // LANES, piece * R % LANES
@@ -640,8 +658,11 @@
 
         def g_y(self, piece, t):
             to = lax.rem(a + t, A)
-            number = self.gy + piece * (A - 1) + t - 1
-            copy = remote(self.rows(piece), yd_ref.at[t - 1, piece], number, number, {"a": to})
+            number = piece * (A - 1) + t - 1
+            landing = yd_ref.at[t - 1, piece]
+            copy = remote(
+                self.rows(piece), landing, self.gys + number, self.gy + number, {"a": to}
+            )
             return to, copy
 
         def gy_send(self, start=True):
@@ -667,8 +688,11 @@
 
         def g_z(self, piece, s):
             to = lax.rem(e + s, E)
-            number = self.gz + piece * (E - 1) + s - 1
-            copy = remote(self.rows(piece), zd_ref.at[s - 1, piece], number, number, {"e": to})
+            number = piece * (E - 1) + s - 1
+            landing = zd_ref.at[s - 1, piece]
+            copy = remote(
+                self.rows(piece), landing, self.gzs + number, self.gz + number, {"e": to}
+            )
             return to, copy
 
         def gz_send(self, start=True):
@@ -717,7 +741,7 @@
 
     dense = Dense()
 
-    chain = wires.take(10), wires.take(10)
+    chain, chain_out = (wires.take(10), wires.take(10)), (wires.out(10), wires.out(10))
     to_b, to_f, to_c = {"b": 1 - b}, {"f": 1 - f}, {"c": 1 - c}
     nb, nf, dg = slot(1 - b, f, c), slot(b, 1 - f, c), slot(1 - b, 1 - f, c)
 
@@ -732,7 +756,9 @@
 
         def copy(self, number, place, which, device):
             here = self.part(place, which)
-            self.copies.append(wires.send(self.first + number, here, here, device))
+            self.copies.append(
+                wires.send(chain_out[0] + number, self.first + number, here, here, device)
+            )
 
         def landed(self, number, place, which):
             wires.arrived(self.first + number, self.part(place, which))
@@ -789,8 +815,8 @@
     def scatter(multiply, lean, early=None, late=None):
         first, copies = chain[1], []
 
-        def send(*copy):
-            copies.append(wires.send(*copy))
+        def send(number, *copy):
+            copies.append(wires.send(chain_out[1] + number - first, number, *copy))
 
         multiply((1 - c) * half_rows, half_rows)
         for k, (bb, ff) in enumerate(places):
@@ -1045,9 +1071,9 @@
     row_loop(first_norm)
     normed = Gather(hg_ref, True)
     sent(tokens.copies)
+    o_w.z_send(0)
     normed.start()
-    for db in range(2):
-        o_w.z_send(db)
+    o_w.z_send(1)
     u_w.z_arrive(0)
     normed.relay()
     u_w.z_arrive(1)
@@ -1124,8 +1150,8 @@
 
         blocks(width // 512, cols // bn, body)
 
-    for flow in (normed, q_w, g_w, u_w, o_w):
-        sent(flow.copies)
+    for flow in (q_w, g_w, u_w, o_w):
+        flow.sent()
     weight_grad(dg_ref, mb_ref, go_ref, uc, uc)
     o_w.buf = go_ref
     o_w.gy_send()
@@ -1211,8 +1237,7 @@
     def qkv_grad():
         weight_grad(xg_ref, mb_ref, wq_ref, qc, qc)
 
-        q_w.gy_send()
-        sent(s_w.copies)
+        s_w.sent()
 
         @pl.loop(0, width // LANES)
         def _(k):
@@ -1222,6 +1247,7 @@
                 ws_ref[span((k * (LANES // R) + j) * 16, 16), :] = part.astype(BF16)
 
         s_w.gy_send()
+        q_w.gy_send()
         dense.gy_add()
 
     scatter(onto_partial((mb_ref, wq_ref)), True, qkv_grad, late_adds)
@@ -1258,8 +1284,9 @@
     dense.g_end()
     for result in results:
         result.wait()
-    for flow in (q_w, g_w, u_w, o_w, s_w, tokens, attended):
-        sent(flow.copies)
+    for flow in (q_w, g_w, u_w, o_w, s_w):
+        flow.sent()
+    sent(attended.copies)
 
 
 def final_kernel(count, plain, *refs):
@@ -1348,6 +1375,8 @@
     larger = tiles % GROUP
     uc = (tiles // GROUP + 1) * LANES
     wires = 8 * (2 * GROUP + 4 * (E - 1) + 4 * E * (A - 1))
+    outs = 3 * (2 * GROUP + 4 * (E - 1) + 4 * E * (A - 1)) + 10
+    outs += (sw // R) * 2 * (A + E) + 2 + 2 * 10
     wires += (sw // R) * 2 * (A + E) + 2 + 2 * 10
     group_rows = GROUP * rows
     sizes = (A, E, R, rows, width, sw, uc, larger, (2.0 * LAYERS) ** 0.5, head_dim ** (-0.5))
@@ -1417,7 +1446,7 @@
             pltpu.VMEM((4 * R, max(uc, qc)), BF16),
             pltpu.VMEM((R, width), BF16),
             pltpu.SemaphoreType.DMA((SHARED + 12,)),
-            pltpu.SemaphoreType.DMA((wires,)),
+            pltpu.SemaphoreType.DMA((outs,)),
             pltpu.SemaphoreType.DMA((wires,)),
         ],
         compiler_params=pltpu.CompilerParams(

time: 418 us -> 417 us (level)
  no operation moved by 1% of the time
where the time goes in v7:
time: 417 us; the launch traced here: 415 us
  Pallas kernels  413 us (99%)
    pallas_call x1, Pallas kernels, on_device(): pl.pallas_call(functools.partial(layer_kernel, sizes), out_shape=[shape((...  407 us

profile of v7, /device:TPU:0, one launch (start us, length us, event | category | flops | bytes accessed | tf_op | source)
XLA Modules:
  0.0 415.0 jit_solution(4202900385297136520)
XLA Ops:
  0.6 0.7 maximum_bitcast_fusion
  1.3 0.6 pad.4.sp_ref
  1.9 406.8 %shard_map.170 = (f32[16,128]{1,0:T(8,128)}, bf16[128,2048]{1,0:T(8,128)(2,1)}, f32[128,2048]{1,0:T(8,128)}, bf16[64,6144]{1,0:T(8,128)(2,1)}, bf16[64,10922]{1,...) custom-call(s32[1,4]{1,0:T(1,128)} %len_ref.1, ...), custom_call_target="tpu_custom_call" | custom-call | tf_op jit(solution)/shard_map/pallas_call | solution.py:1387
  408.8 6.0 %shard_map.171 = (f32[7,64]{1,0:T(8,128)}, f32[2,64]{1,0:T(2,128)}, bf16[128,2048]{1,0:T(8,128)(2,1)}, f32[128,2048]{1,0:T(8,128)}, f32[64,10922]{1,0:T(8,128)},...) custom-call(f32[16,128]{1,0:T(8,128)} %get-tuple-element.23.refs_0_, ...), custom_call_target="tpu_custom_call" | custom-call | tf_op jit(solution)/shard_map/pallas_call | solution.py:1325
